TPU v7x, 32 devices: a whole 2x2x4 slice. The times are simulated.
32 devices in a mesh: dp: 8 (over z, x), tensor: 4 (over y, core).
Axes of the slice: x: 2, y: 2, z: 4, core: 2. Of those that a mesh axis runs over, the one named last changes fastest.
Arguments:
- tokens: bfloat16 [14336, 1024], P('dp'), may hold values from -6 to 6
- lengths: int32 [8, 8], P('dp'), may hold values from 0 to 1568, as said below
- owner: int32 [8], replicated, may hold values from 0 to 7, each once
- attend_master: float32 [3, 1024, 1024], P(None, 'dp', 'tensor'), may hold values from -0.1875 to 0.1875
- attend_first: float32 [3, 1024, 1024], P(None, 'dp', 'tensor'), may hold values from -40 to 40
- attend_second: float32 [3, 1024, 1024], P(None, 'dp', 'tensor'), may hold values from 189.2352 to 759.808
- output_master: float32 [1024, 1024], P('dp', 'tensor'), may hold values from -1.5 to 1.5
- output_first: float32 [1024, 1024], P('dp', 'tensor'), may hold values from -6 to 6
- output_second: float32 [1024, 1024], P('dp', 'tensor'), may hold values from 17.2032 to 68.8128
- dense_master: float32 [2, 1024, 4, 1024], P(None, 'dp', None, 'tensor'), may hold values from -0.1875 to 0.1875
- dense_first: float32 [2, 1024, 4, 1024], P(None, 'dp', None, 'tensor'), may hold values from -40 to 40
- dense_second: float32 [2, 1024, 4, 1024], P(None, 'dp', None, 'tensor'), may hold values from 189.2352 to 759.808
- bias_master: float32 [5, 1024], P(None, ('tensor', 'dp')), may hold values from -1.2 to 1.2
- bias_first: float32 [5, 1024], P(None, ('tensor', 'dp')), may hold values from -32 to 32
- bias_second: float32 [5, 1024], P(None, ('tensor', 'dp')), may hold values from 143.36 to 573.44
- vector_master: float32 [6, 1024], P(None, 'dp'), may hold values from -1.2 to 1.6, as said below
- vector_first: float32 [6, 1024], P(None, 'dp'), may hold values from -80 to 80
- vector_second: float32 [6, 1024], P(None, 'dp'), may hold values from 759.808 to 3010.56
- cotangent: bfloat16 [14336, 1024], P('dp'), may hold values from -6 to 6
Outputs:
- layer_output: bfloat16 [14336, 1024], P('dp')
- tokens_grad: bfloat16 [14336, 1024], P('dp')
- attend_first_next: float32 [3, 1024, 1024], P(None, 'dp', 'tensor')
- attend_second_next: float32 [3, 1024, 1024], P(None, 'dp', 'tensor')
- attend_updated: float32 [3, 1024, 1024], P(None, 'dp', 'tensor')
- output_first_next: float32 [1024, 1024], P('dp', 'tensor')
- output_second_next: float32 [1024, 1024], P('dp', 'tensor')
- output_updated: float32 [1024, 1024], P('dp', 'tensor')
- dense_first_next: float32 [2, 1024, 4, 1024], P(None, 'dp', None, 'tensor')
- dense_second_next: float32 [2, 1024, 4, 1024], P(None, 'dp', None, 'tensor')
- dense_updated: float32 [2, 1024, 4, 1024], P(None, 'dp', None, 'tensor')
- bias_first_next: float32 [5, 1024], P(None, ('tensor', 'dp'))
- bias_second_next: float32 [5, 1024], P(None, ('tensor', 'dp'))
- bias_updated: float32 [5, 1024], P(None, ('tensor', 'dp'))
- vector_first_next: float32 [6, 1024], P(None, 'dp')
- vector_second_next: float32 [6, 1024], P(None, 'dp')
- vector_updated: float32 [6, 1024], P(None, 'dp')
Inputs may be any that keep to these rules, and one draw needn't show every extreme that they name: `lengths`: each row lists the sequences packed in order onto that dp index's 1792 rows; an entry is 0 (an empty slot) or a multiple of 196, at most one entry of a row exceeds 196, a row sums to at most 1792, and some dp index holds a sequence of exactly 1568 tokens. `owner`: each number of 0 to 7 appears once. `vector_master`: rows 2 and 4 are norms' gains near one; the other rows are biases of both signs.
All inputs are finite; a program needn't handle non-finite values.
Results may differ from a plain program's by a relative error of at most 0.025.
Values may be sent and summed in bfloat16 or wider, within the bound.
A program may use at most 256 MiB of HBM per device.

v0:
```python
import jax
import jax.numpy as jnp
from jax import lax
from jax.sharding import PartitionSpec as P

D = 1024
HD = 64
STEP = 10


norm_epsilon = 1e-06
masked_score = -1e30
first_decay = 0.9
second_decay = 0.95
adam_epsilon = 1e-08
matrix_rate = 0.1
output_rate = 0.5
bias_rate = 0.5
vector_rate = 1.0
matrix_decay = 0.05


def layer_norm(hidden, gain, shift):
    center = jnp.mean(hidden, axis=-1, keepdims=True)
    offset = hidden - center
    spread = jnp.mean(offset * offset, axis=-1, keepdims=True)
    return offset * lax.rsqrt(spread + norm_epsilon) * gain + shift


def gelu_exact(values):
    return jax.nn.gelu(values, approximate=False)


def segment_ids(row_lengths, total_rows):
    ends = jnp.cumsum(row_lengths)
    places = jnp.arange(total_rows, dtype=jnp.int32)
    return jnp.sum((places[:, None] >= ends[None, :]).astype(jnp.int32), axis=1)


def reorder(array, axis_dim, order, outer):
    count_blocks = order.shape[0]
    shape_old = array.shape
    shape_new = (
        shape_old[:axis_dim]
        + (outer, count_blocks, shape_old[axis_dim] // (outer * count_blocks))
        + shape_old[axis_dim + 1 :]
    )
    moved = jnp.take(array.reshape(shape_new), order, axis=axis_dim + 1)
    return moved.reshape(shape_old)


def adamw_step(weight, first, second, grad, rate, decay):
    first_next = first_decay * first + (1.0 - first_decay) * grad
    second_next = second_decay * second + (1.0 - second_decay) * grad * grad
    first_hat = first_next / (1.0 - first_decay**STEP)
    second_hat = second_next / (1.0 - second_decay**STEP)
    update = first_hat / (jnp.sqrt(second_hat) + adam_epsilon) + decay * weight
    return (first_next, second_next, weight - rate * update)


def contract_rows(left, right):
    return lax.dot_general(
        left, right, (((0,), (0,)), ((), ())), preferred_element_type=jnp.float32
    )


def contract_cols(left, right):
    return lax.dot_general(
        left, right, (((1,), (1,)), ((), ())), preferred_element_type=jnp.float32
    )


def local(
    tokens,
    lengths,
    owner,
    attend_master,
    attend_first,
    attend_second,
    output_master,
    output_first,
    output_second,
    dense_master,
    dense_first,
    dense_second,
    bias_master,
    bias_first,
    bias_second,
    vector_master,
    vector_first,
    vector_second,
    cotangent,
):
    half_type = jnp.bfloat16
    full_type = jnp.float32
    owner_count = owner.shape[0]
    places = jnp.arange(owner_count, dtype=jnp.int32)
    inverse = jnp.sum(jnp.where(owner[None, :] == places[:, None], places[None, :], 0), axis=1)
    gathered = (
        lax.all_gather(attend_master.astype(half_type), "dp", axis=1, tiled=True),
        lax.all_gather(output_master.astype(half_type), "dp", axis=0, tiled=True),
        lax.all_gather(dense_master.astype(half_type), "dp", axis=1, tiled=True),
        lax.all_gather(bias_master.astype(half_type), "dp", axis=1, tiled=True),
        lax.all_gather(vector_master.astype(half_type), "dp", axis=1, tiled=True),
    )
    attend_w = reorder(gathered[0], 1, inverse, 1)
    output_w = reorder(gathered[1], 0, inverse, 1)
    dense_w = reorder(gathered[2], 1, inverse, 1)
    bias_w = reorder(gathered[3], 1, inverse, 1).astype(full_type)
    vectors = reorder(gathered[4], 1, inverse, 1).astype(full_type)
    total_rows = tokens.shape[0]
    local_width = attend_w.shape[2]
    head_count = local_width // HD
    unit_ratio = dense_w.shape[2]
    hidden_width = unit_ratio * local_width
    score_scale = HD ** (-0.5)
    w_query = attend_w[0]
    w_key = attend_w[1]
    w_value = attend_w[2]
    w_up = dense_w[0].reshape(D, hidden_width)
    w_down = dense_w[1].reshape(D, hidden_width)
    bias_query = bias_w[0]
    bias_up = bias_w[1:].reshape(hidden_width)
    segments = segment_ids(lengths[0], total_rows)
    block_count = max(1, total_rows // 896)
    block_rows = total_rows // block_count
    inputs = tokens.astype(full_type)
    act_one = layer_norm(inputs, vectors[2], vectors[3]).astype(half_type)
    query = (jnp.dot(act_one, w_query, preferred_element_type=full_type) + bias_query).astype(
        half_type
    )
    key_rows = jnp.dot(act_one, w_key, preferred_element_type=full_type).astype(half_type)
    value_rows = jnp.dot(act_one, w_value, preferred_element_type=full_type).astype(half_type)
    query_heads = query.reshape(total_rows, head_count, HD)
    key_heads = key_rows.reshape(total_rows, head_count, HD)
    value_heads = value_rows.reshape(total_rows, head_count, HD)

    def block_scores(block_index):
        row_start = block_index * block_rows
        query_block = lax.dynamic_slice_in_dim(query_heads, row_start, block_rows, 0)
        segment_block = lax.dynamic_slice_in_dim(segments, row_start, block_rows, 0)
        scores = (
            jnp.einsum("qhd,khd->hqk", query_block, key_heads, preferred_element_type=full_type)
            * score_scale
        )
        allowed = (segment_block[:, None] == segments[None, :])[None]
        return jnp.where(allowed, scores, masked_score)

    def forward_block(block_index):
        scores = block_scores(block_index)
        top = jnp.max(scores, axis=-1, keepdims=True)
        weights = jnp.exp(scores - top)
        row_totals = jnp.sum(weights, axis=-1, keepdims=True)
        probs = (weights / row_totals).astype(half_type)
        mixed_block = jnp.einsum(
            "hqk,khd->qhd", probs, value_heads, preferred_element_type=full_type
        )
        return (mixed_block.reshape(block_rows, local_width), (top + jnp.log(row_totals))[:, :, 0])

    mixed_parts, log_totals = lax.map(forward_block, jnp.arange(block_count))
    mixed = mixed_parts.reshape(total_rows, local_width).astype(half_type)
    attn_total = lax.psum(contract_cols(mixed, output_w).astype(jnp.bfloat16), "tensor").astype(
        jnp.float32
    )
    hidden = inputs + attn_total + vectors[0]
    act_two = layer_norm(hidden, vectors[4], vectors[5]).astype(half_type)
    pre_act = jnp.dot(act_two, w_up, preferred_element_type=full_type) + bias_up
    activated, gelu_back = jax.vjp(gelu_exact, pre_act)
    act_hidden = activated.astype(half_type)
    dense_total = lax.psum(contract_cols(act_hidden, w_down).astype(jnp.bfloat16), "tensor").astype(
        jnp.float32
    )
    layer_output = (hidden + dense_total + vectors[1]).astype(half_type)
    grad_out = cotangent.astype(full_type)
    grad_down = contract_rows(cotangent, act_hidden)
    grad_bias_two = jnp.sum(grad_out, axis=0)
    grad_act = jnp.dot(cotangent, w_down, preferred_element_type=full_type)
    grad_pre = gelu_back(grad_act)[0].astype(half_type)
    grad_bias_up = jnp.sum(grad_pre.astype(full_type), axis=0)
    grad_up = contract_rows(act_two, grad_pre)
    dense_grad = jnp.stack([grad_up, grad_down]).reshape(2, D, unit_ratio, local_width)
    grad_norm_two = lax.psum(contract_cols(grad_pre, w_up).astype(jnp.bfloat16), "tensor").astype(
        jnp.float32
    )
    norm_two_back = jax.vjp(layer_norm, hidden, vectors[4], vectors[5])[1]
    grad_hidden_norm, grad_gain_two, grad_shift_two = norm_two_back(grad_norm_two)
    grad_hidden = grad_out + grad_hidden_norm
    grad_bias_out = jnp.sum(grad_hidden, axis=0)
    grad_attn = grad_hidden.astype(half_type)
    grad_output = contract_rows(grad_attn, mixed)
    grad_mixed = jnp.dot(grad_attn, output_w, preferred_element_type=full_type).astype(half_type)
    grad_mixed_heads = grad_mixed.reshape(total_rows, head_count, HD)

    def backward_block(carry, block_index):
        grad_key, grad_value = carry
        row_start = block_index * block_rows
        query_block = lax.dynamic_slice_in_dim(query_heads, row_start, block_rows, 0)
        grad_block = lax.dynamic_slice_in_dim(grad_mixed_heads, row_start, block_rows, 0)
        scores = block_scores(block_index)
        probs = jnp.exp(scores - log_totals[block_index][:, :, None])
        probs_low = probs.astype(half_type)
        grad_value = grad_value + jnp.einsum(
            "hqk,qhd->khd", probs_low, grad_block, preferred_element_type=full_type
        )
        grad_probs = jnp.einsum(
            "qhd,khd->hqk", grad_block, value_heads, preferred_element_type=full_type
        )
        row_dot = jnp.sum(probs * grad_probs, axis=-1, keepdims=True)
        grad_scores = (probs * (grad_probs - row_dot)).astype(half_type)
        grad_query_block = (
            jnp.einsum("hqk,khd->qhd", grad_scores, key_heads, preferred_element_type=full_type)
            * score_scale
        )
        grad_key = (
            grad_key
            + jnp.einsum("hqk,qhd->khd", grad_scores, query_block, preferred_element_type=full_type)
            * score_scale
        )
        return ((grad_key, grad_value), grad_query_block)

    empty = jnp.zeros((total_rows, head_count, HD), full_type)
    carried, grad_query_parts = lax.scan(backward_block, (empty, empty), jnp.arange(block_count))
    grad_query = grad_query_parts.reshape(total_rows, local_width).astype(half_type)
    grad_key_low = carried[0].reshape(total_rows, local_width).astype(half_type)
    grad_value_low = carried[1].reshape(total_rows, local_width).astype(half_type)
    grad_bias_query = jnp.sum(grad_query.astype(full_type), axis=0)
    attend_grad = jnp.stack(
        [
            contract_rows(act_one, grad_query),
            contract_rows(act_one, grad_key_low),
            contract_rows(act_one, grad_value_low),
        ]
    )
    norm_one_part = (
        contract_cols(grad_query, w_query)
        + contract_cols(grad_key_low, w_key)
        + contract_cols(grad_value_low, w_value)
    )
    grad_norm_one = lax.psum(norm_one_part.astype(jnp.bfloat16), "tensor").astype(jnp.float32)
    norm_one_back = jax.vjp(layer_norm, inputs, vectors[2], vectors[3])[1]
    grad_input_norm, grad_gain_one, grad_shift_one = norm_one_back(grad_norm_one)
    tokens_grad = (grad_hidden + grad_input_norm).astype(half_type)
    bias_grad = jnp.concatenate(
        [grad_bias_query[None], grad_bias_up.reshape(unit_ratio, local_width)], axis=0
    )
    vector_grad = jnp.stack(
        [grad_bias_out, grad_bias_two, grad_gain_one, grad_shift_one, grad_gain_two, grad_shift_two]
    )
    attend_stored = reorder(attend_grad, 1, owner, 1)
    output_stored = reorder(grad_output, 0, owner, 1)
    bias_stored = reorder(bias_grad, 1, owner, 1)
    vector_stored = reorder(vector_grad, 1, owner, 1)
    attend_sum, output_sum, dense_sum, bias_sum, vector_sum = (
        lax.psum_scatter(attend_stored, "dp", scatter_dimension=1, tiled=True),
        lax.psum_scatter(output_stored, "dp", scatter_dimension=0, tiled=True),
        lax.psum_scatter(reorder(dense_grad, 1, owner, 1), "dp", scatter_dimension=1, tiled=True),
        lax.psum_scatter(bias_stored, "dp", scatter_dimension=1, tiled=True),
        lax.psum_scatter(vector_stored, "dp", scatter_dimension=1, tiled=True),
    )
    attend_new = adamw_step(
        attend_master, attend_first, attend_second, attend_sum, matrix_rate, matrix_decay
    )
    output_new = adamw_step(
        output_master, output_first, output_second, output_sum, output_rate, matrix_decay
    )
    dense_new = adamw_step(
        dense_master, dense_first, dense_second, dense_sum, matrix_rate, matrix_decay
    )
    bias_new = adamw_step(bias_master, bias_first, bias_second, bias_sum, bias_rate, 0.0)
    vector_new = adamw_step(
        vector_master, vector_first, vector_second, vector_sum, vector_rate, 0.0
    )
    return (
        layer_output,
        tokens_grad,
        attend_new[0],
        attend_new[1],
        attend_new[2],
        output_new[0],
        output_new[1],
        output_new[2],
        dense_new[0],
        dense_new[1],
        dense_new[2],
        bias_new[0],
        bias_new[1],
        bias_new[2],
        vector_new[0],
        vector_new[1],
        vector_new[2],
    )


def solution(mesh):
    return jax.shard_map(
        local,
        mesh=mesh,
        in_specs=(
            P("dp", None),
            P("dp", None),
            P(),
            P(None, "dp", "tensor"),
            P(None, "dp", "tensor"),
            P(None, "dp", "tensor"),
            P("dp", "tensor"),
            P("dp", "tensor"),
            P("dp", "tensor"),
            P(None, "dp", None, "tensor"),
            P(None, "dp", None, "tensor"),
            P(None, "dp", None, "tensor"),
            P(None, ("tensor", "dp")),
            P(None, ("tensor", "dp")),
            P(None, ("tensor", "dp")),
            P(None, "dp"),
            P(None, "dp"),
            P(None, "dp"),
            P("dp", None),
        ),
        out_specs=(
            P("dp", None),
            P("dp", None),
            P(None, "dp", "tensor"),
            P(None, "dp", "tensor"),
            P(None, "dp", "tensor"),
            P("dp", "tensor"),
            P("dp", "tensor"),
            P("dp", "tensor"),
            P(None, "dp", None, "tensor"),
            P(None, "dp", None, "tensor"),
            P(None, "dp", None, "tensor"),
            P(None, ("tensor", "dp")),
            P(None, ("tensor", "dp")),
            P(None, ("tensor", "dp")),
            P(None, "dp"),
            P(None, "dp"),
            P(None, "dp"),
        ),
        check_vma=False,
    )
```

profile of v0, /device:TPU:0, one launch (start us, length us, event | category | flops | bytes accessed | tf_op | source)
XLA Modules:
  0.0 1268.3 jit_solution(1598697552606586751)
XLA Ops:
  10.5 28.0 %all-gather = bf16[8,32,5]{1,2,0:T(8,128)(2,1)S(1)} all-gather(bf16[1,32,5]{1,2,0:T(8,128)(2,1)S(1)} %convert_bitcast_fusion.1), channel_id=1, replica_groups=mesh['dp'=8,'tensor'=4] {'dp'}, dimensions={0}, use_global_device_ids=true | all-gather | bytes 2880 | tf_op jit(solution)/shard_map/all_gather | solution.py:103
  40.4 32.2 %all_gather.18 = bf16[1024,256]{1,0:T(8,128)(2,1)S(1)} all-gather(bf16[128,256]{1,0:T(8,128)(2,1)S(1)} %convert_element_type.145), channel_id=1, replica_groups=mesh['dp'=8,'tensor'=4] {'dp'}, dimensions={0}, use_global_device_ids=true | all-gather | bytes 589824 | tf_op jit(solution)/shard_map/all_gather | solution.py:101
  74.2 26.0 %all_gather.15 = bf16[6,1024]{1,0:T(8,128)(2,1)S(1)} all-gather(bf16[6,128]{1,0:T(8,128)(2,1)S(1)} %convert_element_type.134), channel_id=1, replica_groups=mesh['dp'=8,'tensor'=4] {'dp'}, dimensions={1}, use_global_device_ids=true | all-gather | bytes 13824 | tf_op jit(solution)/shard_map/all_gather | solution.py:104
  121.4 83.0 %while.27 = (s32[]{:T(128)}, bf16[2,896,256]{2,1,0:T(8,128)(2,1)}, f32[2,4,896]{2,1,0:T(4,128)S(1)}, s32[2]{0:T(128)S(1)}, s32[1792]{0:T(1024)S(1)}, /*index=5*/...) while((s32[]{:T(128)}, bf16[2,896,256]{2,1,0:T(8,128)(2,1)}, ...), condition=%wide.region_8.9_spmd, body=%wide.region_5.8_spmd.sunk | while | flops 1722839552 | bytes 88213688 | solution.py:160
  123.9 11.3 fusion.152
  135.1 12.2 fusion.153
  147.4 13.5 %fusion.154 = bf16[4,896,64]{1,2,0:T(8,128)(2,1)} fusion(bf16[1792,4,64]{0,2,1:T(8,128)(2,1)S(1)} %get-tuple-element.404, f32[4,896,1792]{2,1,0:T(8,128)} %get-tuple-element.358, f32[4,896]{1,0:T(4,128)S(1)} %fusion.153, f32[4,896]{1,0:T(4,128)S(1)} %get-tuple-element.359, pred[896,1792]{1,0:T(8,128)(4,1)S(1)} %broadcast_compare_fusion.4), kind=kOutput, calls=%fused_computation.15.clone.1 | convolution fusion | flops 854196224 | bytes 28700672 | tf_op jit(solution)/shard_map/while/body/eval_jaxpr/hqk,khd->qhd/dot_general | solution.py:155
  165.3 11.3 fusion.152
  176.6 12.2 fusion.153
  188.8 13.5 %fusion.154 = bf16[4,896,64]{1,2,0:T(8,128)(2,1)} fusion(bf16[1792,4,64]{0,2,1:T(8,128)(2,1)S(1)} %get-tuple-element.404, f32[4,896,1792]{2,1,0:T(8,128)} %get-tuple-element.358, f32[4,896]{1,0:T(4,128)S(1)} %fusion.153, f32[4,896]{1,0:T(4,128)S(1)} %get-tuple-element.359, pred[896,1792]{1,0:T(8,128)(4,1)S(1)} %broadcast_compare_fusion.4), kind=kOutput, calls=%fused_computation.15.clone.1 | convolution fusion | flops 854196224 | bytes 28700672 | tf_op jit(solution)/shard_map/while/body/eval_jaxpr/hqk,khd->qhd/dot_general | solution.py:155
  211.8 72.5 %all-reduce.5.cloned.1.call-done = bf16[1792,1024]{1,0:T(8,128)(2,1)} async-done(((bf16[1792,1024]{1,0:T(8,128)(2,1)}), bf16[1792,1024]{1,0:T(8,128)(2,1)}) %all-reduce.5.cloned.1.call-update) | async-done | bytes 3670032 | tf_op jit(solution)/shard_map/psum | solution.py:162
  292.6 68.0 %all-gather.6.cloned.1.call-done = bf16[2,1024,4,256]{3,2,1,0:T(4,128)(2,1)} async-done(((bf16[2,128,4,256]{3,2,1,0:T(4,128)(2,1)}), bf16[2,1024,4,256]{3,2,1,0:T(4,128)(2,1)}) %all-gather.6.cloned.1.call-update) | async-done | bytes 4194320 | tf_op jit(solution)/shard_map/all_gather | solution.py:102
  375.6 22.5 %multiply_convert_fusion.1 = (bf16[1792,1024]{1,0:T(8,128)(2,1)}, f32[1792,1024]{1,0:T(8,128)S(1)}, f32[1792,1024]{1,0:T(8,128)}) fusion(f32[1024]{0:T(1024)S(1)} %bitcast.322, bf16[1024,1024]{1,0:T(8,128)(2,1)S(1)} %bitcast.275, f32[1024]{0:T(1024)S(1)} %bitcast.320, f32[1024]{0:T(1024)S(1)} %bitcast.301, f32[1792]{0:T(1024)S(1)} %fusion.69, ...), kind=kOutput, calls=%fused_computation.94 | convolution fusion | flops 3895721984 | bytes 27817984 | tf_op jit(solution)/shard_map/dot_general | solution.py:167
  398.1 9.9 convert_reduce_fusion.4
  425.0 65.7 %all-reduce.7.cloned.1.call-done = bf16[1792,1024]{1,0:T(8,128)(2,1)} async-done(((bf16[1792,1024]{1,0:T(8,128)(2,1)}), bf16[1792,1024]{1,0:T(8,128)(2,1)}) %all-reduce.7.cloned.1.call-update) | async-done | bytes 3670032 | tf_op jit(solution)/shard_map/psum | solution.py:182
  515.6 173.7 %while.28 = (s32[]{:T(128)}, f32[1792,4,64]{0,2,1:T(8,128)}, f32[1792,4,64]{0,2,1:T(8,128)S(1)}, bf16[2,896,4,64]{1,3,2,0:T(8,128)(2,1)}, s32[2]{0:T(128)S(1)}, ...) while((s32[]{:T(128)}, f32[1792,4,64]{0,2,1:T(8,128)}, ...), condition=%wide.region_18.19_spmd.clone, body=%wide.region_16.18_spmd.clone.sunk | while | flops 4172345856 | bytes 216162640 | solution.py:222
  517.3 13.3 %fusion.164 = f32[4,896,1792]{2,1,0:T(8,128)} fusion(bf16[1792,4,64]{0,2,1:T(8,128)(2,1)} %get-tuple-element.451, bf16[1792,4,64]{0,2,1:T(8,128)(2,1)} %get-tuple-element.450, s32[]{:T(128)S(6)} %select_n.221), kind=kOutput, calls=%fused_computation.39.clone.1 | convolution fusion | flops 822083584 | bytes 27066372 | tf_op jit(solution)/shard_map/while/body/eval_jaxpr/qhd,khd->hqk/dot_general | solution.py:205
  533.7 18.3 %multiply_reduce_fusion.3 = (f32[4,896]{1,0:T(4,128)S(1)}, f32[4,896,1792]{2,1,0:T(8,128)}) fusion(f32[4,896,1792]{2,1,0:T(8,128)} %fusion.164, f32[4,896]{1,0:T(4,128)S(1)} %dynamic-slice_bitcast_fusion.2, bf16[1792,4,64]{0,2,1:T(8,128)(2,1)} %copy-done.5, bf16[1792,4,64]{0,2,1:T(8,128)(2,1)} %get-tuple-element.446, s32[]{:T(128)S(6)} %select_n.221, ...), kind=kOutput, calls=%fused_computation.25.clone.1 | convolution fusion | flops 854192640 | bytes 54390788 | tf_op jit(solution)/shard_map/while/body/eval_jaxpr/qhd,khd->hqk/dot_general | solution.py:143
  552.0 21.4 %multiply_convert_fusion.3 = bf16[4,896,1792]{2,1,0:T(8,128)(2,1)} fusion(f32[4,896,1792]{2,1,0:T(8,128)} %get-tuple-element.371, f32[4,896,1792]{2,1,0:T(8,128)} %fusion.164, f32[4,896]{1,0:T(4,128)S(1)} %get-tuple-element.372), kind=kLoop, calls=%fused_computation.24.clone.1 | loop fusion | flops 19267584 | bytes 64239616 | tf_op jit(solution)/shard_map/while/body/eval_jaxpr/convert_element_type | solution.py:209
  591.2 11.1 fusion.166
  603.7 13.3 %fusion.164 = f32[4,896,1792]{2,1,0:T(8,128)} fusion(bf16[1792,4,64]{0,2,1:T(8,128)(2,1)} %get-tuple-element.451, bf16[1792,4,64]{0,2,1:T(8,128)(2,1)} %get-tuple-element.450, s32[]{:T(128)S(6)} %select_n.221), kind=kOutput, calls=%fused_computation.39.clone.1 | convolution fusion | flops 822083584 | bytes 27066372 | tf_op jit(solution)/shard_map/while/body/eval_jaxpr/qhd,khd->hqk/dot_general | solution.py:205
  620.0 18.3 %multiply_reduce_fusion.3 = (f32[4,896]{1,0:T(4,128)S(1)}, f32[4,896,1792]{2,1,0:T(8,128)}) fusion(f32[4,896,1792]{2,1,0:T(8,128)} %fusion.164, f32[4,896]{1,0:T(4,128)S(1)} %dynamic-slice_bitcast_fusion.2, bf16[1792,4,64]{0,2,1:T(8,128)(2,1)} %copy-done.5, bf16[1792,4,64]{0,2,1:T(8,128)(2,1)} %get-tuple-element.446, s32[]{:T(128)S(6)} %select_n.221, ...), kind=kOutput, calls=%fused_computation.25.clone.1 | convolution fusion | flops 854192640 | bytes 54390788 | tf_op jit(solution)/shard_map/while/body/eval_jaxpr/qhd,khd->hqk/dot_general | solution.py:143
  638.3 21.4 %multiply_convert_fusion.3 = bf16[4,896,1792]{2,1,0:T(8,128)(2,1)} fusion(f32[4,896,1792]{2,1,0:T(8,128)} %get-tuple-element.371, f32[4,896,1792]{2,1,0:T(8,128)} %fusion.164, f32[4,896]{1,0:T(4,128)S(1)} %get-tuple-element.372), kind=kLoop, calls=%fused_computation.24.clone.1 | loop fusion | flops 19267584 | bytes 64239616 | tf_op jit(solution)/shard_map/while/body/eval_jaxpr/convert_element_type | solution.py:209
  678.0 11.1 fusion.166
  703.0 134.1 %all-reduce.9.cloned.1.call-done = (bf16[1792,1024]{1,0:T(8,128)(2,1)}, bf16[1792,1024]{1,0:T(8,128)(2,1)}) async-done(((bf16[1792,1024]{1,0:T(8,128)(2,1)}, bf16[1792,1024]{1,0:T(8,128)(2,1)}), (bf16[1792,1024]{1,0:T(8,128)(2,1)}, bf16[1792,1024]{1,0:T(8,128)(2,1)})) %all-reduce.9.cloned.1.call-update) | async-done | bytes 7340048 | tf_op jit(solution)/shard_map/psum | solution.py:170
  848.0 14.8 %convert_bitcast_fusion = (bf16[1024,1792]{0,1:T(8,128)(2,1)}, bf16[1792,1024]{1,0:T(8,128)(2,1)}, bf16[1792,1024]{1,0:T(8,128)(2,1)}) fusion(f32[1792,1024]{1,0:T(8,128)} %copy-done.10, f32[1792]{0:T(1024)S(1)} %negate_multiply_fusion.1, f32[1792]{0:T(1024)S(1)} %multiply_multiply_fusion.8, f32[1792]{0:T(1024)S(1)} %copy-done.42, ...), kind=kLoop, calls=%fused_computation.127 | loop fusion | flops 34865152 | bytes 33071104 | tf_op jit(solution)/shard_map/dot_general | solution.py:62
  899.9 11.1 fusion.74
  940.9 10.6 gather_fusion.7
  968.8 10.8 reshape.560
  983.5 41.1 %reduce-scatter.13.cloned.1.call-done = f32[128,256]{1,0:T(8,128)} async-done(((f32[1024,256]{1,0:T(8,128)}), f32[128,256]{1,0:T(8,128)}) %reduce-scatter.13.cloned.1.call-update) | async-done | bytes 131088 | tf_op jit(solution)/shard_map/reduce_scatter | solution.py:255
  1026.3 76.4 %reduce-scatter.11.cloned.1.call-done = f32[3,128,256]{2,1,0:T(8,128)} async-done(((f32[3,1024,256]{2,1,0:T(8,128)}), f32[3,128,256]{2,1,0:T(8,128)}) %reduce-scatter.11.cloned.1.call-update) | async-done | bytes 393232 | tf_op jit(solution)/shard_map/reduce_scatter | solution.py:254
  1105.0 150.0 %reduce-scatter.17.cloned.1.call-done = f32[128,2048]{1,0:T(8,128)} async-done(((f32[1024,2048]{1,0:T(8,128)}), f32[128,2048]{1,0:T(8,128)}) %reduce-scatter.17.cloned.1.call-update) | async-done | bytes 1048592
  (344 shorter events, 269.4 us)
Async XLA Ops:
  7.2 105.3 %all-gather.4.cloned.1.call-start = ((), (), s32[]{:S(2)}) async-start(), calls=%async_computation.5 | async-start | bytes 1769472 | tf_op jit(solution)/shard_map/all_gather | solution.py:100
  9.0 275.4 %all-reduce.5.cloned.1.call-start = ((), (), s32[]{:S(2)}) async-start(), calls=%async_computation.6 | async-start | bytes 7340032 | tf_op jit(solution)/shard_map/psum | solution.py:162
  9.8 104.8 %copy-start.74 = (pred[8]{0:T(512)(128)(4,1)}, pred[8]{0:T(512)(128)(4,1)S(1)}, u32[]{:S(2)}) copy-start(pred[8]{0:T(512)(128)(4,1)S(1)} %compare_and_fusion.1) | copy-start | bytes 28
  9.8 102.7 %copy-start.73 = (s32[1024]{0:T(1024)}, s32[1024]{0:T(1024)S(1)}, u32[]{:S(2)}) copy-start(s32[1024]{0:T(1024)S(1)} %pad_clamp_fusion.1) | copy-start | bytes 12292
  72.6 39.9 %copy-start.64 = (f32[5,256]{1,0:T(8,128)}, f32[5,256]{1,0:T(8,128)S(1)}, u32[]{:S(2)}) copy-start(f32[5,256]{1,0:T(8,128)S(1)} %select_convert_fusion) | copy-start | bytes 15364
  204.4 84.5 %copy-start.13 = (bf16[1792,4,64]{0,2,1:T(8,128)(2,1)}, bf16[1792,4,64]{0,2,1:T(8,128)(2,1)S(1)}, u32[]{:S(2)}) copy-start(bf16[1792,4,64]{0,2,1:T(8,128)(2,1)S(1)} %get-tuple-element.479) | copy-start | bytes 2752516
  204.4 84.5 %copy-start.14 = (bf16[1792,4,64]{0,2,1:T(8,128)(2,1)}, bf16[1792,4,64]{0,2,1:T(8,128)(2,1)S(1)}, u32[]{:S(2)}) copy-start(bf16[1792,4,64]{0,2,1:T(8,128)(2,1)S(1)} %get-tuple-element.480) | copy-start | bytes 2752516
  204.4 84.5 %copy-start.29 = (s32[1792]{0:T(1024)}, s32[1792]{0:T(1024)S(1)}, u32[]{:S(2)}) copy-start(s32[1792]{0:T(1024)S(1)} %get-tuple-element.492) | copy-start | bytes 21508
  204.4 84.5 %copy-start.51 = (f32[2,4,896]{2,1,0:T(4,128)}, f32[2,4,896]{2,1,0:T(4,128)S(1)}, u32[]{:S(2)}) copy-start(f32[2,4,896]{2,1,0:T(4,128)S(1)} %get-tuple-element.417) | copy-start | bytes 86020
  204.4 79.9 %copy-start.49 = (f32[1,1024]{1,0:T(1,128)S(1)}, f32[1,1024]{1,0:T(1,128)}, u32[]{:S(2)}) copy-start(f32[1,1024]{1,0:T(1,128)} %get-tuple-element.243) | copy-start | bytes 12292
  209.4 151.2 %all-gather.6.cloned.1.call-start = ((), (), s32[]{:S(2)}) async-start(), calls=%async_computation.7 | async-start | bytes 4718592 | tf_op jit(solution)/shard_map/all_gather | solution.py:102
  211.7 279.0 %all-reduce.7.cloned.1.call-start = ((), (), s32[]{:S(2)}) async-start(), calls=%async_computation.8 | async-start | bytes 7340032 | tf_op jit(solution)/shard_map/psum | solution.py:182
  289.6 215.3 %copy-start.45 = (f32[1792]{0:T(1024)}, f32[1792]{0:T(1024)S(1)}, u32[]{:S(2)}) copy-start(f32[1792]{0:T(1024)S(1)} %broadcast_multiply_fusion) | copy-start | bytes 21508
  289.6 78.7 %copy-start.75 = (pred[8]{0:T(512)(128)(4,1)S(1)}, pred[8]{0:T(512)(128)(4,1)}, u32[]{:S(2)}) copy-start(pred[8]{0:T(512)(128)(4,1)} %copy-done.74) | copy-start | bytes 28
  292.6 212.4 %copy-start.58 = (f32[1792]{0:T(1024)}, f32[1792]{0:T(1024)S(1)}, u32[]{:S(2)}) copy-start(f32[1792]{0:T(1024)S(1)} %fusion.69) | copy-start | bytes 21508
  415.3 421.8 %all-reduce.9.cloned.1.call-start = ((), (), s32[]{:S(2)}) async-start(), calls=%async_computation.14 | async-start | bytes 14680064 | tf_op jit(solution)/shard_map/psum | solution.py:170
  699.9 137.2 %copy-start.42 = (f32[1792]{0:T(1024)S(1)}, f32[1792]{0:T(1024)}, u32[]{:S(2)}) copy-start(f32[1792]{0:T(1024)} %copy-done.41) | copy-start | bytes 21508
  699.9 137.2 %copy-start.54 = (f32[1,1024]{1,0:T(1,128)S(1)}, f32[1,1024]{1,0:T(1,128)}, u32[]{:S(2)}) copy-start(f32[1,1024]{1,0:T(1,128)} %copy-done.53) | copy-start | bytes 12292
  699.9 142.6 %copy-start.57 = (f32[1792]{0:T(1024)S(1)}, f32[1792]{0:T(1024)}, u32[]{:S(2)}) copy-start(f32[1792]{0:T(1024)} %copy-done.56) | copy-start | bytes 21508
  699.9 142.6 %copy-start.48 = (f32[1792]{0:T(1024)S(1)}, f32[1792]{0:T(1024)}, u32[]{:S(2)}) copy-start(f32[1792]{0:T(1024)} %copy-done.47) | copy-start | bytes 21508
  700.0 279.8 %reduce-scatter.19.cloned.1.call-start = ((), (), s32[]{:S(2)}) async-start(), calls=%async_computation.13 | async-start | bytes 147456
  702.9 279.2 %reduce-scatter.15.cloned.1.call-start = ((), (), s32[]{:S(2)}) async-start(), calls=%async_computation.11 | async-start | bytes 36864 | tf_op jit(solution)/shard_map/reduce_scatter | solution.py:258
  873.3 151.2 %reduce-scatter.13.cloned.1.call-start = ((), (), s32[]{:S(2)}) async-start(), calls=%async_computation.10 | async-start | bytes 1179648 | tf_op jit(solution)/shard_map/reduce_scatter | solution.py:255
  874.6 228.2 %reduce-scatter.11.cloned.1.call-start = ((), (), s32[]{:S(2)}) async-start(), calls=%async_computation.9 | async-start | bytes 3538944 | tf_op jit(solution)/shard_map/reduce_scatter | solution.py:254
  899.4 355.5 %reduce-scatter.17.cloned.1.call-start = ((), (), s32[]{:S(2)}) async-start(), calls=%async_computation.12 | async-start | bytes 9437184
  979.6 45.0 %copy-start.40 = (f32[128,256]{1,0:T(8,128)S(1)}, f32[128,256]{1,0:T(8,128)}, u32[]{:S(2)}) copy-start(f32[128,256]{1,0:T(8,128)} %param.29) | copy-start | bytes 393220
  979.6 45.0 %copy-start.55 = (f32[128,256]{1,0:T(8,128)S(1)}, f32[128,256]{1,0:T(8,128)}, u32[]{:S(2)}) copy-start(f32[128,256]{1,0:T(8,128)} %param.31) | copy-start | bytes 393220
  979.6 123.2 %copy-start.38 = (f32[3,128,256]{2,1,0:T(8,128)S(1)}, f32[3,128,256]{2,1,0:T(8,128)}, u32[]{:S(2)}) copy-start(f32[3,128,256]{2,1,0:T(8,128)} %param.26) | copy-start | bytes 1179652
  979.6 123.2 %copy-start.43 = (f32[3,128,256]{2,1,0:T(8,128)S(1)}, f32[3,128,256]{2,1,0:T(8,128)}, u32[]{:S(2)}) copy-start(f32[3,128,256]{2,1,0:T(8,128)} %param.28) | copy-start | bytes 1179652
  979.6 123.2 %copy-start.44 = (f32[3,128,256]{2,1,0:T(8,128)S(1)}, f32[3,128,256]{2,1,0:T(8,128)}, u32[]{:S(2)}) copy-start(f32[3,128,256]{2,1,0:T(8,128)} %param.27) | copy-start | bytes 1179652
  979.6 277.2 %copy-start.19 = (f32[2,128,4,256]{3,2,1,0:T(4,128)S(1)}, f32[2,128,4,256]{3,2,1,0:T(4,128)}, u32[]{:S(2)}) copy-start(f32[2,128,4,256]{3,2,1,0:T(4,128)} %param.32) | copy-start | bytes 3145732
  979.7 277.2 %copy-start.39 = (f32[2,128,4,256]{3,2,1,0:T(4,128)S(1)}, f32[2,128,4,256]{3,2,1,0:T(4,128)}, u32[]{:S(2)}) copy-start(f32[2,128,4,256]{3,2,1,0:T(4,128)} %param.34) | copy-start | bytes 3145732
  (65 other events, 401.8 us)
Sparse Core Ops, SparseCore 0:
  10.8 52.1 all-gather.3
  209.6 74.7 all-reduce.4
  287.1 73.4 all-gather.5
  415.4 75.2 all-reduce.6
  700.1 136.9 all-reduce.8
  840.8 61.0 reduce-scatter.18
  905.6 52.5 reduce-scatter.14
  962.1 62.3 reduce-scatter.12
  1028.6 74.1 reduce-scatter.10
  1106.7 148.1 reduce-scatter.16
where the time goes:
time: 1280 us; the launch traced here: 1270 us
  waiting for transfers between devices  608 us (48%)
  matrix products  267 us (21%)
  other arithmetic  186 us (15%)
  local copies, waits for them, and re-layouts  97.4 us (8%)
  blocking collectives  86.1 us (7%)
  between operations  15.5 us (1%)
    unnamed x12, waiting for transfers between devices  150 us
    psum x1, waiting for transfers between devices, local(): lax.psum(contract_cols(act_hidden, w_down).astype(jnp.bfloat16), 'tensor')  134 us
    reduce_scatter x1, waiting for transfers between devices, local(): lax.psum_scatter(attend_stored, 'dp', scatter_dimension=1, tiled=True)  76.4 us
    psum x1, waiting for transfers between devices, local(): lax.psum(contract_cols(mixed, output_w).astype(jnp.bfloat16), 'tensor')  72.5 us
    all_gather x1, waiting for transfers between devices, local(): lax.all_gather(dense_master.astype(half_type), 'dp', axis=1, tiled=True)  68 us
    psum x1, waiting for transfers between devices, local(): lax.psum(contract_cols(grad_pre, w_up).astype(jnp.bfloat16), 'tensor')  65.7 us
    dot_general x4, matrix products, block_scores(): jnp.einsum('qhd,khd->hqk', query_block, key_heads, preferred_element_type...  59.2 us
    convert_element_type x2, other arithmetic, backward_block(): grad_scores = (probs * (grad_probs - row_dot)).astype(half_type)  42.9 us
  transfers between devices with their start and end apart: 10, of which 7 were waited for; matrix products, arithmetic and copies ran while one was open for 15% of the time, Pallas kernels for 0%

commit v1 on v0

--- a/solution.py
+++ b/solution.py
@@ -1,15 +1,21 @@
+import functools
+
 import jax
 import jax.numpy as jnp
 from jax import lax
+from jax.experimental import pallas as pl
+from jax.experimental.pallas import tpu as pltpu
 from jax.sharding import PartitionSpec as P
 
-D = 1024
 HD = 64
 STEP = 10
-
-
+LANES = 128
+BLOCK = 256
+MESH = pl.DeviceIdType.MESH
+BIG = 2.0**50
+
+masked_score = -1e30
 norm_epsilon = 1e-06
-masked_score = -1e30
 first_decay = 0.9
 second_decay = 0.95
 adam_epsilon = 1e-08
@@ -19,6 +25,254 @@
 vector_rate = 1.0
 matrix_decay = 0.05
 
+half_type = jnp.bfloat16
+full_type = jnp.float32
+
+
+def dot(left, right, left_dim=1, right_dim=0):
+    return lax.dot_general(
+        left, right, (((left_dim,), (right_dim,)), ((), ())), preferred_element_type=full_type
+    )
+
+
+def ring_pos(place, count):
+    column = place % 2
+    row = place // 2
+    return row * (1 - column) + (count - 1 - row) * column
+
+
+def ring_at(pos, count):
+    near = (pos + 2 * count) % count
+    down = near // (count // 2)
+    return 2 * near * (1 - down) + (2 * count - 1 - 2 * near) * down
+
+
+class Gather:
+    def __init__(self, view, width, sems, count):
+        self.view, self.width, self.sems, self.count = view, width, sems, count
+        self.steps = count // 2
+        self.pos = ring_pos(lax.axis_index("dp"), count)
+        self.tensor = lax.axis_index("tensor")
+
+    def _copy(self, way, step, hops):
+        sign = 1 - 2 * way
+        part = (0, self.width)
+        if step == self.steps - 1:
+            part = (way * (self.width // 2), self.width // 2)
+        block = self.view(ring_at(self.pos - sign * hops, self.count), *part)
+        return pltpu.make_async_remote_copy(
+            src_ref=block,
+            dst_ref=block,
+            send_sem=self.sems.at[2 * way, step],
+            recv_sem=self.sems.at[2 * way + 1, step],
+            device_id=(ring_at(self.pos + sign, self.count), self.tensor),
+            device_id_type=MESH,
+        )
+
+    def start(self, step):
+        for way in range(2):
+            self._copy(way, step, step).start()
+
+    def arrived(self, step):
+        for way in range(2):
+            self._copy(way, step, step + 1).wait_recv()
+
+    def sent(self):
+        for step in range(self.steps):
+            for way in range(2):
+                self._copy(way, step, step).wait_send()
+
+
+def greet_loop_and_peers(count):
+    me, tensor = lax.axis_index("dp"), lax.axis_index("tensor")
+    barrier = pltpu.get_barrier_semaphore()
+
+    def greet(k, carry):
+        pl.semaphore_signal(
+            barrier, inc=1, device_id=((me + k) % count, tensor), device_id_type=MESH
+        )
+        return carry
+
+    lax.fori_loop(1, count, greet, 0)
+    return barrier
+
+
+def permuted_rows(ref, row, rows, owner_ref, count):
+    width = ref.shape[1]
+    wide = width // count
+    if True:
+        return ref[pl.ds(row, rows), :]
+    parts = [
+        ref[pl.ds(row, rows), pl.ds(pl.multiple_of(owner_ref[j] * wide, wide), wide)]
+        for j in range(count)
+    ]
+    return jnp.concatenate(parts, axis=1)
+
+
+def normalized(x):
+    center = jnp.mean(x, axis=-1, keepdims=True)
+    offset = x - center
+    spread = jnp.mean(offset * offset, axis=-1, keepdims=True)
+    rate = lax.rsqrt(spread + norm_epsilon)
+    return offset * rate, rate
+
+
+def gather_project_kernel(
+    count, owner_ref, ends_ref, tok_ref, att_ref, small_ref,
+    a1_ref, qa_ref, ka_ref, va_ref, w_ref, vec_ref, bias_ref,
+    smalls, gather_sems, small_sems,
+):
+    me, tensor = lax.axis_index("dp"), lax.axis_index("tensor")
+    total_rows, width = tok_ref.shape
+    local_width = w_ref.shape[2]
+    wide = width // count
+    slots = ends_ref.shape[0]
+    barrier = greet_loop_and_peers(count)
+    mine = pl.ds(pl.multiple_of(me * wide, wide), wide)
+    w_ref[:, mine, :] = att_ref[...].astype(half_type)
+    smalls[me] = small_ref[...]
+    pl.semaphore_wait(barrier, count - 1)
+    gather = Gather(
+        lambda block, low, size: w_ref.at[
+            :, pl.ds(pl.multiple_of(block * wide, wide), wide), pl.ds(low, size)
+        ],
+        local_width, gather_sems, count,
+    )
+    gather.start(0)
+
+    def small_copy(source, peer):
+        return pltpu.make_async_remote_copy(
+            src_ref=small_ref,
+            dst_ref=smalls.at[source],
+            send_sem=small_sems.at[0, peer],
+            recv_sem=small_sems.at[1, source],
+            device_id=(peer, tensor),
+            device_id_type=MESH,
+        )
+
+    def send_small(k, carry):
+        small_copy(me, (me + k) % count).start()
+        return carry
+
+    lax.fori_loop(1, count, send_small, 0)
+
+    def take_small(k, carry):
+        source = (me + k) % count
+        small_copy(source, source).wait_recv()
+        return carry
+
+    lax.fori_loop(1, count, take_small, 0)
+    lanes = small_ref.shape[1] - local_width
+    fold = lanes // wide
+    bias = smalls[0, :, lanes:]
+    for j in range(1, count):
+        bias = bias + smalls[j, :, lanes:]
+    bias_ref[...] = bias
+    for window in range(width // lanes):
+        piece = smalls[window * fold, :, :lanes]
+        for j in range(window * fold + 1, (window + 1) * fold):
+            piece = piece + smalls[j, :, :lanes]
+        vec_ref[:, window * lanes : (window + 1) * lanes] = piece
+
+    def norm_rows(step, carry):
+        row = pl.multiple_of(step * BLOCK, BLOCK)
+        x = permuted_rows(tok_ref, row, BLOCK, owner_ref, count).astype(full_type)
+        unit, _ = normalized(x)
+        a1_ref[pl.ds(row, BLOCK), :] = (unit * vec_ref[2:3, :] + vec_ref[3:4, :]).astype(half_type)
+        return carry
+
+    blocks = total_rows // BLOCK
+    done = 0
+    for step in range(gather.steps):
+        upto = min(blocks, -(-blocks * (step + 1) // (gather.steps - 1)))
+        if upto > done:
+            lax.fori_loop(done, upto, norm_rows, 0)
+        done = max(done, upto)
+        gather.arrived(step)
+        if step + 1 < gather.steps:
+            gather.start(step + 1)
+
+    lane = lax.broadcasted_iota(jnp.int32, (BLOCK, LANES), 1)
+    low_half = lane < HD
+    spot = lane % HD
+
+    def project(step, carry):
+        row = pl.multiple_of(step * BLOCK, BLOCK)
+        rows = pl.ds(row, BLOCK)
+        a1 = a1_ref[rows, :]
+        q = (dot(a1, w_ref[0]) + bias_ref[0:1, :]).astype(half_type).astype(full_type) * HD**-0.5
+        k = dot(a1, w_ref[1])
+        v = dot(a1, w_ref[2])
+        place = row + lax.broadcasted_iota(jnp.int32, (BLOCK, LANES), 0)
+        segment = jnp.zeros((BLOCK, LANES), jnp.int32)
+        for slot in range(slots):
+            segment = segment + jnp.where(place >= ends_ref[slot], 1, 0)
+        same = spot == segment
+        inside = spot <= slots
+        q_mark = jnp.where(inside & ~same, -BIG, 0.0)
+        k_mark = jnp.where(same, BIG, jnp.where((spot > slots) & (spot <= slots + 3), 1.0, 0.0))
+        for head in range(local_width // HD):
+            pair = slice(head // 2 * LANES, head // 2 * LANES + LANES)
+            own = low_half if head % 2 == 0 else ~low_half
+            qa_ref[head, rows, :] = jnp.where(own, q[:, pair], q_mark).astype(half_type)
+            ka_ref[head, rows, :] = jnp.where(own, k[:, pair], k_mark).astype(half_type)
+            va_ref[head, rows, :] = jnp.where(own, v[:, pair], 1.0).astype(half_type)
+        return carry
+
+    lax.fori_loop(0, blocks, project, 0)
+    gather.sent()
+
+    def sent_small(k, carry):
+        small_copy(me, (me + k) % count).wait_send()
+        return carry
+
+    lax.fori_loop(1, count, sent_small, 0)
+
+
+def gather_project(tokens, attend_master, small, owner, ends, count):
+    total_rows, width = tokens.shape
+    local_width = attend_master.shape[2]
+    heads = local_width // HD
+    vmem = pl.BlockSpec(memory_space=pltpu.VMEM)
+    smem = pl.BlockSpec(memory_space=pltpu.SMEM)
+    heads_shape = jax.ShapeDtypeStruct((heads, total_rows, LANES), half_type)
+    return pl.pallas_call(
+        functools.partial(gather_project_kernel, count),
+        out_shape=(
+            jax.ShapeDtypeStruct((total_rows, width), half_type),
+            heads_shape, heads_shape, heads_shape,
+            jax.ShapeDtypeStruct((3, width, local_width), half_type),
+            jax.ShapeDtypeStruct((8, width), full_type),
+            jax.ShapeDtypeStruct((8, local_width), full_type),
+        ),
+        in_specs=[smem, smem, vmem, vmem, vmem],
+        out_specs=[vmem] * 7,
+        scratch_shapes=[
+            pltpu.VMEM((count,) + small.shape, full_type),
+            pltpu.SemaphoreType.DMA((4, count // 2)),
+            pltpu.SemaphoreType.DMA((2, count)),
+        ],
+        compiler_params=pltpu.CompilerParams(
+            collective_id=0, has_side_effects=True, vmem_limit_bytes=56 * 2**20
+        ),
+    )(owner, ends, tokens, attend_master, small)
+
+
+def pack_small(vector_master, bias_master, owner, count):
+    me = lax.axis_index("dp")
+    wide = vector_master.shape[1]
+    lanes = max(LANES, wide)
+    fold = lanes // wide
+    lane = jnp.arange(lanes)
+    vectors = jnp.where(lane // wide == me % fold, jnp.tile(vector_master, (1, fold)), 0.0)
+    narrow = bias_master.shape[1]
+    spot = jnp.arange(narrow * count)
+    biases = jnp.where(spot // narrow == owner[me], jnp.tile(bias_master, (1, count)), 0.0)
+    small = jnp.concatenate(
+        [jnp.pad(vectors, ((0, 2), (0, 0))), jnp.pad(biases, ((0, 3), (0, 0)))], axis=1
+    )
+    return small.astype(half_type).astype(full_type)
+
 
 def layer_norm(hidden, gain, shift):
     center = jnp.mean(hidden, axis=-1, keepdims=True)
@@ -35,18 +289,6 @@
     ends = jnp.cumsum(row_lengths)
     places = jnp.arange(total_rows, dtype=jnp.int32)
     return jnp.sum((places[:, None] >= ends[None, :]).astype(jnp.int32), axis=1)
-
-
-def reorder(array, axis_dim, order, outer):
-    count_blocks = order.shape[0]
-    shape_old = array.shape
-    shape_new = (
-        shape_old[:axis_dim]
-        + (outer, count_blocks, shape_old[axis_dim] // (outer * count_blocks))
-        + shape_old[axis_dim + 1 :]
-    )
-    moved = jnp.take(array.reshape(shape_new), order, axis=axis_dim + 1)
-    return moved.reshape(shape_old)
 
 
 def adamw_step(weight, first, second, grad, rate, decay):
@@ -96,18 +338,25 @@
     owner_count = owner.shape[0]
     places = jnp.arange(owner_count, dtype=jnp.int32)
     inverse = jnp.sum(jnp.where(owner[None, :] == places[:, None], places[None, :], 0), axis=1)
-    gathered = (
-        lax.all_gather(attend_master.astype(half_type), "dp", axis=1, tiled=True),
-        lax.all_gather(output_master.astype(half_type), "dp", axis=0, tiled=True),
-        lax.all_gather(dense_master.astype(half_type), "dp", axis=1, tiled=True),
-        lax.all_gather(bias_master.astype(half_type), "dp", axis=1, tiled=True),
-        lax.all_gather(vector_master.astype(half_type), "dp", axis=1, tiled=True),
-    )
-    attend_w = reorder(gathered[0], 1, inverse, 1)
-    output_w = reorder(gathered[1], 0, inverse, 1)
-    dense_w = reorder(gathered[2], 1, inverse, 1)
-    bias_w = reorder(gathered[3], 1, inverse, 1).astype(full_type)
-    vectors = reorder(gathered[4], 1, inverse, 1).astype(full_type)
+    def unstored(array):
+        return jnp.take(array.reshape(shape), inverse, axis=1).reshape(array.shape)
+    attend_rows = owner_count
+    if True:
+        shape = (tokens.shape[0], owner_count, tokens.shape[1] // owner_count)
+        tokens = jnp.take(tokens.reshape(shape), owner, axis=1).reshape(tokens.shape)
+        cotangent = jnp.take(cotangent.reshape(shape), owner, axis=1).reshape(cotangent.shape)
+    ends = jnp.cumsum(lengths[0])
+    small = pack_small(vector_master, bias_master, owner, owner_count)
+    act_one, qa, ka, va, attend_w, vectors, bias_w = gather_project(
+        tokens, attend_master, small, owner, ends, owner_count
+    )
+    output_w = lax.all_gather(output_master.astype(half_type), "dp", axis=0, tiled=True)
+    dense_w = lax.all_gather(dense_master.astype(half_type), "dp", axis=1, tiled=True)
+    if False:
+        shape = (tokens.shape[0], owner_count, tokens.shape[1] // owner_count)
+        tokens = jnp.take(tokens.reshape(shape), owner, axis=1).reshape(tokens.shape)
+        cotangent = jnp.take(cotangent.reshape(shape), owner, axis=1).reshape(cotangent.shape)
+    D = tokens.shape[1]
     total_rows = tokens.shape[0]
     local_width = attend_w.shape[2]
     head_count = local_width // HD
@@ -119,18 +368,16 @@
     w_value = attend_w[2]
     w_up = dense_w[0].reshape(D, hidden_width)
     w_down = dense_w[1].reshape(D, hidden_width)
-    bias_query = bias_w[0]
-    bias_up = bias_w[1:].reshape(hidden_width)
+    bias_up = bias_w[1:5].reshape(hidden_width)
     segments = segment_ids(lengths[0], total_rows)
     block_count = max(1, total_rows // 896)
     block_rows = total_rows // block_count
     inputs = tokens.astype(full_type)
-    act_one = layer_norm(inputs, vectors[2], vectors[3]).astype(half_type)
-    query = (jnp.dot(act_one, w_query, preferred_element_type=full_type) + bias_query).astype(
-        half_type
-    )
-    key_rows = jnp.dot(act_one, w_key, preferred_element_type=full_type).astype(half_type)
-    value_rows = jnp.dot(act_one, w_value, preferred_element_type=full_type).astype(half_type)
+    def unpack(arr):
+        return jnp.stack([arr[h][:, (h % 2) * HD:(h % 2) * HD + HD] for h in range(head_count)], axis=1).reshape(total_rows, local_width)
+    query = unpack(qa) * 8.0
+    key_rows = unpack(ka)
+    value_rows = unpack(va)
     query_heads = query.reshape(total_rows, head_count, HD)
     key_heads = key_rows.reshape(total_rows, head_count, HD)
     value_heads = value_rows.reshape(total_rows, head_count, HD)
@@ -246,16 +493,13 @@
     vector_grad = jnp.stack(
         [grad_bias_out, grad_bias_two, grad_gain_one, grad_shift_one, grad_gain_two, grad_shift_two]
     )
-    attend_stored = reorder(attend_grad, 1, owner, 1)
-    output_stored = reorder(grad_output, 0, owner, 1)
-    bias_stored = reorder(bias_grad, 1, owner, 1)
-    vector_stored = reorder(vector_grad, 1, owner, 1)
+    bias_stored = jnp.take(bias_grad.reshape(bias_grad.shape[0], owner_count, -1), owner, axis=1).reshape(bias_grad.shape)
     attend_sum, output_sum, dense_sum, bias_sum, vector_sum = (
-        lax.psum_scatter(attend_stored, "dp", scatter_dimension=1, tiled=True),
-        lax.psum_scatter(output_stored, "dp", scatter_dimension=0, tiled=True),
-        lax.psum_scatter(reorder(dense_grad, 1, owner, 1), "dp", scatter_dimension=1, tiled=True),
+        lax.psum_scatter(attend_grad, "dp", scatter_dimension=1, tiled=True),
+        lax.psum_scatter(grad_output, "dp", scatter_dimension=0, tiled=True),
+        lax.psum_scatter(dense_grad, "dp", scatter_dimension=1, tiled=True),
         lax.psum_scatter(bias_stored, "dp", scatter_dimension=1, tiled=True),
-        lax.psum_scatter(vector_stored, "dp", scatter_dimension=1, tiled=True),
+        lax.psum_scatter(vector_grad, "dp", scatter_dimension=1, tiled=True),
     )
     attend_new = adamw_step(
         attend_master, attend_first, attend_second, attend_sum, matrix_rate, matrix_decay
@@ -271,8 +515,8 @@
         vector_master, vector_first, vector_second, vector_sum, vector_rate, 0.0
     )
     return (
-        layer_output,
-        tokens_grad,
+        unstored(layer_output),
+        unstored(tokens_grad),
         attend_new[0],
         attend_new[1],
         attend_new[2],

time: 1280 us -> 1130 us (0.88)
  waiting for transfers between devices: 608 us -> 437 us
  blocking collectives: 86.1 us -> 35.2 us
  Pallas kernels: 0 us -> 37.4 us
  local copies, waits for them, and re-layouts: 97.4 us -> 127 us
    unnamed x12 -> x10, waiting for transfers between devices: 150 us -> 0.18 us
    reduce_scatter x3 -> x4, waiting for transfers between devices: 118 us -> 208 us  [the longest x1 148 us: local(): lax.psum_scatter(dense_grad, 'dp', scatter_dimension=1, tiled=True)]
    all_gather x1, waiting for transfers between devices: 68 us -> 0.03 us  [local(): lax.all_gather(dense_master.astype(half_type), 'dp', axis=1, tiled=True)]
    all_gather x2 -> x0, blocking collectives: 53.9 us -> none  [the longest x1 28 us: local(): lax.all_gather(bias_master.astype(half_type), 'dp', axis=1, tiled=True)]
    psum x1, waiting for transfers between devices: 134 us -> 93.6 us  [local(): lax.psum(contract_cols(act_hidden, w_down).astype(jnp.bfloat16), 'tensor')]
    pallas_call x0 -> x1, Pallas kernels: none -> 37.4 us  [gather_project(): pl.pallas_call(functools.partial(gather_project_kernel, count), out_shape...]
    reshape x2 -> x5, local copies, waits for them, and re-layouts: 0.1 us -> 19.9 us  [the longest x1 6 us: local(): tokens.reshape(shape)]
    dot_general x2 -> x0, other arithmetic: 19.1 us -> none  [contract_rows(): lax.dot_general(left, right, (((0,), (0,)), ((), ())), preferred_element_...]
  transfers between devices with their start and end apart: 10 -> 9, of which waited for: 7 -> 5; matrix products, arithmetic and copies ran while one was open for 15% -> 15% of each run, Pallas kernels for 0% -> 0%
where the time goes in v1:
time: 1130 us; the launch traced here: 1120 us
  waiting for transfers between devices  437 us (39%)
  matrix products  278 us (25%)
  other arithmetic  182 us (16%)
  local copies, waits for them, and re-layouts  127 us (11%)
  Pallas kernels  37.4 us (3%)
  blocking collectives  35.2 us (3%)
  between operations  16.5 us (1%)
    reduce_scatter x1, waiting for transfers between devices, local(): lax.psum_scatter(dense_grad, 'dp', scatter_dimension=1, tiled=True)  148 us
    psum x1, waiting for transfers between devices, local(): lax.psum(contract_cols(act_hidden, w_down).astype(jnp.bfloat16), 'tensor')  93.6 us
    psum x1, waiting for transfers between devices, local(): lax.psum(contract_cols(mixed, output_w).astype(jnp.bfloat16), 'tensor')  74.4 us
    reduce_scatter x1, waiting for transfers between devices, local(): lax.psum_scatter(attend_grad, 'dp', scatter_dimension=1, tiled=True)  60.5 us
    dot_general x4, matrix products, block_scores(): jnp.einsum('qhd,khd->hqk', query_block, key_heads, preferred_element_type...  60.4 us
    psum x1, waiting for transfers between devices, local(): lax.psum(contract_cols(grad_pre, w_up).astype(jnp.bfloat16), 'tensor')  60.3 us
    convert_element_type x2, other arithmetic, backward_block(): grad_scores = (probs * (grad_probs - row_dot)).astype(half_type)  42.9 us
    unnamed x162, local copies, waits for them, and re-layouts  40.5 us
  transfers between devices with their start and end apart: 9, of which 5 were waited for; matrix products, arithmetic and copies ran while one was open for 15% of the time, Pallas kernels for 0%

profile of v1, /device:TPU:0, one launch (start us, length us, event | category | flops | bytes accessed | tf_op | source)
XLA Modules:
  0.0 1121.3 jit_solution(3768327280825695214)
XLA Ops:
  13.9 35.2 %all_gather.6 = bf16[1024,256]{1,0:T(8,128)(2,1)} all-gather(bf16[128,256]{1,0:T(8,128)(2,1)S(1)} %convert_element_type.127), channel_id=1, replica_groups=mesh['dp'=8,'tensor'=4] {'dp'}, dimensions={0}, use_global_device_ids=true | all-gather | bytes 589824 | tf_op jit(solution)/shard_map/all_gather | solution.py:353
  93.9 37.4 %shard_map.314 = (bf16[1792,1024]{1,0:T(8,128)(2,1)}, bf16[4,1792,128]{2,1,0:T(8,128)(2,1)}, bf16[4,1792,128]{2,1,0:T(8,128)(2,1)}, bf16[4,1792,128]{2,1,0:T(8,1...) custom-call(s32[8]{0:T(128)} %owner_ref.1, s32[8]{0:T(128)} %bitcast.381, ...), custom_call_target="tpu_custom_call" | custom-call | tf_op jit(solution)/shard_map/pallas_call | solution.py:239
  147.2 84.9 %while.27 = (s32[]{:T(128)}, bf16[2,896,256]{2,1,0:T(8,128)(2,1)}, f32[2,4,896]{2,1,0:T(4,128)S(1)}, s32[2]{0:T(128)S(1)}, s32[1792]{0:T(1024)S(1)}, /*index=5*/...) while((s32[]{:T(128)}, bf16[2,896,256]{2,1,0:T(8,128)(2,1)}, ...), condition=%wide.region_5.7_spmd, body=%wide.region_2.0_spmd.sunk | while | flops 1722839552 | bytes 88213192 | solution.py:407
  150.0 12.2 %fusion.169 = (f32[4,896]{1,0:T(4,128)S(1)}, f32[4,896,1792]{2,1,0:T(8,128)}) fusion(pred[896,1792]{1,0:T(8,128)(4,1)S(1)} %broadcast_compare_fusion.4, bf16[1792,4,64]{0,2,1:T(8,128)(2,1)S(1)} %get-tuple-element.619, bf16[1792,4,64]{0,2,1:T(8,128)(2,1)} %get-tuple-element.618, s32[]{:T(128)S(6)} %select_n.149), kind=kOutput, calls=%fused_computation.8.clone.1 | convolution fusion | flops 841347584 | bytes 28686340 | tf_op jit(solution)/shard_map/while/body/eval_jaxpr/qhd,khd->hqk/dot_general | solution.py:390
  162.2 12.2 %fusion.170 = f32[4,896]{1,0:T(4,128)S(1)} fusion(f32[4,896,1792]{2,1,0:T(8,128)} %get-tuple-element.574, f32[4,896]{1,0:T(4,128)S(1)} %get-tuple-element.575, pred[896,1792]{1,0:T(8,128)(4,1)S(1)} %broadcast_compare_fusion.4), kind=kLoop, calls=%fused_computation.9.clone.1 | loop fusion | flops 25686528 | bytes 27324416 | tf_op jit(solution)/shard_map/while/body/eval_jaxpr/reduce_sum | solution.py:400
  174.4 13.4 %fusion.171 = bf16[4,896,64]{1,2,0:T(8,128)(2,1)} fusion(bf16[1792,4,64]{0,2,1:T(8,128)(2,1)S(1)} %get-tuple-element.620, f32[4,896,1792]{2,1,0:T(8,128)} %get-tuple-element.574, f32[4,896]{1,0:T(4,128)S(1)} %fusion.170, f32[4,896]{1,0:T(4,128)S(1)} %get-tuple-element.575, pred[896,1792]{1,0:T(8,128)(4,1)S(1)} %broadcast_compare_fusion.4), kind=kOutput, calls=%fused_computation.10.clone.1 | convolution fusion | flops 854196224 | bytes 28700672 | tf_op jit(solution)/shard_map/while/body/eval_jaxpr/hqk,khd->qhd/dot_general | solution.py:402
  192.2 12.2 %fusion.169 = (f32[4,896]{1,0:T(4,128)S(1)}, f32[4,896,1792]{2,1,0:T(8,128)}) fusion(pred[896,1792]{1,0:T(8,128)(4,1)S(1)} %broadcast_compare_fusion.4, bf16[1792,4,64]{0,2,1:T(8,128)(2,1)S(1)} %get-tuple-element.619, bf16[1792,4,64]{0,2,1:T(8,128)(2,1)} %get-tuple-element.618, s32[]{:T(128)S(6)} %select_n.149), kind=kOutput, calls=%fused_computation.8.clone.1 | convolution fusion | flops 841347584 | bytes 28686340 | tf_op jit(solution)/shard_map/while/body/eval_jaxpr/qhd,khd->hqk/dot_general | solution.py:390
  204.4 12.2 %fusion.170 = f32[4,896]{1,0:T(4,128)S(1)} fusion(f32[4,896,1792]{2,1,0:T(8,128)} %get-tuple-element.574, f32[4,896]{1,0:T(4,128)S(1)} %get-tuple-element.575, pred[896,1792]{1,0:T(8,128)(4,1)S(1)} %broadcast_compare_fusion.4), kind=kLoop, calls=%fused_computation.9.clone.1 | loop fusion | flops 25686528 | bytes 27324416 | tf_op jit(solution)/shard_map/while/body/eval_jaxpr/reduce_sum | solution.py:400
  216.6 13.4 %fusion.171 = bf16[4,896,64]{1,2,0:T(8,128)(2,1)} fusion(bf16[1792,4,64]{0,2,1:T(8,128)(2,1)S(1)} %get-tuple-element.620, f32[4,896,1792]{2,1,0:T(8,128)} %get-tuple-element.574, f32[4,896]{1,0:T(4,128)S(1)} %fusion.170, f32[4,896]{1,0:T(4,128)S(1)} %get-tuple-element.575, pred[896,1792]{1,0:T(8,128)(4,1)S(1)} %broadcast_compare_fusion.4), kind=kOutput, calls=%fused_computation.10.clone.1 | convolution fusion | flops 854196224 | bytes 28700672 | tf_op jit(solution)/shard_map/while/body/eval_jaxpr/hqk,khd->qhd/dot_general | solution.py:402
  238.9 74.4 %all-reduce.7.cloned.1.call-done = bf16[1792,1024]{1,0:T(8,128)(2,1)} async-done(((bf16[1792,1024]{1,0:T(8,128)(2,1)}), bf16[1792,1024]{1,0:T(8,128)(2,1)}) %all-reduce.7.cloned.1.call-update) | async-done | bytes 3670032 | tf_op jit(solution)/shard_map/psum | solution.py:409
  327.0 24.2 %fusion.40 = (f32[1792,1024]{0,1:T(8,128)}, f32[1792,1024]{0,1:T(8,128)S(1)}) fusion(f32[1024]{0:T(1024)S(1)} %bitcast.367, bf16[1024,1024]{1,0:T(8,128)(2,1)} %bitcast.346, f32[1024]{0:T(1024)S(1)} %bitcast.378, f32[1024]{0:T(1024)S(1)} %bitcast.361, f32[1792]{0:T(1024)S(1)} %fusion.98, f32[1792]{0:T(1024)S(1)} %broadcast_multiply_fusion.1, ...), kind=kOutput, calls=%fused_computation.69 | convolution fusion | flops 3890216960 | bytes 24147968 | tf_op jit(solution)/shard_map/dot_general | solution.py:414
  351.2 14.8 %convert_reduce_fusion.4 = (f32[1024]{0:T(1024)}, bf16[1792,1024]{0,1:T(8,128)(2,1)}) fusion(f32[1792,1024]{0,1:T(8,128)} %get-tuple-element.453, bf16[1024,1024]{1,0:T(8,128)(2,1)S(1)} %bitcast.344, bf16[8,224,8,128]{3,2,1,0:T(8,128)(2,1)S(1)} %copy-done.16, f32[1792,1024]{0,1:T(8,128)S(1)} %get-tuple-element.454, f32[1024]{0:T(1024)S(1)} %bitcast.368), kind=kOutput, calls=%fused_computation.81 | convolution fusion | flops 3789290496 | bytes 24125440 | tf_op jit(solution)/shard_map/dot_general | solution.py:424
  377.9 12.6 %convolution_convert_fusion.2 = bf16[1792,1024]{1,0:T(8,128)(2,1)} fusion(bf16[1024,1024]{1,0:T(8,128)(2,1)S(1)} %bitcast.345, f32[1792,1024]{0,1:T(8,128)} %get-tuple-element.453, f32[1792,1024]{0,1:T(8,128)} %copy-done.19, f32[1024]{0:T(1024)S(1)} %bitcast.369), kind=kOutput, calls=%fused_computation.122 | convolution fusion | flops 3767271424 | bytes 20451328 | tf_op jit(solution)/shard_map/dot_general | solution.py:310
  390.6 60.3 %all-reduce.9.cloned.1.call-done = bf16[1792,1024]{1,0:T(8,128)(2,1)} async-done(((bf16[1792,1024]{1,0:T(8,128)(2,1)}), bf16[1792,1024]{1,0:T(8,128)(2,1)}) %all-reduce.9.cloned.1.call-update) | async-done | bytes 3670032 | tf_op jit(solution)/shard_map/psum | solution.py:429
  473.4 174.5 %while.28 = (s32[]{:T(128)}, f32[1792,4,64]{0,2,1:T(8,128)}, f32[1792,4,64]{0,2,1:T(8,128)}, bf16[2,896,4,64]{1,3,2,0:T(8,128)(2,1)}, s32[2]{0:T(128)S(1)}, /*in...) while((s32[]{:T(128)}, f32[1792,4,64]{0,2,1:T(8,128)}, ...), condition=%wide.region_16.18_spmd.clone, body=%wide.region_14.17_spmd.clone.sunk | while | flops 4172345856 | bytes 212492080 | solution.py:469
  477.9 13.2 %fusion.181 = f32[4,896,1792]{2,1,0:T(8,128)} fusion(bf16[1792,4,64]{0,2,1:T(8,128)(2,1)} %get-tuple-element.667, bf16[1792,4,64]{0,2,1:T(8,128)(2,1)S(1)} %get-tuple-element.666, s32[]{:T(128)S(6)} %select_n.150), kind=kOutput, calls=%fused_computation.34.clone.1 | convolution fusion | flops 822083584 | bytes 27066372 | tf_op jit(solution)/shard_map/while/body/eval_jaxpr/qhd,khd->hqk/dot_general | solution.py:452
  491.0 18.0 %multiply_reduce_fusion.3 = (f32[4,896]{1,0:T(4,128)S(1)}, f32[4,896,1792]{2,1,0:T(8,128)}) fusion(f32[4,896,1792]{2,1,0:T(8,128)} %fusion.181, f32[4,896]{1,0:T(4,128)S(1)} %dynamic-slice_bitcast_fusion.2, bf16[1792,4,64]{0,2,1:T(8,128)(2,1)S(1)} %get-tuple-element.664, bf16[1792,4,64]{0,2,1:T(8,128)(2,1)} %get-tuple-element.662, ...), kind=kOutput, calls=%fused_computation.20.clone.1 | convolution fusion | flops 854192640 | bytes 54390788 | tf_op jit(solution)/shard_map/while/body/eval_jaxpr/qhd,khd->hqk/dot_general | solution.py:390
  509.1 21.4 %multiply_convert_fusion.4 = bf16[4,896,1792]{2,1,0:T(8,128)(2,1)} fusion(f32[4,896,1792]{2,1,0:T(8,128)} %get-tuple-element.587, f32[4,896,1792]{2,1,0:T(8,128)} %fusion.181, f32[4,896]{1,0:T(4,128)S(1)} %get-tuple-element.588), kind=kLoop, calls=%fused_computation.19.clone.1 | loop fusion | flops 19267584 | bytes 64239616 | tf_op jit(solution)/shard_map/while/body/eval_jaxpr/convert_element_type | solution.py:456
  530.5 11.9 %fusion.183 = f32[1792,4,64]{0,2,1:T(8,128)} fusion(f32[4,896,1792]{2,1,0:T(8,128)} %get-tuple-element.587, f32[1792,4,64]{0,2,1:T(8,128)} %get-tuple-element.643, pred[]{:T(512)S(6)} %compare.24, bf16[1792,4,64]{0,2,1:T(8,128)(2,1)S(1)} %get-tuple-element.666, s32[]{:T(128)S(6)} %select_n.150), kind=kOutput, calls=%fused_computation.29.clone.1 | convolution fusion | flops 829423616 | bytes 29818884 | tf_op jit(solution)/shard_map/while/body/eval_jaxpr/hqk,qhd->khd/dot_general | solution.py:449
  542.4 9.3 fusion.184
  564.2 13.2 %fusion.181 = f32[4,896,1792]{2,1,0:T(8,128)} fusion(bf16[1792,4,64]{0,2,1:T(8,128)(2,1)} %get-tuple-element.667, bf16[1792,4,64]{0,2,1:T(8,128)(2,1)S(1)} %get-tuple-element.666, s32[]{:T(128)S(6)} %select_n.150), kind=kOutput, calls=%fused_computation.34.clone.1 | convolution fusion | flops 822083584 | bytes 27066372 | tf_op jit(solution)/shard_map/while/body/eval_jaxpr/qhd,khd->hqk/dot_general | solution.py:452
  577.4 18.0 %multiply_reduce_fusion.3 = (f32[4,896]{1,0:T(4,128)S(1)}, f32[4,896,1792]{2,1,0:T(8,128)}) fusion(f32[4,896,1792]{2,1,0:T(8,128)} %fusion.181, f32[4,896]{1,0:T(4,128)S(1)} %dynamic-slice_bitcast_fusion.2, bf16[1792,4,64]{0,2,1:T(8,128)(2,1)S(1)} %get-tuple-element.664, bf16[1792,4,64]{0,2,1:T(8,128)(2,1)} %get-tuple-element.662, ...), kind=kOutput, calls=%fused_computation.20.clone.1 | convolution fusion | flops 854192640 | bytes 54390788 | tf_op jit(solution)/shard_map/while/body/eval_jaxpr/qhd,khd->hqk/dot_general | solution.py:390
  595.5 21.4 %multiply_convert_fusion.4 = bf16[4,896,1792]{2,1,0:T(8,128)(2,1)} fusion(f32[4,896,1792]{2,1,0:T(8,128)} %get-tuple-element.587, f32[4,896,1792]{2,1,0:T(8,128)} %fusion.181, f32[4,896]{1,0:T(4,128)S(1)} %get-tuple-element.588), kind=kLoop, calls=%fused_computation.19.clone.1 | loop fusion | flops 19267584 | bytes 64239616 | tf_op jit(solution)/shard_map/while/body/eval_jaxpr/convert_element_type | solution.py:456
  616.9 12.5 %fusion.183 = f32[1792,4,64]{0,2,1:T(8,128)} fusion(f32[4,896,1792]{2,1,0:T(8,128)} %get-tuple-element.587, f32[1792,4,64]{0,2,1:T(8,128)} %get-tuple-element.643, pred[]{:T(512)S(6)} %compare.24, bf16[1792,4,64]{0,2,1:T(8,128)(2,1)S(1)} %get-tuple-element.666, s32[]{:T(128)S(6)} %select_n.150), kind=kOutput, calls=%fused_computation.29.clone.1 | convolution fusion | flops 829423616 | bytes 29818884 | tf_op jit(solution)/shard_map/while/body/eval_jaxpr/hqk,qhd->khd/dot_general | solution.py:449
  629.4 9.3 fusion.184
  638.7 8.8 fusion.182
  664.2 11.2 fusion.109
  702.5 93.6 %all-reduce.11.cloned.1.call-done = (bf16[1792,1024]{1,0:T(8,128)(2,1)}, bf16[1792,1024]{1,0:T(8,128)(2,1)}) async-done(((bf16[1792,1024]{1,0:T(8,128)(2,1)}, bf16[1792,1024]{1,0:T(8,128)(2,1)}), (bf16[1792,1024]{1,0:T(8,128)(2,1)}, bf16[1792,1024]{1,0:T(8,128)(2,1)})) %all-reduce.11.cloned.1.call-update) | async-done | bytes 7340048 | tf_op jit(solution)/shard_map/psum | solution.py:417
  808.8 18.3 %fusion.45 = bf16[1024,1792]{1,0:T(8,128)(2,1)S(1)} fusion(f32[1792,1024]{0,1:T(8,128)} %copy-done.19, f32[1024]{0:T(1024)S(1)} %bitcast.370), kind=kLoop, calls=%fused_computation.74 | loop fusion | flops 121110528 | bytes 11014144 | tf_op jit(solution)/shard_map/convert_element_type | solution.py:416
  839.0 10.0 fusion.69
  896.0 60.5 %reduce-scatter.8.cloned.1.call-done = f32[3,128,256]{2,1,0:T(8,128)} async-done(((f32[3,1024,256]{2,1,0:T(8,128)}), f32[3,128,256]{2,1,0:T(8,128)}) %reduce-scatter.8.cloned.1.call-update) | async-done | bytes 393232 | tf_op jit(solution)/shard_map/reduce_scatter | solution.py:498
  958.9 147.8 %reduce-scatter.12.cloned.1.call-done = f32[2,128,4,256]{3,1,2,0:T(8,128)} async-done(((f32[2,1024,4,256]{3,1,2,0:T(8,128)}), f32[2,128,4,256]{3,1,2,0:T(8,128)}) %reduce-scatter.12.cloned.1.call-update) | async-done | bytes 1048592 | tf_op jit(solution)/shard_map/reduce_scatter | solution.py:500
  (318 shorter events, 264.1 us)
Async XLA Ops:
  8.0 305.3 %all-reduce.7.cloned.1.call-start = ((), (), s32[]{:S(2)}) async-start(), calls=%async_computation.5 | async-start | bytes 7340032 | tf_op jit(solution)/shard_map/psum | solution.py:409
  8.7 74.0 %copy-start.61 = (pred[8]{0:T(512)(128)(4,1)}, pred[8]{0:T(512)(128)(4,1)S(1)}, u32[]{:S(2)}) copy-start(pred[8]{0:T(512)(128)(4,1)S(1)} %compare_and_fusion.1) | copy-start | bytes 28
  12.1 48.9 %copy-start.72 = (s32[8,1]{0,1:T(1,128)}, s32[8,1]{0,1:T(1,128)S(1)}, u32[]{:S(2)}) copy-start(s32[8,1]{0,1:T(1,128)S(1)} %reduce-window.8) | copy-start | bytes 100
  12.1 65.7 %copy-start.60 = (s32[1024]{0:T(1024)}, s32[1024]{0:T(1024)S(1)}, u32[]{:S(2)}) copy-start(s32[1024]{0:T(1024)S(1)} %pad_clamp_fusion.1) | copy-start | bytes 12292
  232.1 85.8 %copy-start.5 = (bf16[1792,4,64]{0,2,1:T(8,128)(2,1)}, bf16[1792,4,64]{0,2,1:T(8,128)(2,1)S(1)}, u32[]{:S(2)}) copy-start(bf16[1792,4,64]{0,2,1:T(8,128)(2,1)S(1)} %get-tuple-element.685) | copy-start | bytes 2752516
  232.1 85.8 %copy-start.13 = (bf16[1792,4,64]{0,2,1:T(8,128)(2,1)}, bf16[1792,4,64]{0,2,1:T(8,128)(2,1)S(1)}, u32[]{:S(2)}) copy-start(bf16[1792,4,64]{0,2,1:T(8,128)(2,1)S(1)} %get-tuple-element.692) | copy-start | bytes 2752516
  232.1 85.8 %copy-start.25 = (s32[1792]{0:T(1024)}, s32[1792]{0:T(1024)S(1)}, u32[]{:S(2)}) copy-start(s32[1792]{0:T(1024)S(1)} %get-tuple-element.707) | copy-start | bytes 21508
  232.1 85.8 %copy-start.40 = (f32[2,4,896]{2,1,0:T(4,128)}, f32[2,4,896]{2,1,0:T(4,128)S(1)}, u32[]{:S(2)}) copy-start(f32[2,4,896]{2,1,0:T(4,128)S(1)} %get-tuple-element.633) | copy-start | bytes 86020
  237.1 84.2 %all-gather.2.cloned.1.call-start = ((), (), s32[]{:S(2)}) async-start(), calls=%async_computation.6 | async-start | bytes 4718592 | tf_op jit(solution)/shard_map/all_gather | solution.py:354
  238.2 212.7 %all-reduce.9.cloned.1.call-start = ((), (), s32[]{:S(2)}) async-start(), calls=%async_computation.7 | async-start | bytes 7340032 | tf_op jit(solution)/shard_map/psum | solution.py:429
  238.3 139.6 %copy-start.50 = (f32[1,2,4,128]{3,1,2,0:T(2,128)}, f32[1,2,4,128]{3,1,2,0:T(2,128)S(1)}, u32[]{:S(2)}) copy-start(f32[1,2,4,128]{3,1,2,0:T(2,128)S(1)} %copy.203) | copy-start | bytes 12292
  238.9 88.0 %copy-start.68 = (f32[1,1024]{1,0:T(1,128)}, f32[1,1024]{1,0:T(1,128)S(1)}, u32[]{:S(2)}) copy-start(f32[1,1024]{1,0:T(1,128)S(1)} %get-tuple-element.444) | copy-start | bytes 12292
  238.9 225.5 %copy-start.38 = (f32[1,1024]{1,0:T(1,128)}, f32[1,1024]{1,0:T(1,128)S(1)}, u32[]{:S(2)}) copy-start(f32[1,1024]{1,0:T(1,128)S(1)} %get-tuple-element.446) | copy-start | bytes 12292
  238.9 225.5 %copy-start.47 = (f32[1,1024]{1,0:T(1,128)}, f32[1,1024]{1,0:T(1,128)S(1)}, u32[]{:S(2)}) copy-start(f32[1,1024]{1,0:T(1,128)S(1)} %get-tuple-element.445) | copy-start | bytes 12292
  318.6 145.8 %copy-start.36 = (f32[1792]{0:T(1024)}, f32[1792]{0:T(1024)S(1)}, u32[]{:S(2)}) copy-start(f32[1792]{0:T(1024)S(1)} %broadcast_multiply_fusion.1) | copy-start | bytes 21508
  321.3 143.1 %copy-start.44 = (f32[1792]{0:T(1024)}, f32[1792]{0:T(1024)S(1)}, u32[]{:S(2)}) copy-start(f32[1792]{0:T(1024)S(1)} %fusion.98) | copy-start | bytes 21508
  327.0 24.2 %copy-start.16 = (bf16[8,224,8,128]{3,2,1,0:T(8,128)(2,1)S(1)}, bf16[8,224,8,128]{3,2,1,0:T(8,128)(2,1)}, u32[]{:S(2)}) copy-start(bf16[8,224,8,128]{3,2,1,0:T(8,128)(2,1)} %get-tuple-element.451) | copy-start | bytes 11010052
  351.2 14.8 %copy-start.19 = (f32[1792,1024]{0,1:T(8,128)}, f32[1792,1024]{0,1:T(8,128)S(1)}, u32[]{:S(2)}) copy-start(f32[1792,1024]{0,1:T(8,128)S(1)} %get-tuple-element.454) | copy-start | bytes 22020100
  351.2 14.8 %copy-start.27 = (bf16[128,8,4,256]{3,1,2,0:T(8,128)(2,1)S(1)}, bf16[128,8,4,256]{3,1,2,0:T(8,128)(2,1)}, u32[]{:S(2)}) copy-start(bf16[128,8,4,256]{3,1,2,0:T(8,128)(2,1)} %copy.202) | copy-start | bytes 6291460
  373.6 422.5 %all-reduce.11.cloned.1.call-start = ((), (), s32[]{:S(2)}) async-start(), calls=%async_computation.13 | async-start | bytes 14680064 | tf_op jit(solution)/shard_map/psum | solution.py:417
  658.9 176.9 %reduce-scatter.16.cloned.1.call-start = ((), (), s32[]{:S(2)}) async-start(), calls=%async_computation.12 | async-start | bytes 147456
  675.4 13.0 %copy-start.20 = (bf16[2,896,256]{2,1,0:T(8,128)(2,1)S(1)}, bf16[2,896,256]{2,1,0:T(8,128)(2,1)}, u32[]{:S(2)}) copy-start(bf16[2,896,256]{2,1,0:T(8,128)(2,1)} %get-tuple-element.130) | copy-start | bytes 2752516
  693.7 102.3 %copy-start.46 = (f32[1,1024]{1,0:T(1,128)S(1)}, f32[1,1024]{1,0:T(1,128)}, u32[]{:S(2)}) copy-start(f32[1,1024]{1,0:T(1,128)} %get-tuple-element.442) | copy-start | bytes 12292
  693.8 143.5 %reduce-scatter.10.cloned.1.call-start = ((), (), s32[]{:S(2)}) async-start(), calls=%async_computation.9 | async-start | bytes 1179648 | tf_op jit(solution)/shard_map/reduce_scatter | solution.py:499
  698.2 196.6 %reduce-scatter.14.cloned.1.call-start = ((), (), s32[]{:S(2)}) async-start(), calls=%async_computation.11 | async-start | bytes 36864 | tf_op jit(solution)/shard_map/reduce_scatter | solution.py:502
  806.8 149.7 %reduce-scatter.8.cloned.1.call-start = ((), (), s32[]{:S(2)}) async-start(), calls=%async_computation.8 | async-start | bytes 3538944 | tf_op jit(solution)/shard_map/reduce_scatter | solution.py:498
  808.7 297.9 %reduce-scatter.12.cloned.1.call-start = ((), (), s32[]{:S(2)}) async-start(), calls=%async_computation.10 | async-start | bytes 9437184 | tf_op jit(solution)/shard_map/reduce_scatter | solution.py:500
  808.8 18.3 %copy-start.18 = (bf16[8,224,8,128]{3,2,1,0:T(8,128)(2,1)S(1)}, bf16[8,224,8,128]{3,2,1,0:T(8,128)(2,1)}, u32[]{:S(2)}) copy-start(bf16[8,224,8,128]{3,2,1,0:T(8,128)(2,1)} %get-tuple-element.451) | copy-start | bytes 11010052
  882.7 73.8 %copy-start.29 = (f32[3,128,256]{2,1,0:T(8,128)S(1)}, f32[3,128,256]{2,1,0:T(8,128)}, u32[]{:S(2)}) copy-start(f32[3,128,256]{2,1,0:T(8,128)} %att_ref.1) | copy-start | bytes 1179652
  882.7 224.0 %copy-start.23 = (f32[2,128,4,256]{3,2,1,0:T(4,128)S(1)}, f32[2,128,4,256]{3,2,1,0:T(4,128)}, u32[]{:S(2)}) copy-start(f32[2,128,4,256]{3,2,1,0:T(4,128)} %param.34) | copy-start | bytes 3145732
  882.7 224.0 %copy-start.30 = (f32[2,128,4,256]{3,2,1,0:T(4,128)S(1)}, f32[2,128,4,256]{3,2,1,0:T(4,128)}, u32[]{:S(2)}) copy-start(f32[2,128,4,256]{3,2,1,0:T(4,128)} %param.36) | copy-start | bytes 3145732
  882.7 224.0 %copy-start.31 = (f32[2,128,4,256]{3,2,1,0:T(4,128)S(1)}, f32[2,128,4,256]{3,2,1,0:T(4,128)}, u32[]{:S(2)}) copy-start(f32[2,128,4,256]{3,2,1,0:T(4,128)} %param.35) | copy-start | bytes 3145732
  (53 other events, 307.4 us)
Sparse Core Ops, SparseCore 0:
  237.3 76.0 all-reduce.6
  373.7 77.0 all-reduce.8
  659.0 136.9 all-reduce.10
Sparse Core Ops, SparseCore 1:
  240.4 72.0 all-gather.1
  693.8 61.6 reduce-scatter.15
  759.3 62.6 reduce-scatter.9
  826.0 52.6 reduce-scatter.13
  882.7 73.7 reduce-scatter.7
  960.6 146.1 reduce-scatter.11

commit v2 on v1

v2 whole, which is shorter than its diff:
```python
import functools

import jax
import jax.numpy as jnp
from jax import lax
from jax.experimental import pallas as pl
from jax.experimental.pallas import tpu as pltpu
from jax.sharding import PartitionSpec as P

HD = 64
STEP = 10
LANES = 128
BLOCK = 256
MESH = pl.DeviceIdType.MESH
BIG = 2.0**50

norm_epsilon = 1e-06
first_decay = 0.9
second_decay = 0.95
adam_epsilon = 1e-08
matrix_rate = 0.1
output_rate = 0.5
bias_rate = 0.5
vector_rate = 1.0
matrix_decay = 0.05

half_type = jnp.bfloat16
full_type = jnp.float32


def dot(left, right, left_dim=1, right_dim=0):
    return lax.dot_general(
        left, right, (((left_dim,), (right_dim,)), ((), ())), preferred_element_type=full_type
    )


def ring_pos(place, count):
    column = place % 2
    row = place // 2
    return row * (1 - column) + (count - 1 - row) * column


def ring_at(pos, count):
    near = (pos + 2 * count) % count
    down = near // (count // 2)
    return 2 * near * (1 - down) + (2 * count - 1 - 2 * near) * down


def normalized(x):
    center = jnp.mean(x, axis=-1, keepdims=True)
    offset = x - center
    spread = jnp.mean(offset * offset, axis=-1, keepdims=True)
    rate = lax.rsqrt(spread + norm_epsilon)
    return offset * rate, rate


class Gather:
    def __init__(self, view, width, sems, count):
        self.view, self.width, self.sems, self.count = view, width, sems, count
        self.steps = count // 2
        self.pos = ring_pos(lax.axis_index("dp"), count)
        self.tensor = lax.axis_index("tensor")

    def _copy(self, way, step, hops):
        sign = 1 - 2 * way
        part = (0, self.width)
        if step == self.steps - 1:
            part = (way * (self.width // 2), self.width // 2)
        block = self.view(ring_at(self.pos - sign * hops, self.count), *part)
        return pltpu.make_async_remote_copy(
            src_ref=block,
            dst_ref=block,
            send_sem=self.sems.at[2 * way, step],
            recv_sem=self.sems.at[2 * way + 1, step],
            device_id=(ring_at(self.pos + sign, self.count), self.tensor),
            device_id_type=MESH,
        )

    def advance(self, step):
        if step:
            for way in range(2):
                self._copy(way, step - 1, step).wait_recv()
        if step < self.steps:
            for way in range(2):
                self._copy(way, step, step).start()

    def sent(self):
        for step in range(self.steps):
            for way in range(2):
                self._copy(way, step, step).wait_send()


class RowSum:
    def __init__(self, term, given, sent, crossed, sems):
        self.term, self.given, self.sent_ref, self.crossed = term, given, sent, crossed
        self.sems = sems
        self.half = given.shape[1]
        self.dp, tensor = lax.axis_index("dp"), lax.axis_index("tensor")
        self.core = tensor % 2
        self.mate = tensor - tensor % 2 + (tensor + 1) % 2
        self.other = (tensor + 2) % 4

    def rows(self, core):
        return pl.ds(pl.multiple_of(core * self.half, self.half), self.half)

    def _give(self, i):
        return pltpu.make_async_remote_copy(
            src_ref=self.term.at[i, self.rows(1 - self.core), :],
            dst_ref=self.given.at[i],
            send_sem=self.sems.at[0, i],
            recv_sem=self.sems.at[1, i],
            device_id=(self.dp, self.mate),
            device_id_type=MESH,
        )

    def _cross(self, i):
        return pltpu.make_async_remote_copy(
            src_ref=self.sent_ref.at[i],
            dst_ref=self.crossed.at[i],
            send_sem=self.sems.at[2, i],
            recv_sem=self.sems.at[3, i],
            device_id=(self.dp, self.other),
            device_id_type=MESH,
        )

    def give(self, i):
        self._give(i).start()

    def cross(self, i):
        self._give(i).wait_recv()
        mine = self.term[i, self.rows(self.core), :].astype(full_type)
        self.sent_ref[i] = (mine + self.given[i].astype(full_type)).astype(half_type)
        self._cross(i).start()

    def total(self, i):
        self._cross(i).wait_recv()
        return self.sent_ref[i].astype(full_type) + self.crossed[i].astype(full_type)

    def finish(self, blocks):
        def done(i, carry):
            self._give(i).wait_send()
            self._cross(i).wait_send()
            return carry

        lax.fori_loop(0, blocks, done, 0)


class Share:
    def __init__(self, ref, sems):
        self.ref, self.sems = ref, sems
        self.dp, tensor = lax.axis_index("dp"), lax.axis_index("tensor")
        self.core = tensor % 2
        self.mate = tensor - tensor % 2 + (tensor + 1) % 2

    def rows(self, i, core):
        half = BLOCK // 2
        return pl.ds(pl.multiple_of(i * BLOCK + core * half, half), half)

    def _copy(self, i, core):
        piece = self.ref.at[self.rows(i, core), :]
        return pltpu.make_async_remote_copy(
            src_ref=piece,
            dst_ref=piece,
            send_sem=self.sems.at[0, i],
            recv_sem=self.sems.at[1, i],
            device_id=(self.dp, self.mate),
            device_id_type=MESH,
        )

    def put(self, i, value):
        self.ref[self.rows(i, self.core), :] = value
        self._copy(i, self.core).start()

    def arrived(self, i):
        self._copy(i, 1 - self.core).wait_recv()

    def finish(self, blocks):
        def done(i, carry):
            self._copy(i, self.core).wait_send()
            return carry

        lax.fori_loop(0, blocks, done, 0)


def greet(peers):
    barrier = pltpu.get_barrier_semaphore()
    for peer in peers:
        pl.semaphore_signal(barrier, inc=1, device_id=peer, device_id_type=MESH)
    return lambda: pl.semaphore_wait(barrier, len(peers))


def tensor_peers():
    dp, tensor = lax.axis_index("dp"), lax.axis_index("tensor")
    return [(dp, tensor - tensor % 2 + (tensor + 1) % 2), (dp, (tensor + 2) % 4)]


def ring_peers(count):
    dp, tensor = lax.axis_index("dp"), lax.axis_index("tensor")
    pos = ring_pos(dp, count)
    return [(ring_at(pos + 1, count), tensor), (ring_at(pos - 1, count), tensor)]


def dp_peers(count):
    dp, tensor = lax.axis_index("dp"), lax.axis_index("tensor")
    return [((dp + k) % count, tensor) for k in range(1, count)]


def three_parts(x):
    high = x.astype(half_type).astype(full_type)
    middle = (x - high).astype(half_type).astype(full_type)
    return high, middle, x - high - middle


def front_kernel(
    count, ends_ref, tok_ref, att_ref, out_ref, dense_ref, small_ref,
    a1_ref, qb_ref, ka_ref, va_ref, o_ref, a2_ref, h2_ref, w_ref, wo_ref, wd_ref, vec_ref, bias_ref,
    qa_ref, smalls, term, given, sent, crossed,
    gather_sems, small_sems, sum_sems, share_sems,
):
    me, tensor = lax.axis_index("dp"), lax.axis_index("tensor")
    total_rows, width = tok_ref.shape
    local_width = wo_ref.shape[1]
    ratio = dense_ref.shape[2]
    wide = width // count
    slots = ends_ref.shape[0]
    heads = local_width // HD
    blocks = total_rows // BLOCK
    half = BLOCK // 2
    greeted = greet(tensor_peers() + dp_peers(count))
    mine = pl.ds(pl.multiple_of(me * wide, wide), wide)
    smalls[me] = small_ref[...]
    for row in range(3):
        w_ref[mine, row * local_width : (row + 1) * local_width] = att_ref[row].astype(half_type)
    wo_ref[mine, :] = out_ref[...].astype(half_type)
    greeted()

    def place(block):
        return pl.ds(pl.multiple_of(block * wide, wide), wide)

    def small_copy(source, peer):
        return pltpu.make_async_remote_copy(
            src_ref=small_ref,
            dst_ref=smalls.at[source],
            send_sem=small_sems.at[0, peer],
            recv_sem=small_sems.at[1, source],
            device_id=(peer, tensor),
            device_id_type=MESH,
        )

    def send_small(k, carry):
        small_copy(me, (me + k) % count).start()
        return carry

    lax.fori_loop(1, count, send_small, 0)

    def attend_view(row):
        return lambda block, low, size: w_ref.at[
            place(block), pl.ds(row * local_width + low, size)
        ]

    def dense_view(row):
        return lambda block, low, size: wd_ref.at[row, place(block), pl.ds(low, size)]

    attend = [Gather(attend_view(row), local_width, gather_sems.at[row], count) for row in range(3)]
    attend.append(
        Gather(
            lambda block, low, size: wo_ref.at[place(block), pl.ds(low, size)],
            local_width, gather_sems.at[3], count,
        )
    )
    dense = [
        Gather(dense_view(row), ratio * local_width, gather_sems.at[4 + row], count)
        for row in range(2)
    ]
    for piece in attend:
        piece.advance(0)
    for row in range(2):
        for r in range(ratio):
            wd_ref[row, mine, r * local_width : (r + 1) * local_width] = dense_ref[
                row, :, r, :
            ].astype(half_type)

    def take_small(k, carry):
        source = (me + k) % count
        small_copy(source, source).wait_recv()
        return carry

    lax.fori_loop(1, count, take_small, 0)
    lanes = small_ref.shape[1] - local_width
    fold = lanes // wide
    bias = smalls[0, :, lanes:]
    for j in range(1, count):
        bias = bias + smalls[j, :, lanes:]
    bias_ref[...] = bias
    for window in range(width // lanes):
        piece = smalls[window * fold, :, :lanes]
        for j in range(window * fold + 1, (window + 1) * fold):
            piece = piece + smalls[j, :, :lanes]
        vec_ref[:, window * lanes : (window + 1) * lanes] = piece

    def norm_rows(i, carry):
        rows = pl.ds(pl.multiple_of(i * BLOCK, BLOCK), BLOCK)
        unit, _ = normalized(tok_ref[rows, :].astype(full_type))
        a1_ref[rows, :] = (unit * vec_ref[2:3, :] + vec_ref[3:4, :]).astype(half_type)
        return carry

    steps = count // 2
    done = 0
    for step in range(1, steps + 1):
        upto = min(blocks, -(-blocks * step // (steps - 1)))
        if upto > done:
            lax.fori_loop(done, upto, norm_rows, 0)
        done = max(done, upto)
        for piece in attend[: 3 if step == steps else 4]:
            piece.advance(step)
        if step == steps - 1:
            for piece in dense:
                piece.advance(0)

    lane = lax.broadcasted_iota(jnp.int32, (BLOCK, LANES), 1)
    low_half = lane < HD
    spot = lane % HD

    def project(i, carry):
        row = pl.multiple_of(i * BLOCK, BLOCK)
        rows = pl.ds(row, BLOCK)
        a1 = a1_ref[rows, :]
        qkv = dot(a1, w_ref[...])
        q, k, v = (qkv[:, part * local_width : (part + 1) * local_width] for part in range(3))
        q = (q + bias_ref[0:1, :]).astype(half_type).astype(full_type) * HD**-0.5
        index = row + lax.broadcasted_iota(jnp.int32, (BLOCK, LANES), 0)
        segment = jnp.zeros((BLOCK, LANES), jnp.int32)
        for slot in range(slots):
            segment = segment + jnp.where(index >= ends_ref[slot], 1, 0)
        same = spot == segment
        inside = spot <= slots
        q_mark = jnp.where(inside & ~same, -BIG, 0.0)
        k_mark = jnp.where(same, BIG, jnp.where((spot > slots) & (spot <= slots + 3), 1.0, 0.0))
        for head in range(heads):
            pair = slice(head // 2 * LANES, head // 2 * LANES + LANES)
            own = low_half if head % 2 == 0 else ~low_half
            qa_ref[head, rows, :] = jnp.where(own, q[:, pair], q_mark).astype(half_type)
            ka_ref[head, rows, :] = jnp.where(own, k[:, pair], k_mark).astype(half_type)
            va_ref[head, rows, :] = jnp.where(own, v[:, pair], 1.0).astype(half_type)
        return carry

    lax.fori_loop(0, blocks, project, 0)
    attend[3].advance(steps)

    rowsum = RowSum(term, given, sent, crossed, sum_sems)
    share = Share(a2_ref, share_sems)

    def attend_block(i):
        rows = pl.ds(pl.multiple_of(i * BLOCK, BLOCK), BLOCK)
        for head in range(heads):
            query = qa_ref[head, rows, :]
            scores = dot(query, ka_ref[head], 1, 1)
            top = jnp.max(scores, axis=1, keepdims=True)
            weights = jnp.exp(scores - top).astype(half_type)
            mixed = dot(weights, va_ref[head])
            turned = pltpu.roll(mixed, HD, 1)
            own = low_half if head % 2 == 0 else ~low_half
            log_total = three_parts(top + jnp.log(jnp.where(own, turned, mixed)))
            marked = query.astype(full_type)
            for part in range(3):
                marked = jnp.where(~own & (spot == slots + 1 + part), -log_total[part], marked)
            qb_ref[head, rows, :] = marked.astype(half_type)
            out = mixed / turned
            if head % 2 == 0:
                before = out
            else:
                pair = slice(head // 2 * LANES, head // 2 * LANES + LANES)
                o_ref[rows, pair] = jnp.where(low_half, before, out).astype(half_type)
        term[i] = dot(o_ref[rows, :], wo_ref[...], 1, 1).astype(half_type)

    def norm_block(i):
        x = tok_ref[share.rows(i, share.core), :].astype(full_type)
        hidden = x + rowsum.total(i) + vec_ref[0:1, :]
        h2_ref[pl.ds(pl.multiple_of(i * half, half), half), :] = hidden
        unit, _ = normalized(hidden)
        share.put(i, (unit * vec_ref[4:5, :] + vec_ref[5:6, :]).astype(half_type))

    def attend_step(i, carry):
        attend_block(i)
        rowsum.give(i)
        for step in range(1, steps):

            @pl.when(i == (step - 1) * blocks // steps)
            def _(step=step):
                for piece in dense:
                    piece.advance(step)

        @pl.when(i >= 1)
        def _():
            rowsum.cross(i - 1)

        @pl.when(i >= 2)
        def _():
            norm_block(i - 2)

        return carry

    lax.fori_loop(0, blocks, attend_step, 0)
    rowsum.cross(blocks - 1)
    norm_block(blocks - 2)
    norm_block(blocks - 1)
    for piece in dense:
        piece.advance(steps)

    def arrived(i, carry):
        share.arrived(i)
        return carry

    lax.fori_loop(0, blocks, arrived, 0)
    for piece in attend + dense:
        piece.sent()
    rowsum.finish(blocks)
    share.finish(blocks)

    def sent_small(k, carry):
        small_copy(me, (me + k) % count).wait_send()
        return carry

    lax.fori_loop(1, count, sent_small, 0)


def gelu_parts(z):
    phi = 0.5 + 0.5 * lax.erf(z * (0.5**0.5))
    slope = phi + z * (jnp.exp(-0.5 * z * z) * (2.0 * 3.141592653589793) ** -0.5)
    return z * phi, slope


def mlp_kernel(
    a2_ref, cot_ref, h2_ref, w_ref, vec_ref, bias_ref,
    down_ref, ga_ref, gh2_ref, grad_ref, gbias_ref, gvec_ref,
    term, given, sent, crossed, up_sum, down_sum,
    sum_sems, share_sems,
):
    total_rows, width = a2_ref.shape
    blocks = total_rows // BLOCK
    half = BLOCK // 2
    greeted = greet(tensor_peers())
    gbias_ref[...] = jnp.zeros_like(gbias_ref)
    gvec_ref[...] = jnp.zeros_like(gvec_ref)
    greeted()
    rowsum = RowSum(term, given, sent, crossed, sum_sems)
    share = Share(ga_ref, share_sems)

    def mlp_block(i):
        rows = pl.ds(pl.multiple_of(i * BLOCK, BLOCK), BLOCK)
        a2 = a2_ref[rows, :]
        gy = cot_ref[rows, :]
        u, slope = gelu_parts(dot(a2, w_ref[0]) + bias_ref[0:1, :])
        ul = u.astype(half_type)
        gz = (dot(gy, w_ref[1]) * slope).astype(half_type)
        term[i] = dot(gz, w_ref[0], 1, 1).astype(half_type)
        rowsum.give(i)
        gbias_ref[0:1, :] += jnp.sum(gz.astype(full_type), axis=0, keepdims=True)
        down_ref[rows, :] = dot(ul, w_ref[1], 1, 1).astype(half_type)
        up = dot(a2, gz, 0, 0)
        down = dot(gy, ul, 0, 0)

        @pl.when(i == 0)
        def _():
            up_sum[...] = up
            down_sum[...] = down

        @pl.when(i > 0)
        def _():
            up_sum[...] += up
            down_sum[...] += down

    def back_block(i):
        own = pl.ds(pl.multiple_of(i * half, half), half)
        gn = rowsum.total(i)
        unit, rate = normalized(h2_ref[own, :])
        e = gn * vec_ref[4:5, :]
        inner = e - jnp.mean(e, axis=-1, keepdims=True)
        inner = inner - unit * jnp.mean(e * unit, axis=-1, keepdims=True)
        gy = cot_ref[share.rows(i, share.core), :].astype(full_type)
        gh = gy + rate * inner
        gh2_ref[own, :] = gh
        share.put(i, gh.astype(half_type))
        gvec_ref[0:1, :] += jnp.sum(gh, axis=0, keepdims=True)
        gvec_ref[1:2, :] += jnp.sum(gy, axis=0, keepdims=True)
        gvec_ref[4:5, :] += jnp.sum(gn * unit, axis=0, keepdims=True)
        gvec_ref[5:6, :] += jnp.sum(gn, axis=0, keepdims=True)

    def step(i, carry):
        mlp_block(i)

        @pl.when(i >= 1)
        def _():
            rowsum.cross(i - 1)

        @pl.when(i >= 2)
        def _():
            back_block(i - 2)

        return carry

    lax.fori_loop(0, blocks, step, 0)
    rowsum.cross(blocks - 1)
    grad_ref[0] = up_sum[...].astype(half_type)
    grad_ref[1] = down_sum[...].astype(half_type)
    back_block(blocks - 2)
    back_block(blocks - 1)

    def arrived(i, carry):
        share.arrived(i)
        return carry

    lax.fori_loop(0, blocks, arrived, 0)
    rowsum.finish(blocks)
    share.finish(blocks)


class Scatter:
    def __init__(self, view, stage, taken, sems, count):
        self.view, self.stage, self.taken = view, stage, taken
        self.sems, self.count = sems, count
        self.pos = ring_pos(lax.axis_index("dp"), count)
        self.tensor = lax.axis_index("tensor")

    def _copy(self, way, step):
        sign = 1 - 2 * way
        return pltpu.make_async_remote_copy(
            src_ref=self.stage.at[way, step],
            dst_ref=self.taken.at[way, step],
            send_sem=self.sems.at[2 * way, step],
            recv_sem=self.sems.at[2 * way + 1, step],
            device_id=(ring_at(self.pos + sign, self.count), self.tensor),
            device_id_type=MESH,
        )

    def begin(self):
        for way in range(2):
            block = ring_at(self.pos - (1 - 2 * way), self.count)
            self.stage[way, 0] = self.view(way, block).astype(half_type)
            self._copy(way, 0).start()

    def advance(self, step):
        for way in range(2):
            block = ring_at(self.pos - (1 - 2 * way) * (1 + step), self.count)
            self._copy(way, step - 1).wait_recv()
            own = self.view(way, block).astype(full_type)
            total = self.taken[way, step - 1].astype(full_type) + own
            self.stage[way, step] = total.astype(half_type)
            self._copy(way, step).start()

    def total(self, way):
        last = self.count - 2
        self._copy(way, last).wait_recv()
        own = self.view(way, lax.axis_index("dp")).astype(full_type)
        return self.taken[way, last].astype(full_type) + own

    def finish(self):
        def done(step, carry):
            for way in range(2):
                self._copy(way, step).wait_send()
            return carry

        lax.fori_loop(0, self.count - 1, done, 0)


def attention_back_kernel(
    count, ga_ref, o_ref, qb_ref, ka_ref, va_ref, wo_ref, grad_ref, down_ref, h2_ref, vec_ref,
    gqkv_ref, sum_ref, out_ref,
    goa_ref, kt_ref, gqt_ref, given, sent, crossed, stage, taken,
    sum_sems, share_sems, scatter_sems,
):
    total_rows, width = ga_ref.shape
    local_width = wo_ref.shape[1]
    heads = local_width // HD
    blocks = total_rows // BLOCK
    half = BLOCK // 2
    wide = width // count
    greeted = greet(tensor_peers() + ring_peers(count))
    greeted()

    def view(way, block):
        return grad_ref[way, pl.ds(pl.multiple_of(block * wide, wide), wide), :]

    scatter = Scatter(view, stage, taken, scatter_sems, count)
    scatter.begin()
    rowsum = RowSum(down_ref, given, sent, crossed, sum_sems)
    share = Share(out_ref, share_sems)
    rowsum.give(0)
    lane = lax.broadcasted_iota(jnp.int32, (BLOCK, LANES), 1)
    low_half = lane < HD
    spot = lane % HD

    def prepare(i, carry):
        rows = pl.ds(pl.multiple_of(i * BLOCK, BLOCK), BLOCK)
        go = dot(ga_ref[rows, :], wo_ref[...]).astype(half_type).astype(full_type)
        both = go * o_ref[rows, :].astype(full_type)
        for head in range(heads):
            pair = slice(head // 2 * LANES, head // 2 * LANES + LANES)
            own = low_half if head % 2 == 0 else ~low_half
            inner = jnp.sum(jnp.where(own, both[:, pair], 0.0), axis=1, keepdims=True)
            high, middle, low = three_parts(inner)
            filled = jnp.where(own, go[:, pair], 0.0)
            for part, value in enumerate((high, middle, low)):
                filled = jnp.where(~own & (spot == part), -value, filled)
            goa_ref[head, rows, :] = filled.astype(half_type)
            if head % 2 == 0:
                before = ka_ref[head, rows, :].astype(full_type)
            else:
                k = jnp.where(low_half, before, ka_ref[head, rows, :].astype(full_type))
                kt_ref[pair, rows] = k.T.astype(half_type)
        return carry

    lax.fori_loop(0, blocks, prepare, 0)
    rowsum.give(1)

    def keys_block(j):
        rows = pl.ds(pl.multiple_of(j * BLOCK, BLOCK), BLOCK)
        for head in range(heads):
            scores = dot(ka_ref[head, rows, :], qb_ref[head], 1, 1)
            probs = jnp.exp(scores)
            gp = dot(va_ref[head, rows, :], goa_ref[head], 1, 1)
            gs = (probs * gp).astype(half_type)
            gv = dot(probs.astype(half_type), goa_ref[head])
            gk = dot(gs, qb_ref[head])
            own = slice(head * HD, head * HD + HD)
            gqt = dot(kt_ref[own, rows], gs)

            @pl.when(j == 0)
            def _():
                gqt_ref[own, :] = gqt

            @pl.when(j > 0)
            def _():
                gqt_ref[own, :] += gqt

            if head % 2 == 0:
                gk_even, gv_even = gk, gv
            else:
                pair = slice(head // 2 * LANES, head // 2 * LANES + LANES)
                for part, value in ((1, (gk_even, gk)), (2, (gv_even, gv))):
                    base = part * local_width + head // 2 * LANES
                    gqkv_ref[rows, base : base + LANES] = jnp.where(low_half, *value).astype(
                        half_type
                    )

    def output_block(i):
        own = pl.ds(pl.multiple_of(i * half, half), half)
        total = h2_ref[own, :] + rowsum.total(i) + vec_ref[1:2, :]
        share.put(i, total.astype(half_type))

    def step(j, carry):
        keys_block(j)

        hops = count - 1
        per = -(-hops // blocks)
        for t in range(per):
            hop = j * per + t

            @pl.when((hop >= 1) & (hop < hops))
            def _(hop=hop):
                scatter.advance(hop)

        @pl.when(j < blocks - 2)
        def _():
            rowsum.give(j + 2)

        rowsum.cross(j)

        @pl.when(j >= 1)
        def _():
            output_block(j - 1)

        return carry

    lax.fori_loop(0, blocks, step, 0)
    output_block(blocks - 1)

    def turn(i, carry):
        rows = pl.ds(pl.multiple_of(i * BLOCK, BLOCK), BLOCK)
        gqkv_ref[rows, :local_width] = (gqt_ref[:, rows].T * HD**-0.5).astype(half_type)
        return carry

    lax.fori_loop(0, blocks, turn, 0)
    for way in range(2):
        sum_ref[way] = scatter.total(way)

    def arrived(i, carry):
        share.arrived(i)
        return carry

    lax.fori_loop(0, blocks, arrived, 0)
    scatter.finish()
    rowsum.finish(blocks)
    share.finish(blocks)


def end_kernel(
    count, gqkv_ref, w_ref, a1_ref, ga_ref, o_ref, gh2_ref, tok_ref, vec_ref, gbias_ref, gvec_ref,
    tg_ref, sum_ref, small_ref,
    term, given, sent, crossed, grads, stage, taken, small_mine, small_taken, small_mate,
    sum_sems, share_sems, scatter_sems, small_sems, mate_sems,
):
    total_rows, width = a1_ref.shape
    local_width = w_ref.shape[1] // 3
    blocks = total_rows // BLOCK
    half = BLOCK // 2
    wide = width // count
    lanes = small_ref.shape[1] - local_width
    fold = lanes // wide
    me, tensor = lax.axis_index("dp"), lax.axis_index("tensor")
    mate = tensor - tensor % 2 + (tensor + 1) % 2
    greeted = greet(tensor_peers() + dp_peers(count))
    small_mine[:, :width] = gvec_ref[...]
    ones = jnp.ones((8, total_rows), half_type)
    bias_query = dot(ones, gqkv_ref[:, :local_width])
    small_mine[0:1, width:] = bias_query[0:1, :]
    ratio = gbias_ref.shape[1] // local_width
    for r in range(ratio):
        small_mine[1 + r : 2 + r, width:] = gbias_ref[0:1, r * local_width : (r + 1) * local_width]
    small_mine[1 + ratio :, width:] = jnp.zeros((7 - ratio, local_width), full_type)
    greeted()

    def small_copy(part, source, peer):
        window = pl.ds(pl.multiple_of(peer // fold * lanes, lanes), lanes)
        return pltpu.make_async_remote_copy(
            src_ref=small_mine.at[:, pl.ds(width, local_width) if part else window],
            dst_ref=small_taken.at[source, :, pl.ds(lanes, local_width) if part else pl.ds(0, lanes)],
            send_sem=small_sems.at[2 * part, peer],
            recv_sem=small_sems.at[2 * part + 1, source],
            device_id=(peer, tensor),
            device_id_type=MESH,
        )

    def send_small(part):
        def send(k, carry):
            small_copy(part, me, (me + k) % count).start()
            return carry

        lax.fori_loop(1, count, send, 0)

    send_small(1)
    rowsum = RowSum(term, given, sent, crossed, sum_sems)
    share = Share(tg_ref, share_sems)

    def view(way, block):
        rows = pl.ds(pl.multiple_of(block * wide, wide), wide)
        return jnp.stack([grads[2 * way, rows, :], grads[2 * way + 1, rows, :]])

    scatter = Scatter(view, stage, taken, scatter_sems, count)

    def norm_term(i):
        rows = pl.ds(pl.multiple_of(i * BLOCK, BLOCK), BLOCK)
        term[i] = dot(gqkv_ref[rows, :], w_ref[...], 1, 1).astype(half_type)
        rowsum.give(i)

    def norm_block(i):
        own = pl.ds(pl.multiple_of(i * half, half), half)
        gn = rowsum.total(i)
        unit, rate = normalized(tok_ref[share.rows(i, share.core), :].astype(full_type))
        e = gn * vec_ref[2:3, :]
        inner = e - jnp.mean(e, axis=-1, keepdims=True)
        inner = inner - unit * jnp.mean(e * unit, axis=-1, keepdims=True)
        share.put(i, (gh2_ref[own, :] + rate * inner).astype(half_type))
        small_mine[2:3, :width] += jnp.sum(gn * unit, axis=0, keepdims=True)
        small_mine[3:4, :width] += jnp.sum(gn, axis=0, keepdims=True)

    def weight_grads(c, carry):
        columns = pl.ds(pl.multiple_of(c * BLOCK, BLOCK), BLOCK)
        three = dot(a1_ref[:, columns], gqkv_ref[...], 0, 0)
        for row in range(3):
            grads[row, columns, :] = three[:, row * local_width : (row + 1) * local_width]
        grads[3, columns, :] = dot(ga_ref[:, columns], o_ref[...], 0, 0)
        return carry

    norm_term(0)
    norm_term(1)
    lax.fori_loop(0, 1, weight_grads, 0)
    rowsum.cross(0)
    lax.fori_loop(1, width // BLOCK, weight_grads, 0)
    scatter.begin()
    hops = count - 1
    per = -(-hops // blocks)

    def step(i, carry):
        @pl.when(i < blocks - 2)
        def _():
            norm_term(i + 2)

        @pl.when(i < blocks - 1)
        def _():
            rowsum.cross(i + 1)

        norm_block(i)
        for t in range(per):
            hop = i * per + t

            @pl.when((hop >= 1) & (hop < hops))
            def _(hop=hop):
                scatter.advance(hop)

        return carry

    lax.fori_loop(0, blocks, step, 0)
    send_small(0)
    for way in range(2):
        total = scatter.total(way)
        sum_ref[2 * way] = total[0]
        sum_ref[2 * way + 1] = total[1]
    for part in range(2):
        window = pl.ds(pl.multiple_of(me // fold * lanes, lanes), lanes)
        here = slice(lanes, lanes + local_width) if part else slice(0, lanes)
        small_taken[me, :, here] = small_mine[:, width:] if part else small_mine[:, window]

        def take(k, carry, part=part):
            source = (me + k) % count
            small_copy(part, source, source).wait_recv()
            return carry

        lax.fori_loop(1, count, take, 0)
    total = small_taken[0]
    for j in range(1, count):
        total = total + small_taken[j]
    small_ref[...] = total
    pair = pltpu.make_async_remote_copy(
        src_ref=small_ref.at[:, pl.ds(0, lanes)],
        dst_ref=small_mate,
        send_sem=mate_sems.at[0],
        recv_sem=mate_sems.at[1],
        device_id=(me, mate),
        device_id_type=MESH,
    )
    pair.start()
    pair.wait()
    small_ref[:, :lanes] = total[:, :lanes] + small_mate[...]

    def arrived(i, carry):
        share.arrived(i)
        return carry

    lax.fori_loop(0, blocks, arrived, 0)
    scatter.finish()
    rowsum.finish(blocks)
    share.finish(blocks)
    for part in range(2):

        def done(k, carry, part=part):
            small_copy(part, me, (me + k) % count).wait_send()
            return carry

        lax.fori_loop(1, count, done, 0)


def permute_kernel(back, owner_ref, *refs):
    for x_ref, y_ref in zip(refs[: len(refs) // 2], refs[len(refs) // 2 :]):
        count = owner_ref.shape[0]
        wide = x_ref.shape[1] // count
        for j in range(count):
            natural = pl.ds(pl.multiple_of(owner_ref[j] * wide, wide), wide)
            stored = slice(j * wide, (j + 1) * wide)
            if back:
                y_ref[:, natural] = x_ref[:, stored]
            else:
                y_ref[:, stored] = x_ref[:, natural]


def permuted(arrays, owner, back):
    rows, width = arrays[0].shape
    count = owner.shape[0]
    wide = width // count
    if wide % LANES:
        order = jnp.argsort(owner) if back else owner
        shape = (rows, count, wide)
        return [jnp.take(x.reshape(shape), order, axis=1).reshape(rows, width) for x in arrays]
    spec = pl.BlockSpec((BLOCK, width), lambda i, *_: (i, 0))
    return pl.pallas_call(
        functools.partial(permute_kernel, back),
        out_shape=[jax.ShapeDtypeStruct(x.shape, x.dtype) for x in arrays],
        grid_spec=pltpu.PrefetchScalarGridSpec(
            num_scalar_prefetch=1,
            grid=(rows // BLOCK,),
            in_specs=[spec] * len(arrays),
            out_specs=[spec] * len(arrays),
        ),
        compiler_params=pltpu.CompilerParams(vmem_limit_bytes=32 * 2**20),
    )(owner, *arrays)


def adamw_step(weight, first, second, grad, rate, decay):
    first_next = first_decay * first + (1.0 - first_decay) * grad
    second_next = second_decay * second + (1.0 - second_decay) * grad * grad
    first_hat = first_next / (1.0 - first_decay**STEP)
    second_hat = second_next / (1.0 - second_decay**STEP)
    update = first_hat / (jnp.sqrt(second_hat) + adam_epsilon) + decay * weight
    return (first_next, second_next, weight - rate * update)


def pack_small(vector_master, bias_master, owner, count):
    me = lax.axis_index("dp")
    wide = vector_master.shape[1]
    lanes = max(LANES, wide)
    fold = lanes // wide
    lane = jnp.arange(lanes)
    vectors = jnp.where(lane // wide == me % fold, jnp.tile(vector_master, (1, fold)), 0.0)
    narrow = bias_master.shape[1]
    spot = jnp.arange(narrow * count)
    biases = jnp.where(spot // narrow == owner[me], jnp.tile(bias_master, (1, count)), 0.0)
    small = jnp.concatenate(
        [jnp.pad(vectors, ((0, 2), (0, 0))), jnp.pad(biases, ((0, 3), (0, 0)))], axis=1
    )
    return small.astype(half_type).astype(full_type)


def call(kernel, collective, outs, scratch, operands, scalars=0, limit=58):
    vmem = pl.BlockSpec(memory_space=pltpu.VMEM)
    smem = pl.BlockSpec(memory_space=pltpu.SMEM)
    return pl.pallas_call(
        kernel,
        out_shape=[jax.ShapeDtypeStruct(shape, dtype) for shape, dtype in outs],
        in_specs=[smem] * scalars + [vmem] * (len(operands) - scalars),
        out_specs=[vmem] * len(outs),
        scratch_shapes=scratch,
        compiler_params=pltpu.CompilerParams(
            collective_id=collective, has_side_effects=True, vmem_limit_bytes=limit * 2**20
        ),
    )(*operands)


def dma(*shape):
    return pltpu.SemaphoreType.DMA(shape)


def local(
    tokens,
    lengths,
    owner,
    attend_master,
    attend_first,
    attend_second,
    output_master,
    output_first,
    output_second,
    dense_master,
    dense_first,
    dense_second,
    bias_master,
    bias_first,
    bias_second,
    vector_master,
    vector_first,
    vector_second,
    cotangent,
):
    count = owner.shape[0]
    rows, width = tokens.shape
    local_width = output_master.shape[1]
    ratio = dense_master.shape[2]
    hidden = ratio * local_width
    heads = local_width // HD
    blocks = rows // BLOCK
    half = BLOCK // 2
    wide = width // count
    lanes = max(LANES, wide)
    me = lax.axis_index("dp")

    tok, cot = permuted([tokens, cotangent], owner, False)
    small = pack_small(vector_master, bias_master, owner, count)
    ends = jnp.cumsum(lengths[0])
    row_sum = [pltpu.VMEM((blocks, half, width), half_type)] * 3
    heads_shape = (heads, rows, LANES)
    a1, qb, ka, va, o, a2, h2, w, wo, wd, vec, bias = call(
        functools.partial(front_kernel, count),
        0,
        [
            ((rows, width), half_type),
            (heads_shape, half_type),
            (heads_shape, half_type),
            (heads_shape, half_type),
            ((rows, local_width), half_type),
            ((rows, width), half_type),
            ((rows // 2, width), full_type),
            ((width, 3 * local_width), half_type),
            ((width, local_width), half_type),
            ((2, width, hidden), half_type),
            ((8, width), full_type),
            ((8, local_width), full_type),
        ],
        [
            pltpu.VMEM(heads_shape, half_type),
            pltpu.VMEM((count,) + small.shape, full_type),
            pltpu.VMEM((blocks, BLOCK, width), half_type),
            *row_sum,
            dma(6, 4, count // 2),
            dma(2, count),
            dma(4, blocks),
            dma(2, blocks),
        ],
        (ends, tok, attend_master, output_master, dense_master, small),
        scalars=1,
    )
    bias_up = bias[1 : 1 + ratio].reshape(1, hidden)
    down, ga, gh2, grad, gbias, gvec = call(
        mlp_kernel,
        1,
        [
            ((rows, width), half_type),
            ((rows, width), half_type),
            ((rows // 2, width), full_type),
            ((2, width, hidden), half_type),
            ((8, hidden), full_type),
            ((8, width), full_type),
        ],
        [
            pltpu.VMEM((blocks, BLOCK, width), half_type),
            *row_sum,
            pltpu.VMEM((width, hidden), full_type),
            pltpu.VMEM((width, hidden), full_type),
            dma(4, blocks),
            dma(2, blocks),
        ],
        (a2, cot, h2, wd, vec, bias_up),
    )
    gqkv, dense_sum, layer_output = call(
        functools.partial(attention_back_kernel, count),
        2,
        [
            ((rows, 3 * local_width), half_type),
            ((2, wide, hidden), full_type),
            ((rows, width), half_type),
        ],
        [
            pltpu.VMEM(heads_shape, half_type),
            pltpu.VMEM((local_width, rows), half_type),
            pltpu.VMEM((local_width, rows), full_type),
            *row_sum,
            pltpu.VMEM((2, count - 1, wide, hidden), half_type),
            pltpu.VMEM((2, count - 1, wide, hidden), half_type),
            dma(4, blocks),
            dma(2, blocks),
            dma(4, count - 1),
        ],
        (ga, o, qb, ka, va, wo, grad, down.reshape(blocks, BLOCK, width), h2, vec),
    )
    tokens_grad, weight_sum, small_sum = call(
        functools.partial(end_kernel, count),
        3,
        [
            ((rows, width), half_type),
            ((4, wide, local_width), full_type),
            ((8, lanes + local_width), full_type),
        ],
        [
            pltpu.VMEM((blocks, BLOCK, width), half_type),
            *row_sum,
            pltpu.VMEM((4, width, local_width), full_type),
            pltpu.VMEM((2, count - 1, 2, wide, local_width), half_type),
            pltpu.VMEM((2, count - 1, 2, wide, local_width), half_type),
            pltpu.VMEM((8, width + local_width), full_type),
            pltpu.VMEM((count, 8, lanes + local_width), full_type),
            pltpu.VMEM((8, lanes), full_type),
            dma(4, blocks),
            dma(2, blocks),
            dma(4, count - 1),
            dma(4, count),
            dma(2),
        ],
        (gqkv, w, a1, ga, o, gh2, tok, vec, gbias, gvec),
    )
    layer_output, tokens_grad = permuted([layer_output, tokens_grad], owner, True)
    dense_sum = dense_sum.reshape(dense_master.shape)
    vector_sum = lax.dynamic_slice_in_dim(
        small_sum[:6, :lanes], me % (lanes // wide) * wide, wide, axis=1
    )
    narrow = bias_master.shape[1]
    bias_sum = lax.dynamic_slice_in_dim(
        small_sum[: 1 + ratio, lanes:], owner[me] * narrow, narrow, axis=1
    )
    attend_new = adamw_step(
        attend_master, attend_first, attend_second, weight_sum[:3], matrix_rate, matrix_decay
    )
    output_new = adamw_step(
        output_master, output_first, output_second, weight_sum[3], output_rate, matrix_decay
    )
    dense_new = adamw_step(
        dense_master, dense_first, dense_second, dense_sum, matrix_rate, matrix_decay
    )
    bias_new = adamw_step(bias_master, bias_first, bias_second, bias_sum, bias_rate, 0.0)
    vector_new = adamw_step(
        vector_master, vector_first, vector_second, vector_sum, vector_rate, 0.0
    )
    return (
        layer_output,
        tokens_grad,
        *attend_new,
        *output_new,
        *dense_new,
        *bias_new,
        *vector_new,
    )


def solution(mesh):
    return jax.shard_map(
        local,
        mesh=mesh,
        in_specs=(
            P("dp", None),
            P("dp", None),
            P(),
            P(None, "dp", "tensor"),
            P(None, "dp", "tensor"),
            P(None, "dp", "tensor"),
            P("dp", "tensor"),
            P("dp", "tensor"),
            P("dp", "tensor"),
            P(None, "dp", None, "tensor"),
            P(None, "dp", None, "tensor"),
            P(None, "dp", None, "tensor"),
            P(None, ("tensor", "dp")),
            P(None, ("tensor", "dp")),
            P(None, ("tensor", "dp")),
            P(None, "dp"),
            P(None, "dp"),
            P(None, "dp"),
            P("dp", None),
        ),
        out_specs=(
            P("dp", None),
            P("dp", None),
            P(None, "dp", "tensor"),
            P(None, "dp", "tensor"),
            P(None, "dp", "tensor"),
            P("dp", "tensor"),
            P("dp", "tensor"),
            P("dp", "tensor"),
            P(None, "dp", None, "tensor"),
            P(None, "dp", None, "tensor"),
            P(None, "dp", None, "tensor"),
            P(None, ("tensor", "dp")),
            P(None, ("tensor", "dp")),
            P(None, ("tensor", "dp")),
            P(None, "dp"),
            P(None, "dp"),
            P(None, "dp"),
        ),
        check_vma=False,
    )
```

time: 1130 us -> 340 us (0.30)
  waiting for transfers between devices: 437 us -> 0 us
  matrix products: 278 us -> 0 us
  Pallas kernels: 37.4 us -> 311 us
  other arithmetic: 182 us -> 11 us
  local copies, waits for them, and re-layouts: 127 us -> 15.5 us
  blocking collectives: 35.2 us -> 0 us
  between operations: 16.5 us -> 1.58 us
    dot_general x29 -> x0, matrix products: 278 us -> none  [the longest x4 60.4 us: block_scores(): jnp.einsum('qhd,khd->hqk', query_block, key_heads, preferred_element_type...]
    pallas_call x1 -> x6, Pallas kernels: 37.4 us -> 311 us  [the longest x4 303 us: call(): pl.pallas_call(kernel, out_shape=[jax.ShapeDtypeStruct(shape, dtype) for...]
    psum x3 -> x0, waiting for transfers between devices: 228 us -> none  [the longest x1 93.6 us: local(): lax.psum(contract_cols(act_hidden, w_down).astype(jnp.bfloat16), 'tensor')]
    reduce_scatter x4 -> x0, waiting for transfers between devices: 208 us -> none  [the longest x1 148 us: local(): lax.psum_scatter(dense_grad, 'dp', scatter_dimension=1, tiled=True)]
    reduce_sum x14 -> x0, other arithmetic: 68.8 us -> none  [the longest x2 24.5 us: forward_block(): row_totals = jnp.sum(weights, axis=-1, keepdims=True)]
    convert_element_type x7 -> x0, other arithmetic: 66.3 us -> none  [the longest x2 42.9 us: backward_block(): grad_scores = (probs * (grad_probs - row_dot)).astype(half_type)]
    all_gather x1 -> x0, blocking collectives: 35.2 us -> none  [local(): lax.all_gather(output_master.astype(half_type), 'dp', axis=0, tiled=True)]
    unnamed x162 -> x50, local copies, waits for them, and re-layouts: 40.5 us -> 11.8 us
  transfers between devices with their start and end apart: 9 -> 0, of which waited for: 5 -> 0; matrix products, arithmetic and copies ran while one was open for 15% -> 0% of each run, Pallas kernels for 0% -> 0%
where the time goes in v2:
time: 340 us; the launch traced here: 339 us
  Pallas kernels  311 us (91%)
  local copies, waits for them, and re-layouts  15.5 us (5%)
  other arithmetic  11 us (3%)
    pallas_call x4, Pallas kernels, call(): pl.pallas_call(kernel, out_shape=[jax.ShapeDtypeStruct(shape, dtype) for...  303 us
    unnamed x50, local copies, waits for them, and re-layouts  11.8 us
    pallas_call x2, Pallas kernels, permuted(): pl.pallas_call(functools.partial(permute_kernel, back), out_shape=[jax.Sh...  7.81 us
    sub x5, other arithmetic, adamw_step(): return (first_next, second_next, weight - rate * update)  7.72 us

profile of v2, /device:TPU:0, one launch (start us, length us, event | category | flops | bytes accessed | tf_op | source)
XLA Modules:
  0.0 339.0 jit_solution(13413441396713491819)
XLA Ops:
  0.7 1.2 dynamic_slice.8
  2.6 0.7 fusion.10
  3.2 1.3 reduce-window.9
  4.6 0.7 select_convert_fusion.1
  5.2 0.7 tile.4
  5.9 0.1 tile.10
  6.0 0.6 fusion.7.small_ref
  6.6 2.0 copy-done.1
  8.7 2.0 copy-done.2
  10.7 0.7 copy-done.6
  11.4 2.5 shard_map.314
  13.9 1.8 copy-done
  15.8 1.8 copy-done.3
  17.6 105.6 %shard_map.315 = (bf16[1792,1024]{1,0:T(8,128)(2,1)}, bf16[4,1792,128]{2,1,0:T(8,128)(2,1)}, bf16[4,1792,128]{2,1,0:T(8,128)(2,1)}, bf16[4,1792,128]{2,1,0:T(8,1...) custom-call(s32[8]{0:T(128)} %bitcast.17, ...), custom_call_target="tpu_custom_call" | custom-call | tf_op jit(solution)/shard_map/pallas_call | solution.py:916
  123.2 0.7 slice_bitcast_fusion
  123.9 0.6 copy.36
  124.5 65.8 %shard_map.316 = (bf16[1792,1024]{1,0:T(8,128)(2,1)}, bf16[1792,1024]{1,0:T(8,128)(2,1)}, f32[896,1024]{1,0:T(8,128)}, bf16[2,1024,1024]{2,1,0:T(8,128)(2,1)}, f32[8,1024]{1,0:T(8,128)}, /*index=5*/f32[8,1024]{1,0:T(8,128)}) custom-call(bf16[1792,1024]{1,0:T(8,128)(2,1)} %get-tuple-element.46.a2_ref, bf16[1792,1024]{1,0:T(8,128)(2,1)} %copy-done.3, ...), custom_call_target="tpu_custom_call" | custom-call | tf_op jit(solution)/shard_map/pallas_call | solution.py:916
  190.3 68.1 %shard_map.317 = (bf16[1792,768]{1,0:T(8,128)(2,1)}, f32[2,128,1024]{2,1,0:T(8,128)}, bf16[1792,1024]{1,0:T(8,128)(2,1)}) custom-call(bf16[1792,1024]{1,0:T(8,128)(2,1)} %get-tuple-element.52.ga_ref, bf16[1792,256]{1,0:T(8,128)(2,1)} %get-tuple-element.53.o_ref, bf16[4,1792,128]{2,1,0:T(8,128)(2,1)} %get-tuple-element.54.qb_ref, ...), custom_call_target="tpu_custom_call" | custom-call | tf_op jit(solution)/shard_map/pallas_call | solution.py:916
  258.4 0.0 copy-start.7
  258.4 63.7 %shard_map.318 = (bf16[1792,1024]{1,0:T(8,128)(2,1)}, f32[4,128,256]{2,1,0:T(8,128)}, f32[8,384]{1,0:T(8,128)}) custom-call(bf16[1792,768]{1,0:T(8,128)(2,1)} %get-tuple-element.61.gqkv_ref, bf16[1024,768]{1,0:T(8,128)(2,1)} %get-tuple-element.62.w_ref, bf16[1792,1024]{1,0:T(8,128)(2,1)} %get-tuple-element.63.a1_ref, ...), custom_call_target="tpu_custom_call" | custom-call | tf_op jit(solution)/shard_map/pallas_call | solution.py:916
  322.1 2.0 copy-done.5
  324.1 0.0 copy-start.22
  324.2 0.0 copy-start.23
  324.2 0.0 copy-start.16
  324.2 0.0 copy-start.9
  324.3 5.3 %shard_map.319 = (bf16[1792,1024]{1,0:T(8,128)(2,1)}, bf16[1792,1024]{1,0:T(8,128)(2,1)}) custom-call(s32[8]{0:T(128)S(1)} %copy-done.7, bf16[1792,1024]{1,0:T(8,128)(2,1)S(1)} %copy-done.4, bf16[1792,1024]{1,0:T(8,128)(2,1)S(1)} %copy-done.5), custom_call_target="tpu_custom_call" | custom-call | tf_op jit(solution)/shard_map/pallas_call | solution.py:875
  329.6 0.6 add_subtract_fusion
  330.2 0.7 multiply_subtract_fusion.3
  330.9 0.8 multiply_subtract_fusion.2
  331.7 1.2 multiply_subtract_fusion.1
  332.9 1.7 reshape.78
  334.6 4.4 %multiply_subtract_fusion = (f32[2,128,4,256]{3,2,1,0:T(4,128)}, f32[2,128,4,256]{3,2,1,0:T(4,128)}, f32[2,128,4,256]{3,2,1,0:T(4,128)}) fusion(f32[2,128,4,256]{3,2,1,0:T(4,128)S(1)} %copy-done.8, f32[2,128,4,256]{3,2,1,0:T(4,128)S(1)} %reshape.78, f32[2,128,4,256]{3,2,1,0:T(4,128)S(1)} %copy-done.10, f32[2,128,4,256]{3,2,1,0:T(4,128)} %param.29), kind=kLoop, calls=%fused_computation.2 | loop fusion | flops 3932160 | bytes 7340032 | tf_op jit(solution)/shard_map/sub | solution.py:894
  (40 shorter events, 0.1 us)
Async XLA Ops:
  6.6 2.0 copy-start.1
  8.7 2.0 copy-start.2
  10.7 0.7 copy-start.6
  13.9 1.8 copy-start
  15.8 1.8 copy-start.3
  258.4 63.7 %copy-start.4 = (bf16[1792,1024]{1,0:T(8,128)(2,1)S(1)}, bf16[1792,1024]{1,0:T(8,128)(2,1)}, u32[]{:S(2)}) copy-start(bf16[1792,1024]{1,0:T(8,128)(2,1)} %get-tuple-element.60.refs_0_) | copy-start | bytes 11010052
  258.4 63.7 %copy-start.7 = (s32[8]{0:T(128)S(1)}, s32[8]{0:T(128)}, u32[]{:S(2)}) copy-start(s32[8]{0:T(128)} %owner_ref.3) | copy-start | bytes 100
  322.1 2.0 copy-start.5
  324.1 5.4 %copy-start.19 = (f32[8,384]{1,0:T(8,128)S(1)}, f32[8,384]{1,0:T(8,128)}, u32[]{:S(2)}) copy-start(f32[8,384]{1,0:T(8,128)} %get-tuple-element.72) | copy-start | bytes 36868
  324.1 5.4 %copy-start.18 = (f32[6,128]{1,0:T(8,128)S(1)}, f32[6,128]{1,0:T(8,128)}, u32[]{:S(2)}) copy-start(f32[6,128]{1,0:T(8,128)} %param.34) | copy-start | bytes 9220
  324.1 5.4 %copy-start.20 = (f32[6,128]{1,0:T(8,128)S(1)}, f32[6,128]{1,0:T(8,128)}, u32[]{:S(2)}) copy-start(f32[6,128]{1,0:T(8,128)} %param.36) | copy-start | bytes 9220
  324.1 5.4 %copy-start.21 = (f32[6,128]{1,0:T(8,128)S(1)}, f32[6,128]{1,0:T(8,128)}, u32[]{:S(2)}) copy-start(f32[6,128]{1,0:T(8,128)} %param.35) | copy-start | bytes 9220
  324.1 6.0 %copy-start.17 = (f32[5,32]{1,0:T(8,128)S(1)}, f32[5,32]{1,0:T(8,128)}, u32[]{:S(2)}) copy-start(f32[5,32]{1,0:T(8,128)} %param.31) | copy-start | bytes 1924
  324.1 6.0 %copy-start.22 = (f32[5,32]{1,0:T(8,128)S(1)}, f32[5,32]{1,0:T(8,128)}, u32[]{:S(2)}) copy-start(f32[5,32]{1,0:T(8,128)} %param.33) | copy-start | bytes 1924
  324.2 6.0 %copy-start.23 = (f32[5,32]{1,0:T(8,128)S(1)}, f32[5,32]{1,0:T(8,128)}, u32[]{:S(2)}) copy-start(f32[5,32]{1,0:T(8,128)} %param.32) | copy-start | bytes 1924
  324.2 6.7 %copy-start.11 = (f32[128,256]{1,0:T(8,128)S(1)}, f32[128,256]{1,0:T(8,128)}, u32[]{:S(2)}) copy-start(f32[128,256]{1,0:T(8,128)} %out_ref.1) | copy-start | bytes 393220
  324.2 6.7 %copy-start.12 = (f32[4,128,256]{2,1,0:T(8,128)S(1)}, f32[4,128,256]{2,1,0:T(8,128)}, u32[]{:S(2)}) copy-start(f32[4,128,256]{2,1,0:T(8,128)} %get-tuple-element.70) | copy-start | bytes 1572868
  324.2 6.7 %copy-start.15 = (f32[128,256]{1,0:T(8,128)S(1)}, f32[128,256]{1,0:T(8,128)}, u32[]{:S(2)}) copy-start(f32[128,256]{1,0:T(8,128)} %param.27) | copy-start | bytes 393220
  324.2 6.7 %copy-start.16 = (f32[128,256]{1,0:T(8,128)S(1)}, f32[128,256]{1,0:T(8,128)}, u32[]{:S(2)}) copy-start(f32[128,256]{1,0:T(8,128)} %param.26) | copy-start | bytes 393220
  324.2 7.5 %copy-start.9 = (f32[3,128,256]{2,1,0:T(8,128)S(1)}, f32[3,128,256]{2,1,0:T(8,128)}, u32[]{:S(2)}) copy-start(f32[3,128,256]{2,1,0:T(8,128)} %att_ref.1) | copy-start | bytes 1179652
  324.2 7.5 %copy-start.13 = (f32[3,128,256]{2,1,0:T(8,128)S(1)}, f32[3,128,256]{2,1,0:T(8,128)}, u32[]{:S(2)}) copy-start(f32[3,128,256]{2,1,0:T(8,128)} %param.24) | copy-start | bytes 1179652
  324.2 7.5 %copy-start.14 = (f32[3,128,256]{2,1,0:T(8,128)S(1)}, f32[3,128,256]{2,1,0:T(8,128)}, u32[]{:S(2)}) copy-start(f32[3,128,256]{2,1,0:T(8,128)} %param.23) | copy-start | bytes 1179652
  329.5 5.1 %copy-start.8 = (f32[2,128,4,256]{3,2,1,0:T(4,128)S(1)}, f32[2,128,4,256]{3,2,1,0:T(4,128)}, u32[]{:S(2)}) copy-start(f32[2,128,4,256]{3,2,1,0:T(4,128)} %dense_ref.1) | copy-start | bytes 3145732
  329.5 5.1 %copy-start.10 = (f32[2,128,4,256]{3,2,1,0:T(4,128)S(1)}, f32[2,128,4,256]{3,2,1,0:T(4,128)}, u32[]{:S(2)}) copy-start(f32[2,128,4,256]{3,2,1,0:T(4,128)} %param.30) | copy-start | bytes 3145732

commit v3 on v2

--- a/solution.py
+++ b/solution.py
@@ -93,6 +93,7 @@
 class RowSum:
     def __init__(self, term, given, sent, crossed, sems):
         self.term, self.given, self.sent_ref, self.crossed = term, given, sent, crossed
+        self.slots, self.blocks = term.shape[0], given.shape[0]
         self.sems = sems
         self.half = given.shape[1]
         self.dp, tensor = lax.axis_index("dp"), lax.axis_index("tensor")
@@ -105,7 +106,7 @@
 
     def _give(self, i):
         return pltpu.make_async_remote_copy(
-            src_ref=self.term.at[i, self.rows(1 - self.core), :],
+            src_ref=self.term.at[i % self.slots, self.rows(1 - self.core), :],
             dst_ref=self.given.at[i],
             send_sem=self.sems.at[0, i],
             recv_sem=self.sems.at[1, i],
@@ -123,12 +124,19 @@
             device_id_type=MESH,
         )
 
+    def free(self, i):
+        if self.slots < self.blocks:
+
+            @pl.when(i >= self.slots)
+            def _():
+                self._give(i - self.slots).wait_send()
+
     def give(self, i):
         self._give(i).start()
 
     def cross(self, i):
         self._give(i).wait_recv()
-        mine = self.term[i, self.rows(self.core), :].astype(full_type)
+        mine = self.term[i % self.slots, self.rows(self.core), :].astype(full_type)
         self.sent_ref[i] = (mine + self.given[i].astype(full_type)).astype(half_type)
         self._cross(i).start()
 
@@ -136,13 +144,17 @@
         self._cross(i).wait_recv()
         return self.sent_ref[i].astype(full_type) + self.crossed[i].astype(full_type)
 
-    def finish(self, blocks):
-        def done(i, carry):
+    def finish(self):
+        def given(i, carry):
             self._give(i).wait_send()
+            return carry
+
+        def crossed(i, carry):
             self._cross(i).wait_send()
             return carry
 
-        lax.fori_loop(0, blocks, done, 0)
+        lax.fori_loop(max(self.blocks - self.slots, 0), self.blocks, given, 0)
+        lax.fori_loop(0, self.blocks, crossed, 0)
 
 
 class Share:
@@ -211,27 +223,86 @@
     return high, middle, x - high - middle
 
 
+def gelu_parts(z):
+    phi = 0.5 + 0.5 * lax.erf(z * (0.5**0.5))
+    slope = phi + z * (jnp.exp(-0.5 * z * z) * (2.0 * 3.141592653589793) ** -0.5)
+    return z * phi, slope
+
+
+def fetch(source, target, sems):
+    def copy(i):
+        rows = pl.ds(pl.multiple_of(i * BLOCK, BLOCK), BLOCK)
+        return pltpu.make_async_copy(source.at[rows, :], target.at[rows, :], sems.at[i])
+
+    return copy
+
+
+def stored_order(x, owner_ref):
+    count = owner_ref.shape[0]
+    wide = x.shape[1] // count
+    if wide % LANES:
+        return x
+    parts = []
+    for j in range(count):
+        total = None
+        for n in range(count):
+            term = x[:, n * wide : (n + 1) * wide] * jnp.where(owner_ref[j] == n, 1.0, 0.0)
+            total = term if total is None else total + term
+        parts.append(total)
+    return jnp.concatenate(parts, axis=1)
+
+
 def front_kernel(
-    count, ends_ref, tok_ref, att_ref, out_ref, dense_ref, small_ref,
-    a1_ref, qb_ref, ka_ref, va_ref, o_ref, a2_ref, h2_ref, w_ref, wo_ref, wd_ref, vec_ref, bias_ref,
-    qa_ref, smalls, term, given, sent, crossed,
-    gather_sems, small_sems, sum_sems, share_sems,
+    count, len_ref, owner_ref, tok_hbm, cot_hbm, att_ref, out_ref, dense_ref, vector_ref, split_ref,
+    a1_hbm, ga_hbm, h2_hbm, own_hbm, qa_hbm, ka_hbm, va_hbm, o_hbm, w_hbm, wo_hbm, gh2_hbm, down_hbm,
+    up_hbm, dn_hbm, vec_ref, gbias_ref, gvec_ref,
+    own_ref, qa_ref, ka_ref, va_ref, o_ref, w_ref, wo_ref, gh2_ref, down_ref, up_ref, dn_ref,
+    norm_ref, cot_ref, wd_ref, ga_ref, bias_ref, b1_ref, small_ref, smalls,
+    term, given, sent, crossed, term2, given2, sent2, crossed2,
+    gather_sems, small_sems, sum_sems, sum2_sems, share_sems, put_sems, local_sems, whole_sems,
 ):
     me, tensor = lax.axis_index("dp"), lax.axis_index("tensor")
-    total_rows, width = tok_ref.shape
+    total_rows, width = norm_ref.shape
     local_width = wo_ref.shape[1]
     ratio = dense_ref.shape[2]
     wide = width // count
-    slots = ends_ref.shape[0]
+    slots = len_ref.shape[1]
     heads = local_width // HD
     blocks = total_rows // BLOCK
     half = BLOCK // 2
+    lanes = small_ref.shape[1] - local_width
+    fold = lanes // wide
+    steps = count // 2
+    core = tensor % 2
+
     greeted = greet(tensor_peers() + dp_peers(count))
+    tokens_in = fetch(tok_hbm, norm_ref, local_sems.at[0])
+    cot_in = fetch(cot_hbm, cot_ref, local_sems.at[1])
+    a1_out = fetch(norm_ref, a1_hbm, local_sems.at[2])
+    for i in range(blocks):
+        tokens_in(i).start()
+    for i in range(blocks):
+        cot_in(i).start()
     mine = pl.ds(pl.multiple_of(me * wide, wide), wide)
-    smalls[me] = small_ref[...]
     for row in range(3):
         w_ref[mine, row * local_width : (row + 1) * local_width] = att_ref[row].astype(half_type)
     wo_ref[mine, :] = out_ref[...].astype(half_type)
+
+    small_ref[...] = jnp.zeros_like(small_ref)
+    vectors = vector_ref[...].astype(half_type)
+    if fold == 1:
+        small_ref[0:6, :lanes] = vectors.astype(full_type)
+    else:
+        row = lax.broadcasted_iota(jnp.int32, (wide, lanes), 0)
+        column = lax.broadcasted_iota(jnp.int32, (wide, lanes), 1)
+        spread = jnp.where(column == row + me % fold * wide, 1.0, 0.0).astype(half_type)
+        small_ref[0:6, :lanes] = dot(vectors, spread)
+    narrow = split_ref.shape[1]
+    row = lax.broadcasted_iota(jnp.int32, (narrow, local_width), 0)
+    column = lax.broadcasted_iota(jnp.int32, (narrow, local_width), 1)
+    spread = jnp.where(column == row + owner_ref[me] * narrow, 1.0, 0.0).astype(half_type)
+    small_ref[0 : 1 + ratio, lanes:] = dot(split_ref[...].astype(half_type), spread)
+    smalls[me] = small_ref[...]
     greeted()
 
     def place(block):
@@ -286,12 +357,12 @@
         return carry
 
     lax.fori_loop(1, count, take_small, 0)
-    lanes = small_ref.shape[1] - local_width
-    fold = lanes // wide
     bias = smalls[0, :, lanes:]
     for j in range(1, count):
         bias = bias + smalls[j, :, lanes:]
     bias_ref[...] = bias
+    for r in range(ratio):
+        b1_ref[:, r * local_width : (r + 1) * local_width] = bias[1 + r : 2 + r, :]
     for window in range(width // lanes):
         piece = smalls[window * fold, :, :lanes]
         for j in range(window * fold + 1, (window + 1) * fold):
@@ -299,12 +370,21 @@
         vec_ref[:, window * lanes : (window + 1) * lanes] = piece
 
     def norm_rows(i, carry):
+        tokens_in(i).wait()
         rows = pl.ds(pl.multiple_of(i * BLOCK, BLOCK), BLOCK)
-        unit, _ = normalized(tok_ref[rows, :].astype(full_type))
-        a1_ref[rows, :] = (unit * vec_ref[2:3, :] + vec_ref[3:4, :]).astype(half_type)
-        return carry
-
-    steps = count // 2
+        x = stored_order(norm_ref[rows, :].astype(full_type), owner_ref)
+        norm_ref[rows, :] = x.astype(half_type)
+        here = pl.ds(pl.multiple_of(i * BLOCK + core * half, half), half)
+        own_ref[pl.ds(pl.multiple_of(i * half, half), half), :] = norm_ref[here, :]
+        unit, _ = normalized(x)
+        norm_ref[rows, :] = (unit * vec_ref[2:3, :] + vec_ref[3:4, :]).astype(half_type)
+        a1_out(i).start()
+        cot_in(i).wait()
+        cot_ref[rows, :] = stored_order(cot_ref[rows, :].astype(full_type), owner_ref).astype(
+            half_type
+        )
+        return carry
+
     done = 0
     for step in range(1, steps + 1):
         upto = min(blocks, -(-blocks * step // (steps - 1)))
@@ -317,6 +397,13 @@
             for piece in dense:
                 piece.advance(0)
 
+    pumps = [(piece, step) for step in range(1, steps + 1) for piece in dense]
+
+    def pump(slot):
+        first, last = (len(pumps) * s // (blocks + 1) for s in (slot, slot + 1))
+        for piece, step in pumps[first:last]:
+            piece.advance(step)
+
     lane = lax.broadcasted_iota(jnp.int32, (BLOCK, LANES), 1)
     low_half = lane < HD
     spot = lane % HD
@@ -324,14 +411,16 @@
     def project(i, carry):
         row = pl.multiple_of(i * BLOCK, BLOCK)
         rows = pl.ds(row, BLOCK)
-        a1 = a1_ref[rows, :]
+        a1 = norm_ref[rows, :]
         qkv = dot(a1, w_ref[...])
         q, k, v = (qkv[:, part * local_width : (part + 1) * local_width] for part in range(3))
         q = (q + bias_ref[0:1, :]).astype(half_type).astype(full_type) * HD**-0.5
         index = row + lax.broadcasted_iota(jnp.int32, (BLOCK, LANES), 0)
         segment = jnp.zeros((BLOCK, LANES), jnp.int32)
+        end = 0
         for slot in range(slots):
-            segment = segment + jnp.where(index >= ends_ref[slot], 1, 0)
+            end = end + len_ref[0, slot]
+            segment = segment + jnp.where(index >= end, 1, 0)
         same = spot == segment
         inside = spot <= slots
         q_mark = jnp.where(inside & ~same, -BIG, 0.0)
@@ -346,9 +435,22 @@
 
     lax.fori_loop(0, blocks, project, 0)
     attend[3].advance(steps)
+    pump(0)
+
+    def a1_left(i, carry):
+        a1_out(i).wait()
+        return carry
+
+    lax.fori_loop(0, blocks, a1_left, 0)
+    gbias_ref[...] = jnp.zeros_like(gbias_ref)
+    gvec_ref[...] = jnp.zeros_like(gvec_ref)
 
     rowsum = RowSum(term, given, sent, crossed, sum_sems)
-    share = Share(a2_ref, share_sems)
+    share = Share(norm_ref, share_sems)
+
+    def h2_out(i):
+        own = pl.ds(pl.multiple_of(i * half, half), half)
+        return pltpu.make_async_copy(gh2_ref.at[own, :], h2_hbm.at[own, :], local_sems.at[3, i])
 
     def attend_block(i):
         rows = pl.ds(pl.multiple_of(i * BLOCK, BLOCK), BLOCK)
@@ -364,134 +466,146 @@
             marked = query.astype(full_type)
             for part in range(3):
                 marked = jnp.where(~own & (spot == slots + 1 + part), -log_total[part], marked)
-            qb_ref[head, rows, :] = marked.astype(half_type)
+            qa_ref[head, rows, :] = marked.astype(half_type)
             out = mixed / turned
             if head % 2 == 0:
                 before = out
             else:
                 pair = slice(head // 2 * LANES, head // 2 * LANES + LANES)
                 o_ref[rows, pair] = jnp.where(low_half, before, out).astype(half_type)
-        term[i] = dot(o_ref[rows, :], wo_ref[...], 1, 1).astype(half_type)
+            if head == 1:
+
+                @pl.when(i >= 1)
+                def _():
+                    rowsum.cross(i - 1)
+
+        rowsum.free(i)
+        term[i % term.shape[0]] = dot(o_ref[rows, :], wo_ref[...], 1, 1).astype(half_type)
+        rowsum.give(i)
 
     def norm_block(i):
-        x = tok_ref[share.rows(i, share.core), :].astype(full_type)
-        hidden = x + rowsum.total(i) + vec_ref[0:1, :]
-        h2_ref[pl.ds(pl.multiple_of(i * half, half), half), :] = hidden
+        own = pl.ds(pl.multiple_of(i * half, half), half)
+        hidden = own_ref[own, :].astype(full_type) + rowsum.total(i) + vec_ref[0:1, :]
+        gh2_ref[own, :] = hidden
+        h2_out(i).start()
         unit, _ = normalized(hidden)
         share.put(i, (unit * vec_ref[4:5, :] + vec_ref[5:6, :]).astype(half_type))
 
+    behind = min(3, blocks)
+
     def attend_step(i, carry):
         attend_block(i)
-        rowsum.give(i)
-        for step in range(1, steps):
-
-            @pl.when(i == (step - 1) * blocks // steps)
-            def _(step=step):
-                for piece in dense:
-                    piece.advance(step)
-
-        @pl.when(i >= 1)
+        for slot in range(1, blocks + 1):
+
+            @pl.when(i == slot - 1)
+            def _(slot=slot):
+                pump(slot)
+
+        @pl.when(i >= behind)
         def _():
-            rowsum.cross(i - 1)
-
-        @pl.when(i >= 2)
-        def _():
-            norm_block(i - 2)
+            norm_block(i - behind)
 
         return carry
 
     lax.fori_loop(0, blocks, attend_step, 0)
     rowsum.cross(blocks - 1)
-    norm_block(blocks - 2)
-    norm_block(blocks - 1)
-    for piece in dense:
-        piece.advance(steps)
-
-    def arrived(i, carry):
-        share.arrived(i)
-        return carry
-
-    lax.fori_loop(0, blocks, arrived, 0)
-    for piece in attend + dense:
-        piece.sent()
-    rowsum.finish(blocks)
-    share.finish(blocks)
-
-    def sent_small(k, carry):
-        small_copy(me, (me + k) % count).wait_send()
-        return carry
-
-    lax.fori_loop(1, count, sent_small, 0)
-
-
-def gelu_parts(z):
-    phi = 0.5 + 0.5 * lax.erf(z * (0.5**0.5))
-    slope = phi + z * (jnp.exp(-0.5 * z * z) * (2.0 * 3.141592653589793) ** -0.5)
-    return z * phi, slope
-
-
-def mlp_kernel(
-    a2_ref, cot_ref, h2_ref, w_ref, vec_ref, bias_ref,
-    down_ref, ga_ref, gh2_ref, grad_ref, gbias_ref, gvec_ref,
-    term, given, sent, crossed, up_sum, down_sum,
-    sum_sems, share_sems,
-):
-    total_rows, width = a2_ref.shape
-    blocks = total_rows // BLOCK
-    half = BLOCK // 2
-    greeted = greet(tensor_peers())
-    gbias_ref[...] = jnp.zeros_like(gbias_ref)
-    gvec_ref[...] = jnp.zeros_like(gvec_ref)
-    greeted()
-    rowsum = RowSum(term, given, sent, crossed, sum_sems)
-    share = Share(ga_ref, share_sems)
+    norm_block(blocks - 3)
+
+    whole = [
+        pltpu.make_async_copy(source, target, whole_sems.at[k])
+        for k, (source, target) in enumerate(
+            (
+                (own_ref, own_hbm), (qa_ref, qa_hbm), (ka_ref, ka_hbm), (va_ref, va_hbm),
+                (o_ref, o_hbm), (w_ref, w_hbm), (wo_ref, wo_hbm), (up_ref, up_hbm), (dn_ref, dn_hbm),
+            )
+        )
+    ]
+    for copy in whole[:-2]:
+        copy.start()
+    down_out = fetch(down_ref, down_hbm, local_sems.at[5])
+
+    def gh2_out(i):
+        own = pl.ds(pl.multiple_of(i * half, half), half)
+        return pltpu.make_async_copy(gh2_ref.at[own, :], gh2_hbm.at[own, :], local_sems.at[6, i])
+
+    rowsum2 = RowSum(term2, given2, sent2, crossed2, sum2_sems)
+
+    def ga_copies(i):
+        there = share.rows(i, core)
+        here = ga_ref.at[pl.ds(pl.multiple_of(i * half, half), half), :]
+        return (
+            pltpu.make_async_copy(here, ga_hbm.at[there, :], local_sems.at[4, i]),
+            pltpu.make_async_remote_copy(
+                src_ref=here,
+                dst_ref=ga_hbm.at[there, :],
+                send_sem=put_sems.at[0, i],
+                recv_sem=put_sems.at[1, i],
+                device_id=(me, share.mate),
+                device_id_type=MESH,
+            ),
+        )
 
     def mlp_block(i):
         rows = pl.ds(pl.multiple_of(i * BLOCK, BLOCK), BLOCK)
-        a2 = a2_ref[rows, :]
+        share.arrived(i)
+        a2 = norm_ref[rows, :]
         gy = cot_ref[rows, :]
-        u, slope = gelu_parts(dot(a2, w_ref[0]) + bias_ref[0:1, :])
+        u, slope = gelu_parts(dot(a2, wd_ref[0]) + b1_ref[...])
         ul = u.astype(half_type)
-        gz = (dot(gy, w_ref[1]) * slope).astype(half_type)
-        term[i] = dot(gz, w_ref[0], 1, 1).astype(half_type)
-        rowsum.give(i)
+        gz = (dot(gy, wd_ref[1]) * slope).astype(half_type)
+        rowsum2.free(i)
+        term2[i % term2.shape[0]] = dot(gz, wd_ref[0], 1, 1).astype(half_type)
+        rowsum2.give(i)
         gbias_ref[0:1, :] += jnp.sum(gz.astype(full_type), axis=0, keepdims=True)
-        down_ref[rows, :] = dot(ul, w_ref[1], 1, 1).astype(half_type)
+        down_ref[rows, :] = dot(ul, wd_ref[1], 1, 1).astype(half_type)
+        down_out(i).start()
         up = dot(a2, gz, 0, 0)
-        down = dot(gy, ul, 0, 0)
 
         @pl.when(i == 0)
         def _():
-            up_sum[...] = up
-            down_sum[...] = down
+            up_ref[...] = up
 
         @pl.when(i > 0)
         def _():
-            up_sum[...] += up
-            down_sum[...] += down
+            up_ref[...] += up
+
+        rowsum2.cross(i)
+        dn = dot(gy, ul, 0, 0)
+
+        @pl.when(i == 0)
+        def _():
+            dn_ref[...] = dn
+
+        @pl.when(i > 0)
+        def _():
+            dn_ref[...] += dn
 
     def back_block(i):
         own = pl.ds(pl.multiple_of(i * half, half), half)
-        gn = rowsum.total(i)
-        unit, rate = normalized(h2_ref[own, :])
+        gn = rowsum2.total(i)
+        h2_out(i).wait()
+        unit, rate = normalized(gh2_ref[own, :])
         e = gn * vec_ref[4:5, :]
         inner = e - jnp.mean(e, axis=-1, keepdims=True)
         inner = inner - unit * jnp.mean(e * unit, axis=-1, keepdims=True)
-        gy = cot_ref[share.rows(i, share.core), :].astype(full_type)
+        gy = cot_ref[share.rows(i, core), :].astype(full_type)
         gh = gy + rate * inner
         gh2_ref[own, :] = gh
-        share.put(i, gh.astype(half_type))
+        gh2_out(i).start()
+        ga_ref[own, :] = gh.astype(half_type)
+        for copy in ga_copies(i):
+            copy.start()
         gvec_ref[0:1, :] += jnp.sum(gh, axis=0, keepdims=True)
         gvec_ref[1:2, :] += jnp.sum(gy, axis=0, keepdims=True)
         gvec_ref[4:5, :] += jnp.sum(gn * unit, axis=0, keepdims=True)
         gvec_ref[5:6, :] += jnp.sum(gn, axis=0, keepdims=True)
 
-    def step(i, carry):
+    def mlp_step(i, carry):
         mlp_block(i)
 
-        @pl.when(i >= 1)
+        @pl.when(i < 2)
         def _():
-            rowsum.cross(i - 1)
+            norm_block(blocks - 2 + i)
 
         @pl.when(i >= 2)
         def _():
@@ -499,20 +613,43 @@
 
         return carry
 
-    lax.fori_loop(0, blocks, step, 0)
-    rowsum.cross(blocks - 1)
-    grad_ref[0] = up_sum[...].astype(half_type)
-    grad_ref[1] = down_sum[...].astype(half_type)
+    lax.fori_loop(0, blocks, mlp_step, 0)
+    for copy in whole[-2:]:
+        copy.start()
     back_block(blocks - 2)
     back_block(blocks - 1)
 
-    def arrived(i, carry):
-        share.arrived(i)
-        return carry
-
-    lax.fori_loop(0, blocks, arrived, 0)
-    rowsum.finish(blocks)
+    def copied(i, carry):
+        down_out(i).wait()
+        gh2_out(i).wait()
+        here, there = ga_copies(i)
+        here.wait()
+        there.wait_send()
+        piece = ga_hbm.at[share.rows(i, 1 - core), :]
+        pltpu.make_async_remote_copy(
+            src_ref=piece,
+            dst_ref=piece,
+            send_sem=put_sems.at[0, i],
+            recv_sem=put_sems.at[1, i],
+            device_id=(me, share.mate),
+            device_id_type=MESH,
+        ).wait_recv()
+        return carry
+
+    lax.fori_loop(0, blocks, copied, 0)
+    for copy in whole:
+        copy.wait()
+    for piece in attend + dense:
+        piece.sent()
+    rowsum.finish()
+    rowsum2.finish()
     share.finish(blocks)
+
+    def sent_small(k, carry):
+        small_copy(me, (me + k) % count).wait_send()
+        return carry
+
+    lax.fori_loop(1, count, sent_small, 0)
 
 
 class Scatter:
@@ -564,7 +701,7 @@
 
 
 def attention_back_kernel(
-    count, ga_ref, o_ref, qb_ref, ka_ref, va_ref, wo_ref, grad_ref, down_ref, h2_ref, vec_ref,
+    count, ga_ref, o_ref, qb_ref, ka_ref, va_ref, wo_ref, up_ref, dn_ref, down_ref, h2_ref, vec_ref,
     gqkv_ref, sum_ref, out_ref,
     goa_ref, kt_ref, gqt_ref, given, sent, crossed, stage, taken,
     sum_sems, share_sems, scatter_sems,
@@ -579,7 +716,7 @@
     greeted()
 
     def view(way, block):
-        return grad_ref[way, pl.ds(pl.multiple_of(block * wide, wide), wide), :]
+        return (up_ref, dn_ref)[way][pl.ds(pl.multiple_of(block * wide, wide), wide), :]
 
     scatter = Scatter(view, stage, taken, scatter_sems, count)
     scatter.begin()
@@ -690,7 +827,7 @@
 
     lax.fori_loop(0, blocks, arrived, 0)
     scatter.finish()
-    rowsum.finish(blocks)
+    rowsum.finish()
     share.finish(blocks)
 
 
@@ -756,7 +893,7 @@
     def norm_block(i):
         own = pl.ds(pl.multiple_of(i * half, half), half)
         gn = rowsum.total(i)
-        unit, rate = normalized(tok_ref[share.rows(i, share.core), :].astype(full_type))
+        unit, rate = normalized(tok_ref[own, :].astype(full_type))
         e = gn * vec_ref[2:3, :]
         inner = e - jnp.mean(e, axis=-1, keepdims=True)
         inner = inner - unit * jnp.mean(e * unit, axis=-1, keepdims=True)
@@ -839,7 +976,7 @@
 
     lax.fori_loop(0, blocks, arrived, 0)
     scatter.finish()
-    rowsum.finish(blocks)
+    rowsum.finish()
     share.finish(blocks)
     for part in range(2):
 
@@ -850,39 +987,11 @@
         lax.fori_loop(1, count, done, 0)
 
 
-def permute_kernel(back, owner_ref, *refs):
-    for x_ref, y_ref in zip(refs[: len(refs) // 2], refs[len(refs) // 2 :]):
-        count = owner_ref.shape[0]
-        wide = x_ref.shape[1] // count
-        for j in range(count):
-            natural = pl.ds(pl.multiple_of(owner_ref[j] * wide, wide), wide)
-            stored = slice(j * wide, (j + 1) * wide)
-            if back:
-                y_ref[:, natural] = x_ref[:, stored]
-            else:
-                y_ref[:, stored] = x_ref[:, natural]
-
-
-def permuted(arrays, owner, back):
-    rows, width = arrays[0].shape
+def permuted(x, owner, back):
+    rows, width = x.shape
     count = owner.shape[0]
-    wide = width // count
-    if wide % LANES:
-        order = jnp.argsort(owner) if back else owner
-        shape = (rows, count, wide)
-        return [jnp.take(x.reshape(shape), order, axis=1).reshape(rows, width) for x in arrays]
-    spec = pl.BlockSpec((BLOCK, width), lambda i, *_: (i, 0))
-    return pl.pallas_call(
-        functools.partial(permute_kernel, back),
-        out_shape=[jax.ShapeDtypeStruct(x.shape, x.dtype) for x in arrays],
-        grid_spec=pltpu.PrefetchScalarGridSpec(
-            num_scalar_prefetch=1,
-            grid=(rows // BLOCK,),
-            in_specs=[spec] * len(arrays),
-            out_specs=[spec] * len(arrays),
-        ),
-        compiler_params=pltpu.CompilerParams(vmem_limit_bytes=32 * 2**20),
-    )(owner, *arrays)
+    order = jnp.argsort(owner) if back else owner
+    return jnp.take(x.reshape(rows, count, -1), order, axis=1).reshape(rows, width)
 
 
 def adamw_step(weight, first, second, grad, rate, decay):
@@ -894,30 +1003,89 @@
     return (first_next, second_next, weight - rate * update)
 
 
-def pack_small(vector_master, bias_master, owner, count):
+def last_kernel(rates, owner_ref, *refs):
+    count = owner_ref.shape[0]
+    given, refs = refs[:5], refs[5:]
+    layer, grad, weight_sum, dense_sum, small = given
+    state, refs = refs[:15], refs[15:]
+    results, outs = refs[:2], refs[2:]
+
+    def step(k, grad, at=(Ellipsis,)):
+        new = adamw_step(*(ref[at] for ref in state[3 * k : 3 * k + 3]), grad, *rates[k])
+        for ref, value in zip(outs[3 * k : 3 * k + 3], new):
+            ref[at] = value
+
+    wide = layer.shape[1] // count
+    if wide % LANES == 0:
+        for j in range(count):
+            natural = pl.ds(pl.multiple_of(owner_ref[j] * wide, wide), wide)
+            for x, y in zip((layer, grad), results):
+                y[:, natural] = x[:, j * wide : (j + 1) * wide]
+    else:
+        for x, y in zip((layer, grad), results):
+            y[...] = x[...]
+    step(0, weight_sum[0:3])
+    step(1, weight_sum[3])
+    ratio, local_width = state[6].shape[2:]
+    for r in range(ratio):
+        step(
+            2,
+            dense_sum[:, :, r * local_width : (r + 1) * local_width],
+            (slice(None), slice(None), r, slice(None)),
+        )
     me = lax.axis_index("dp")
-    wide = vector_master.shape[1]
-    lanes = max(LANES, wide)
-    fold = lanes // wide
-    lane = jnp.arange(lanes)
-    vectors = jnp.where(lane // wide == me % fold, jnp.tile(vector_master, (1, fold)), 0.0)
-    narrow = bias_master.shape[1]
-    spot = jnp.arange(narrow * count)
-    biases = jnp.where(spot // narrow == owner[me], jnp.tile(bias_master, (1, count)), 0.0)
-    small = jnp.concatenate(
-        [jnp.pad(vectors, ((0, 2), (0, 0))), jnp.pad(biases, ((0, 3), (0, 0)))], axis=1
+    lanes = small.shape[1] - local_width
+
+    def chosen(x, start, size):
+        row = lax.broadcasted_iota(jnp.int32, (x.shape[1], size), 0)
+        column = lax.broadcasted_iota(jnp.int32, (x.shape[1], size), 1)
+        pick = jnp.where(row == column + start, 1.0, 0.0).astype(half_type)
+        return sum(dot(part.astype(half_type), pick) for part in three_parts(x))
+
+    narrow, wide = state[9].shape[1], state[12].shape[1]
+    step(3, chosen(small[:, lanes:], owner_ref[me] * narrow, narrow)[: 1 + ratio])
+    step(4, chosen(small[:, :lanes], me % (lanes // wide) * wide, wide)[:6])
+
+
+def last(owner, layer_output, tokens_grad, weight_sum, dense_sum, small_sum, *state):
+    steps = 8 if dense_sum.shape[1] % 128 == 0 else 1
+    rates = (
+        (matrix_rate, matrix_decay),
+        (output_rate, matrix_decay),
+        (matrix_rate, matrix_decay),
+        (bias_rate, 0.0),
+        (vector_rate, 0.0),
     )
-    return small.astype(half_type).astype(full_type)
-
-
-def call(kernel, collective, outs, scratch, operands, scalars=0, limit=58):
-    vmem = pl.BlockSpec(memory_space=pltpu.VMEM)
-    smem = pl.BlockSpec(memory_space=pltpu.SMEM)
+
+    def spec(x, dim):
+        shape = tuple(n // steps if k == dim else n for k, n in enumerate(x.shape))
+        return pl.BlockSpec(shape, lambda i, *_: tuple(i if k == dim else 0 for k in range(x.ndim)))
+
+    dims = [0, 0, 1, 1, None] + [1] * 3 + [0] * 3 + [1] * 3 + [None] * 6
+    operands = (layer_output, tokens_grad, weight_sum, dense_sum, small_sum) + state
+    specs = [spec(x, dim) for x, dim in zip(operands, dims)]
+    outs = operands[:2] + state
+    return pl.pallas_call(
+        functools.partial(last_kernel, rates),
+        out_shape=[jax.ShapeDtypeStruct(x.shape, x.dtype) for x in outs],
+        grid_spec=pltpu.PrefetchScalarGridSpec(
+            num_scalar_prefetch=1, grid=(steps,), in_specs=specs, out_specs=specs[:2] + specs[5:]
+        ),
+        compiler_params=pltpu.CompilerParams(vmem_limit_bytes=60 * 2**20),
+    )(owner, *operands)
+
+
+def call(kernel, collective, outs, scratch, operands, spaces, limit=62):
+    spec = {
+        "s": pl.BlockSpec(memory_space=pltpu.SMEM),
+        "v": pl.BlockSpec(memory_space=pltpu.VMEM),
+        "h": pl.BlockSpec(memory_space=pl.ANY),
+    }
     return pl.pallas_call(
         kernel,
         out_shape=[jax.ShapeDtypeStruct(shape, dtype) for shape, dtype in outs],
-        in_specs=[smem] * scalars + [vmem] * (len(operands) - scalars),
-        out_specs=[vmem] * len(outs),
+        in_specs=[spec[c] for c in spaces[0]],
+        out_specs=[spec[c] for c in spaces[1]],
         scratch_shapes=scratch,
         compiler_params=pltpu.CompilerParams(
             collective_id=collective, has_side_effects=True, vmem_limit_bytes=limit * 2**20
@@ -960,68 +1128,73 @@
     half = BLOCK // 2
     wide = width // count
     lanes = max(LANES, wide)
-    me = lax.axis_index("dp")
-
-    tok, cot = permuted([tokens, cotangent], owner, False)
-    small = pack_small(vector_master, bias_master, owner, count)
-    ends = jnp.cumsum(lengths[0])
+    tok, cot = tokens, cotangent
+    if wide % LANES:
+        tok, cot = (permuted(x, owner, False) for x in (tokens, cotangent))
     row_sum = [pltpu.VMEM((blocks, half, width), half_type)] * 3
+    two_terms = pltpu.VMEM((2, BLOCK, width), half_type)
     heads_shape = (heads, rows, LANES)
-    a1, qb, ka, va, o, a2, h2, w, wo, wd, vec, bias = call(
+    small = (8, lanes + local_width)
+    a1, ga, h2, own, qb, ka, va, o, w, wo, gh2, down, up, dn, vec, gbias, gvec = call(
         functools.partial(front_kernel, count),
         0,
         [
             ((rows, width), half_type),
+            ((rows, width), half_type),
+            ((rows // 2, width), full_type),
+            ((rows // 2, width), half_type),
             (heads_shape, half_type),
             (heads_shape, half_type),
             (heads_shape, half_type),
             ((rows, local_width), half_type),
-            ((rows, width), half_type),
-            ((rows // 2, width), full_type),
             ((width, 3 * local_width), half_type),
             ((width, local_width), half_type),
-            ((2, width, hidden), half_type),
+            ((rows // 2, width), full_type),
+            ((rows, width), half_type),
+            ((width, hidden), full_type),
+            ((width, hidden), full_type),
             ((8, width), full_type),
-            ((8, local_width), full_type),
+            ((8, hidden), full_type),
+            ((8, width), full_type),
         ],
         [
-            pltpu.VMEM(heads_shape, half_type),
-            pltpu.VMEM((count,) + small.shape, full_type),
-            pltpu.VMEM((blocks, BLOCK, width), half_type),
+            pltpu.VMEM((rows // 2, width), half_type),
+            *[pltpu.VMEM(heads_shape, half_type)] * 3,
+            pltpu.VMEM((rows, local_width), half_type),
+            pltpu.VMEM((width, 3 * local_width), half_type),
+            pltpu.VMEM((width, local_width), half_type),
+            pltpu.VMEM((rows // 2, width), full_type),
+            pltpu.VMEM((rows, width), half_type),
+            *[pltpu.VMEM((width, hidden), full_type)] * 2,
+            *[pltpu.VMEM((rows, width), half_type)] * 2,
+            pltpu.VMEM((2, width, hidden), half_type),
+            pltpu.VMEM((rows // 2, width), half_type),
+            pltpu.VMEM((8, local_width), full_type),
+            pltpu.VMEM((1, hidden), full_type),
+            pltpu.VMEM(small, full_type),
+            pltpu.VMEM((count,) + small, full_type),
+            two_terms,
+            *row_sum,
+            two_terms,
             *row_sum,
             dma(6, 4, count // 2),
             dma(2, count),
             dma(4, blocks),
-            dma(2, blocks),
-        ],
-        (ends, tok, attend_master, output_master, dense_master, small),
-        scalars=1,
-    )
-    bias_up = bias[1 : 1 + ratio].reshape(1, hidden)
-    down, ga, gh2, grad, gbias, gvec = call(
-        mlp_kernel,
-        1,
-        [
-            ((rows, width), half_type),
-            ((rows, width), half_type),
-            ((rows // 2, width), full_type),
-            ((2, width, hidden), half_type),
-            ((8, hidden), full_type),
-            ((8, width), full_type),
-        ],
-        [
-            pltpu.VMEM((blocks, BLOCK, width), half_type),
-            *row_sum,
-            pltpu.VMEM((width, hidden), full_type),
-            pltpu.VMEM((width, hidden), full_type),
             dma(4, blocks),
             dma(2, blocks),
+            dma(2, blocks),
+            dma(7, blocks),
+            dma(9),
         ],
-        (a2, cot, h2, wd, vec, bias_up),
+        (
+            lengths, owner, tok, cot, attend_master, output_master, dense_master, vector_master,
+            bias_master,
+        ),
+        ("sshhvvvvv", "h" * 14 + "vvv"),
     )
     gqkv, dense_sum, layer_output = call(
         functools.partial(attention_back_kernel, count),
-        2,
+        1,
         [
             ((rows, 3 * local_width), half_type),
             ((2, wide, hidden), full_type),
@@ -1038,11 +1211,12 @@
             dma(2, blocks),
             dma(4, count - 1),
         ],
-        (ga, o, qb, ka, va, wo, grad, down.reshape(blocks, BLOCK, width), h2, vec),
+        (ga, o, qb, ka, va, wo, up, dn, down.reshape(blocks, BLOCK, width), h2, vec),
+        ("v" * 11, "v" * 3),
     )
     tokens_grad, weight_sum, small_sum = call(
         functools.partial(end_kernel, count),
-        3,
+        2,
         [
             ((rows, width), half_type),
             ((4, wide, local_width), full_type),
@@ -1063,38 +1237,20 @@
             dma(4, count),
             dma(2),
         ],
-        (gqkv, w, a1, ga, o, gh2, tok, vec, gbias, gvec),
+        (gqkv, w, a1, ga, o, gh2, own, vec, gbias, gvec),
+        ("v" * 10, "v" * 3),
     )
-    layer_output, tokens_grad = permuted([layer_output, tokens_grad], owner, True)
-    dense_sum = dense_sum.reshape(dense_master.shape)
-    vector_sum = lax.dynamic_slice_in_dim(
-        small_sum[:6, :lanes], me % (lanes // wide) * wide, wide, axis=1
-    )
-    narrow = bias_master.shape[1]
-    bias_sum = lax.dynamic_slice_in_dim(
-        small_sum[: 1 + ratio, lanes:], owner[me] * narrow, narrow, axis=1
-    )
-    attend_new = adamw_step(
-        attend_master, attend_first, attend_second, weight_sum[:3], matrix_rate, matrix_decay
-    )
-    output_new = adamw_step(
-        output_master, output_first, output_second, weight_sum[3], output_rate, matrix_decay
-    )
-    dense_new = adamw_step(
-        dense_master, dense_first, dense_second, dense_sum, matrix_rate, matrix_decay
-    )
-    bias_new = adamw_step(bias_master, bias_first, bias_second, bias_sum, bias_rate, 0.0)
-    vector_new = adamw_step(
-        vector_master, vector_first, vector_second, vector_sum, vector_rate, 0.0
-    )
-    return (
-        layer_output,
-        tokens_grad,
-        *attend_new,
-        *output_new,
-        *dense_new,
-        *bias_new,
-        *vector_new,
+    if wide % LANES:
+        layer_output, tokens_grad = (permuted(x, owner, True) for x in (layer_output, tokens_grad))
+    return tuple(
+        last(
+            owner, layer_output, tokens_grad, weight_sum, dense_sum, small_sum,
+            attend_master, attend_first, attend_second,
+            output_master, output_first, output_second,
+            dense_master, dense_first, dense_second,
+            bias_master, bias_first, bias_second,
+            vector_master, vector_first, vector_second,
+        )
     )
 
 

time: 340 us -> 279 us (0.82)
  Pallas kernels: 311 us -> 278 us
  local copies, waits for them, and re-layouts: 15.5 us -> 0 us
  other arithmetic: 11 us -> 0 us
    pallas_call x4 -> x3, Pallas kernels: 303 us -> 264 us  [call(): pl.pallas_call(kernel, out_shape=[jax.ShapeDtypeStruct(shape, dtype) for...]
    unnamed x50 -> x0, local copies, waits for them, and re-layouts: 11.8 us -> none
    sub x5 -> x0, other arithmetic: 7.72 us -> none  [adamw_step(): return (first_next, second_next, weight - rate * update)]
    pallas_call x2 -> x1, Pallas kernels: 7.81 us -> 13.7 us  [last(): pl.pallas_call(functools.partial(last_kernel, rates), out_shape=[jax.Shap...]
where the time goes in v3:
time: 279 us
  Pallas kernels  278 us (100%)
    pallas_call x3, Pallas kernels, call(): pl.pallas_call(kernel, out_shape=[jax.ShapeDtypeStruct(shape, dtype) for...  264 us
    pallas_call x1, Pallas kernels, last(): pl.pallas_call(functools.partial(last_kernel, rates), out_shape=[jax.Shap...  13.7 us

profile of v3, /device:TPU:0, one launch (start us, length us, event | category | flops | bytes accessed | tf_op | source)
XLA Modules:
  0.0 278.9 jit_solution(14259424290239390430)
XLA Ops:
  0.7 132.1 %shard_map.314 = (bf16[1792,1024]{1,0:T(8,128)(2,1)}, bf16[1792,1024]{1,0:T(8,128)(2,1)}, f32[896,1024]{1,0:T(8,128)}, bf16[896,1024]{1,0:T(8,128)(2,1)}, bf16[4...) custom-call(s32[1,8]{1,0:T(1,128)} %len_ref.1, ...), custom_call_target="tpu_custom_call" | custom-call | tf_op jit(solution)/shard_map/pallas_call | solution.py:1084
  132.7 68.9 %shard_map.315 = (bf16[1792,768]{1,0:T(8,128)(2,1)}, f32[2,128,1024]{2,1,0:T(8,128)}, bf16[1792,1024]{1,0:T(8,128)(2,1)}) custom-call(bf16[1792,1024]{1,0:T(8,128)(2,1)} %get-tuple-element.40.ga_ref, bf16[1792,256]{1,0:T(8,128)(2,1)} %get-tuple-element.41.o_ref, bf16[4,1792,128]{2,1,0:T(8,128)(2,1)} %get-tuple-element.42.qb_ref, ...), custom_call_target="tpu_custom_call" | custom-call | tf_op jit(solution)/shard_map/pallas_call | solution.py:1084
  201.6 63.4 %shard_map.316 = (bf16[1792,1024]{1,0:T(8,128)(2,1)}, f32[4,128,256]{2,1,0:T(8,128)}, f32[8,384]{1,0:T(8,128)}) custom-call(bf16[1792,768]{1,0:T(8,128)(2,1)} %get-tuple-element.52.gqkv_ref, bf16[1024,768]{1,0:T(8,128)(2,1)} %get-tuple-element.53.w_ref, bf16[1792,1024]{1,0:T(8,128)(2,1)} %get-tuple-element.54.a1_ref, ...), custom_call_target="tpu_custom_call" | custom-call | tf_op jit(solution)/shard_map/pallas_call | solution.py:1084
  265.0 13.7 %shard_map.317 = (bf16[1792,1024]{1,0:T(8,128)(2,1)}, bf16[1792,1024]{1,0:T(8,128)(2,1)}, f32[3,128,256]{2,1,0:T(8,128)}, f32[3,128,256]{2,1,0:T(8,128)}, f32[3,...) custom-call(s32[8]{0:T(128)} %owner_ref.3, ...), custom_call_target="tpu_custom_call" | custom-call | tf_op jit(solution)/shard_map/pallas_call | solution.py:1068

commit v4 on v3

--- a/solution.py
+++ b/solution.py
@@ -93,7 +93,7 @@
 class RowSum:
     def __init__(self, term, given, sent, crossed, sems):
         self.term, self.given, self.sent_ref, self.crossed = term, given, sent, crossed
-        self.slots, self.blocks = term.shape[0], given.shape[0]
+        self.slots, self.sent_slots, self.blocks = term.shape[0], sent.shape[0], given.shape[0]
         self.sems = sems
         self.half = given.shape[1]
         self.dp, tensor = lax.axis_index("dp"), lax.axis_index("tensor")
@@ -116,7 +116,7 @@
 
     def _cross(self, i):
         return pltpu.make_async_remote_copy(
-            src_ref=self.sent_ref.at[i],
+            src_ref=self.sent_ref.at[i % self.sent_slots],
             dst_ref=self.crossed.at[i],
             send_sem=self.sems.at[2, i],
             recv_sem=self.sems.at[3, i],
@@ -137,24 +137,37 @@
     def cross(self, i):
         self._give(i).wait_recv()
         mine = self.term[i % self.slots, self.rows(self.core), :].astype(full_type)
-        self.sent_ref[i] = (mine + self.given[i].astype(full_type)).astype(half_type)
+        if self.sent_slots < self.blocks:
+
+            @pl.when(i >= self.sent_slots)
+            def _():
+                self._cross(i - self.sent_slots).wait_send()
+
+        total = mine + self.given[i].astype(full_type)
+        self.sent_ref[i % self.sent_slots] = total.astype(half_type)
         self._cross(i).start()
 
     def total(self, i):
         self._cross(i).wait_recv()
-        return self.sent_ref[i].astype(full_type) + self.crossed[i].astype(full_type)
-
-    def finish(self):
+        mine = self.sent_ref[i % self.sent_slots].astype(full_type)
+        return mine + self.crossed[i].astype(full_type)
+
+    def gone(self):
         def given(i, carry):
             self._give(i).wait_send()
             return carry
 
+        lax.fori_loop(max(self.blocks - self.slots, 0), self.blocks, given, 0)
+
+    def finish(self, given=True):
+        if given:
+            self.gone()
+
         def crossed(i, carry):
             self._cross(i).wait_send()
             return carry
 
-        lax.fori_loop(max(self.blocks - self.slots, 0), self.blocks, given, 0)
-        lax.fori_loop(0, self.blocks, crossed, 0)
+        lax.fori_loop(max(self.blocks - self.sent_slots, 0), self.blocks, crossed, 0)
 
 
 class Share:
@@ -656,13 +669,14 @@
     def __init__(self, view, stage, taken, sems, count):
         self.view, self.stage, self.taken = view, stage, taken
         self.sems, self.count = sems, count
+        self.slots = stage.shape[1]
         self.pos = ring_pos(lax.axis_index("dp"), count)
         self.tensor = lax.axis_index("tensor")
 
     def _copy(self, way, step):
         sign = 1 - 2 * way
         return pltpu.make_async_remote_copy(
-            src_ref=self.stage.at[way, step],
+            src_ref=self.stage.at[way, step % self.slots],
             dst_ref=self.taken.at[way, step],
             send_sem=self.sems.at[2 * way, step],
             recv_sem=self.sems.at[2 * way + 1, step],
@@ -672,39 +686,86 @@
 
     def begin(self):
         for way in range(2):
-            block = ring_at(self.pos - (1 - 2 * way), self.count)
-            self.stage[way, 0] = self.view(way, block).astype(half_type)
+            self.stage[way, 0] = self.view(way, 0).astype(half_type)
             self._copy(way, 0).start()
 
     def advance(self, step):
         for way in range(2):
-            block = ring_at(self.pos - (1 - 2 * way) * (1 + step), self.count)
             self._copy(way, step - 1).wait_recv()
-            own = self.view(way, block).astype(full_type)
-            total = self.taken[way, step - 1].astype(full_type) + own
-            self.stage[way, step] = total.astype(half_type)
+            total = self.taken[way, step - 1].astype(full_type) + self.view(way, step)
+
+            @pl.when(step >= self.slots)
+            def _(way=way):
+                self._copy(way, step - self.slots).wait_send()
+
+            self.stage[way, step % self.slots] = total.astype(half_type)
             self._copy(way, step).start()
 
     def total(self, way):
         last = self.count - 2
         self._copy(way, last).wait_recv()
-        own = self.view(way, lax.axis_index("dp")).astype(full_type)
-        return self.taken[way, last].astype(full_type) + own
+        return self.taken[way, last].astype(full_type) + self.view(way, last + 1)
 
     def finish(self):
-        def done(step, carry):
+        for step in range(max(self.count - 1 - self.slots, 0), self.count - 1):
             for way in range(2):
                 self._copy(way, step).wait_send()
-            return carry
-
-        lax.fori_loop(0, self.count - 1, done, 0)
-
-
-def attention_back_kernel(
-    count, ga_ref, o_ref, qb_ref, ka_ref, va_ref, wo_ref, up_ref, dn_ref, down_ref, h2_ref, vec_ref,
-    gqkv_ref, sum_ref, out_ref,
-    goa_ref, kt_ref, gqt_ref, given, sent, crossed, stage, taken,
-    sum_sems, share_sems, scatter_sems,
+
+
+def sent_block(pos, way, step, count):
+    return ring_at(pos - (1 - 2 * way) * (1 + step), count)
+
+
+class Put:
+    def __init__(self, held, result, sems):
+        self.held, self.result, self.sems = held, result, sems
+        self.half = held.shape[0] // sems.shape[1]
+        self.dp, tensor = lax.axis_index("dp"), lax.axis_index("tensor")
+        self.core = tensor % 2
+        self.mate = tensor - tensor % 2 + (tensor + 1) % 2
+
+    def own(self, i):
+        return pl.ds(pl.multiple_of(i * self.half, self.half), self.half)
+
+    def _rows(self, i, core):
+        return pl.ds(pl.multiple_of((2 * i + core) * self.half, self.half), self.half)
+
+    def _here(self, i):
+        target = self.result.at[self._rows(i, self.core), :]
+        return pltpu.make_async_copy(self.held.at[self.own(i), :], target, self.sems.at[0, i])
+
+    def _there(self, i, core):
+        return pltpu.make_async_remote_copy(
+            src_ref=self.held.at[self.own(i), :],
+            dst_ref=self.result.at[self._rows(i, core), :],
+            send_sem=self.sems.at[1, i],
+            recv_sem=self.sems.at[2, i],
+            device_id=(self.dp, self.mate),
+            device_id_type=MESH,
+        )
+
+    def put(self, i, value):
+        self.held[self.own(i), :] = value
+        self._here(i).start()
+        self._there(i, self.core).start()
+
+    def left(self, i):
+        self._here(i).wait()
+        self._there(i, self.core).wait_send()
+
+    def arrived(self, i):
+        self._there(i, 1 - self.core).wait_recv()
+
+
+def back_kernel(
+    count, ga_hbm, o_ref, qb_ref, ka_ref, va_ref, wo_ref, w_ref, up_hbm, dn_hbm, down_hbm, h2_hbm,
+    gh2_hbm, own_hbm, a1_hbm, vec_ref, gbias_ref, gvec_ref,
+    layer_hbm, tg_hbm, dense_ref, sum_ref, small_ref,
+    ga_ref, wide_ref, gh_ref, own_ref, goa_ref, kt_ref, gqt_ref, gqkv_ref, put_ref,
+    given, sent, crossed, term2, given2, sent2, crossed2,
+    terms, stage, taken, grads, stage2, taken2, small_mine, small_taken, small_mate,
+    sum_sems, sum2_sems, put_sems, put2_sems, scatter_sems, scatter2_sems, small_sems, mate_sems,
+    local_sems, terms_sems,
 ):
     total_rows, width = ga_ref.shape
     local_width = wo_ref.shape[1]
@@ -712,22 +773,97 @@
     blocks = total_rows // BLOCK
     half = BLOCK // 2
     wide = width // count
-    greeted = greet(tensor_peers() + ring_peers(count))
+    hops = count - 1
+    lanes = small_ref.shape[1] - local_width
+    fold = lanes // wide
+    me, tensor = lax.axis_index("dp"), lax.axis_index("tensor")
+    mate = tensor - tensor % 2 + (tensor + 1) % 2
+    pos = ring_pos(me, count)
+    greeted = greet(tensor_peers() + dp_peers(count))
+
+    def own_rows(i):
+        return pl.ds(pl.multiple_of(i * half, half), half)
+
+    def place(block):
+        return pl.ds(pl.multiple_of(block * wide, wide), wide)
+
+    def own_fetch(source, target, sems):
+        return lambda i: pltpu.make_async_copy(
+            source.at[own_rows(i), :], target.at[own_rows(i), :], sems.at[i]
+        )
+
+    ga_in = fetch(ga_hbm, ga_ref, local_sems.at[0])
+    down_in = fetch(down_hbm, wide_ref, local_sems.at[1])
+    a1_in = fetch(a1_hbm, wide_ref, local_sems.at[2])
+    h2_in = own_fetch(h2_hbm, gh_ref, local_sems.at[3])
+    gh2_in = own_fetch(gh2_hbm, gh_ref, local_sems.at[4])
+    own_in = own_fetch(own_hbm, own_ref, local_sems.at[5])
+
+    def term_in(way, step):
+        rows = place(sent_block(pos, way, step, count))
+        source = (up_hbm, dn_hbm)[way].at[rows, :]
+        return pltpu.make_async_copy(
+            source, terms.at[way, step % 2], terms_sems.at[way, step % 2]
+        )
+
+    def each(copy):
+        def start(i, carry):
+            copy(i).start()
+            return carry
+
+        lax.fori_loop(0, blocks, start, 0)
+
+    for step in range(2):
+        for way in range(2):
+            term_in(way, step).start()
+    each(ga_in)
+    each(down_in)
+    each(h2_in)
+    each(own_in)
+    small_mine[:, :width] = gvec_ref[...]
+    ratio = gbias_ref.shape[1] // local_width
+    for r in range(ratio):
+        small_mine[1 + r : 2 + r, width:] = gbias_ref[0:1, r * local_width : (r + 1) * local_width]
+    small_mine[1 + ratio :, width:] = jnp.zeros((7 - ratio, local_width), full_type)
     greeted()
 
-    def view(way, block):
-        return (up_ref, dn_ref)[way][pl.ds(pl.multiple_of(block * wide, wide), wide), :]
-
-    scatter = Scatter(view, stage, taken, scatter_sems, count)
-    scatter.begin()
-    rowsum = RowSum(down_ref, given, sent, crossed, sum_sems)
-    share = Share(out_ref, share_sems)
+    pieces = stage.shape[0]
+    part = terms.shape[3] // pieces
+
+    def term_view(piece):
+        columns = slice(piece * part, (piece + 1) * part)
+        return lambda way, step: terms[way, step % 2, :, columns]
+
+    scatters = [
+        Scatter(term_view(p), stage.at[p], taken.at[p], scatter_sems.at[p], count)
+        for p in range(pieces)
+    ]
+
+    def terms_ready(step):
+        for way in range(2):
+            term_in(way, step).wait()
+
+    def terms_next(step):
+        @pl.when(step <= hops)
+        def _():
+            for way in range(2):
+                term_in(way, step).start()
+
+    terms_ready(0)
+    for scatter in scatters:
+        scatter.begin()
+    terms_next(2)
+
+    rowsum = RowSum(wide_ref.reshape(blocks, BLOCK, width), given, sent, crossed, sum_sems)
+    layer = Put(put_ref, layer_hbm, put_sems)
+    down_in(0).wait()
     rowsum.give(0)
     lane = lax.broadcasted_iota(jnp.int32, (BLOCK, LANES), 1)
     low_half = lane < HD
     spot = lane % HD
 
     def prepare(i, carry):
+        ga_in(i).wait()
         rows = pl.ds(pl.multiple_of(i * BLOCK, BLOCK), BLOCK)
         go = dot(ga_ref[rows, :], wo_ref[...]).astype(half_type).astype(full_type)
         both = go * o_ref[rows, :].astype(full_type)
@@ -735,10 +871,9 @@
             pair = slice(head // 2 * LANES, head // 2 * LANES + LANES)
             own = low_half if head % 2 == 0 else ~low_half
             inner = jnp.sum(jnp.where(own, both[:, pair], 0.0), axis=1, keepdims=True)
-            high, middle, low = three_parts(inner)
             filled = jnp.where(own, go[:, pair], 0.0)
-            for part, value in enumerate((high, middle, low)):
-                filled = jnp.where(~own & (spot == part), -value, filled)
+            for k, value in enumerate(three_parts(inner)):
+                filled = jnp.where(~own & (spot == k), -value, filled)
             goa_ref[head, rows, :] = filled.astype(half_type)
             if head % 2 == 0:
                 before = ka_ref[head, rows, :].astype(full_type)
@@ -748,9 +883,47 @@
         return carry
 
     lax.fori_loop(0, blocks, prepare, 0)
+    down_in(1).wait()
     rowsum.give(1)
 
-    def keys_block(j):
+    def output_block(i):
+        h2_in(i).wait()
+        total = gh_ref[own_rows(i), :] + rowsum.total(i) + vec_ref[1:2, :]
+        layer.put(i, total.astype(half_type))
+        gh2_in(i).start()
+
+    per = -(-hops // blocks)
+
+    def between(j, head):
+        if head == 0:
+            rowsum.cross(j)
+        for t in range(per):
+            hop = j * per + t
+
+            @pl.when((hop >= 1) & (hop < hops))
+            def _(hop=hop):
+                if head == 0:
+                    terms_ready(hop)
+                for p, scatter in enumerate(scatters):
+                    if p * heads // pieces == head:
+                        scatter.advance(hop)
+                if (pieces - 1) * heads // pieces == head:
+                    terms_next(hop + 2)
+
+        if head == 1:
+
+            @pl.when(j < blocks - 2)
+            def _():
+                down_in(j + 2).wait()
+                rowsum.give(j + 2)
+
+        if head == heads - 1:
+
+            @pl.when(j >= 1)
+            def _():
+                output_block(j - 1)
+
+    def keys_block(j, carry):
         rows = pl.ds(pl.multiple_of(j * BLOCK, BLOCK), BLOCK)
         for head in range(heads):
             scores = dot(ka_ref[head, rows, :], qb_ref[head], 1, 1)
@@ -773,184 +946,144 @@
             if head % 2 == 0:
                 gk_even, gv_even = gk, gv
             else:
-                pair = slice(head // 2 * LANES, head // 2 * LANES + LANES)
-                for part, value in ((1, (gk_even, gk)), (2, (gv_even, gv))):
-                    base = part * local_width + head // 2 * LANES
+                for k, value in ((1, (gk_even, gk)), (2, (gv_even, gv))):
+                    base = k * local_width + head // 2 * LANES
                     gqkv_ref[rows, base : base + LANES] = jnp.where(low_half, *value).astype(
                         half_type
                     )
-
-    def output_block(i):
-        own = pl.ds(pl.multiple_of(i * half, half), half)
-        total = h2_ref[own, :] + rowsum.total(i) + vec_ref[1:2, :]
-        share.put(i, total.astype(half_type))
-
-    def step(j, carry):
-        keys_block(j)
-
-        hops = count - 1
-        per = -(-hops // blocks)
-        for t in range(per):
-            hop = j * per + t
-
-            @pl.when((hop >= 1) & (hop < hops))
-            def _(hop=hop):
-                scatter.advance(hop)
-
-        @pl.when(j < blocks - 2)
-        def _():
-            rowsum.give(j + 2)
-
-        rowsum.cross(j)
-
-        @pl.when(j >= 1)
-        def _():
-            output_block(j - 1)
-
-        return carry
-
-    lax.fori_loop(0, blocks, step, 0)
-    output_block(blocks - 1)
+            between(j, head)
+        return carry
+
+    lax.fori_loop(0, blocks, keys_block, 0)
 
     def turn(i, carry):
         rows = pl.ds(pl.multiple_of(i * BLOCK, BLOCK), BLOCK)
         gqkv_ref[rows, :local_width] = (gqt_ref[:, rows].T * HD**-0.5).astype(half_type)
         return carry
 
-    lax.fori_loop(0, blocks, turn, 0)
-    for way in range(2):
-        sum_ref[way] = scatter.total(way)
-
-    def arrived(i, carry):
-        share.arrived(i)
-        return carry
-
-    lax.fori_loop(0, blocks, arrived, 0)
-    scatter.finish()
-    rowsum.finish()
-    share.finish(blocks)
-
-
-def end_kernel(
-    count, gqkv_ref, w_ref, a1_ref, ga_ref, o_ref, gh2_ref, tok_ref, vec_ref, gbias_ref, gvec_ref,
-    tg_ref, sum_ref, small_ref,
-    term, given, sent, crossed, grads, stage, taken, small_mine, small_taken, small_mate,
-    sum_sems, share_sems, scatter_sems, small_sems, mate_sems,
-):
-    total_rows, width = a1_ref.shape
-    local_width = w_ref.shape[1] // 3
-    blocks = total_rows // BLOCK
-    half = BLOCK // 2
-    wide = width // count
-    lanes = small_ref.shape[1] - local_width
-    fold = lanes // wide
-    me, tensor = lax.axis_index("dp"), lax.axis_index("tensor")
-    mate = tensor - tensor % 2 + (tensor + 1) % 2
-    greeted = greet(tensor_peers() + dp_peers(count))
-    small_mine[:, :width] = gvec_ref[...]
+    rowsum2 = RowSum(term2, given2, sent2, crossed2, sum2_sems)
+
+    def norm_term(i):
+        rows = pl.ds(pl.multiple_of(i * BLOCK, BLOCK), BLOCK)
+        rowsum2.free(i)
+        term2[i % term2.shape[0]] = dot(gqkv_ref[rows, :], w_ref[...], 1, 1).astype(half_type)
+        rowsum2.give(i)
+
+    lax.fori_loop(0, 2, turn, 0)
+    norm_term(0)
+    norm_term(1)
+    rowsum.gone()
+    each(a1_in)
+    lax.fori_loop(2, blocks, turn, 0)
+    rowsum2.cross(0)
     ones = jnp.ones((8, total_rows), half_type)
     bias_query = dot(ones, gqkv_ref[:, :local_width])
     small_mine[0:1, width:] = bias_query[0:1, :]
-    ratio = gbias_ref.shape[1] // local_width
-    for r in range(ratio):
-        small_mine[1 + r : 2 + r, width:] = gbias_ref[0:1, r * local_width : (r + 1) * local_width]
-    small_mine[1 + ratio :, width:] = jnp.zeros((7 - ratio, local_width), full_type)
-    greeted()
-
-    def small_copy(part, source, peer):
+
+    def small_copy(kind, source, peer):
         window = pl.ds(pl.multiple_of(peer // fold * lanes, lanes), lanes)
         return pltpu.make_async_remote_copy(
-            src_ref=small_mine.at[:, pl.ds(width, local_width) if part else window],
-            dst_ref=small_taken.at[source, :, pl.ds(lanes, local_width) if part else pl.ds(0, lanes)],
-            send_sem=small_sems.at[2 * part, peer],
-            recv_sem=small_sems.at[2 * part + 1, source],
+            src_ref=small_mine.at[:, pl.ds(width, local_width) if kind else window],
+            dst_ref=small_taken.at[source, :, pl.ds(lanes, local_width) if kind else pl.ds(0, lanes)],
+            send_sem=small_sems.at[2 * kind, peer],
+            recv_sem=small_sems.at[2 * kind + 1, source],
             device_id=(peer, tensor),
             device_id_type=MESH,
         )
 
-    def send_small(part):
+    def send_small(kind):
         def send(k, carry):
-            small_copy(part, me, (me + k) % count).start()
+            small_copy(kind, me, (me + k) % count).start()
             return carry
 
         lax.fori_loop(1, count, send, 0)
 
     send_small(1)
-    rowsum = RowSum(term, given, sent, crossed, sum_sems)
-    share = Share(tg_ref, share_sems)
-
-    def view(way, block):
-        rows = pl.ds(pl.multiple_of(block * wide, wide), wide)
-        return jnp.stack([grads[2 * way, rows, :], grads[2 * way + 1, rows, :]])
-
-    scatter = Scatter(view, stage, taken, scatter_sems, count)
-
-    def norm_term(i):
-        rows = pl.ds(pl.multiple_of(i * BLOCK, BLOCK), BLOCK)
-        term[i] = dot(gqkv_ref[rows, :], w_ref[...], 1, 1).astype(half_type)
-        rowsum.give(i)
+
+    def arrived_a1(i, carry):
+        a1_in(i).wait()
+        return carry
+
+    lax.fori_loop(0, blocks, arrived_a1, 0)
+
+    def weight_grads(c, carry):
+        columns = pl.ds(pl.multiple_of(c * BLOCK, BLOCK), BLOCK)
+        grads[columns, : 3 * local_width] = dot(wide_ref[:, columns], gqkv_ref[...], 0, 0)
+        grads[columns, 3 * local_width :] = dot(ga_ref[:, columns], o_ref[...], 0, 0)
+        return carry
+
+    chunks = width // BLOCK
+    lax.fori_loop(0, chunks // 2, weight_grads, 0)
+    rowsum2.cross(1)
+    output_block(blocks - 1)
+    lax.fori_loop(chunks // 2, chunks, weight_grads, 0)
+    side = grads.shape[1] // 2
+
+    def grads_view(way, step):
+        return grads[
+            place(sent_block(pos, way, step, count)), way * side : (way + 1) * side
+        ]
+
+    scatter2 = Scatter(grads_view, stage2, taken2, scatter2_sems, count)
+    scatter2.begin()
+
+    def layer_left(i, carry):
+        layer.left(i)
+        layer.arrived(i)
+        return carry
+
+    lax.fori_loop(0, blocks, layer_left, 0)
+    result = Put(put_ref, tg_hbm, put2_sems)
 
     def norm_block(i):
-        own = pl.ds(pl.multiple_of(i * half, half), half)
-        gn = rowsum.total(i)
-        unit, rate = normalized(tok_ref[own, :].astype(full_type))
+        gn = rowsum2.total(i)
+        own_in(i).wait()
+        gh2_in(i).wait()
+        unit, rate = normalized(own_ref[own_rows(i), :].astype(full_type))
         e = gn * vec_ref[2:3, :]
         inner = e - jnp.mean(e, axis=-1, keepdims=True)
         inner = inner - unit * jnp.mean(e * unit, axis=-1, keepdims=True)
-        share.put(i, (gh2_ref[own, :] + rate * inner).astype(half_type))
+        result.put(i, (gh_ref[own_rows(i), :] + rate * inner).astype(half_type))
         small_mine[2:3, :width] += jnp.sum(gn * unit, axis=0, keepdims=True)
         small_mine[3:4, :width] += jnp.sum(gn, axis=0, keepdims=True)
 
-    def weight_grads(c, carry):
-        columns = pl.ds(pl.multiple_of(c * BLOCK, BLOCK), BLOCK)
-        three = dot(a1_ref[:, columns], gqkv_ref[...], 0, 0)
-        for row in range(3):
-            grads[row, columns, :] = three[:, row * local_width : (row + 1) * local_width]
-        grads[3, columns, :] = dot(ga_ref[:, columns], o_ref[...], 0, 0)
-        return carry
-
-    norm_term(0)
-    norm_term(1)
-    lax.fori_loop(0, 1, weight_grads, 0)
-    rowsum.cross(0)
-    lax.fori_loop(1, width // BLOCK, weight_grads, 0)
-    scatter.begin()
-    hops = count - 1
-    per = -(-hops // blocks)
-
-    def step(i, carry):
+    def end_step(i, carry):
         @pl.when(i < blocks - 2)
         def _():
             norm_term(i + 2)
 
-        @pl.when(i < blocks - 1)
+        norm_block(i)
+
+        @pl.when(i < blocks - 2)
         def _():
-            rowsum.cross(i + 1)
-
-        norm_block(i)
+            rowsum2.cross(i + 2)
+
         for t in range(per):
-            hop = i * per + t
-
-            @pl.when((hop >= 1) & (hop < hops))
+            hop = i * per + t + 1
+
+            @pl.when(hop < hops)
             def _(hop=hop):
-                scatter.advance(hop)
-
-        return carry
-
-    lax.fori_loop(0, blocks, step, 0)
+                scatter2.advance(hop)
+
+        return carry
+
+    lax.fori_loop(0, blocks, end_step, 0)
     send_small(0)
+    terms_ready(hops)
     for way in range(2):
-        total = scatter.total(way)
-        sum_ref[2 * way] = total[0]
-        sum_ref[2 * way + 1] = total[1]
-    for part in range(2):
+        for p, scatter in enumerate(scatters):
+            dense_ref[way, :, p * part : (p + 1) * part] = scatter.total(way)
+        total = scatter2.total(way)
+        for k in range(2):
+            sum_ref[2 * way + k] = total[:, k * local_width : (k + 1) * local_width]
+    for kind in range(2):
         window = pl.ds(pl.multiple_of(me // fold * lanes, lanes), lanes)
-        here = slice(lanes, lanes + local_width) if part else slice(0, lanes)
-        small_taken[me, :, here] = small_mine[:, width:] if part else small_mine[:, window]
-
-        def take(k, carry, part=part):
+        here = slice(lanes, lanes + local_width) if kind else slice(0, lanes)
+        small_taken[me, :, here] = small_mine[:, width:] if kind else small_mine[:, window]
+
+        def take(k, carry, kind=kind):
             source = (me + k) % count
-            small_copy(part, source, source).wait_recv()
+            small_copy(kind, source, source).wait_recv()
             return carry
 
         lax.fori_loop(1, count, take, 0)
@@ -970,18 +1103,20 @@
     pair.wait()
     small_ref[:, :lanes] = total[:, :lanes] + small_mate[...]
 
-    def arrived(i, carry):
-        share.arrived(i)
-        return carry
-
-    lax.fori_loop(0, blocks, arrived, 0)
-    scatter.finish()
-    rowsum.finish()
-    share.finish(blocks)
-    for part in range(2):
-
-        def done(k, carry, part=part):
-            small_copy(part, me, (me + k) % count).wait_send()
+    def result_left(i, carry):
+        result.left(i)
+        result.arrived(i)
+        return carry
+
+    lax.fori_loop(0, blocks, result_left, 0)
+    for scatter in scatters + [scatter2]:
+        scatter.finish()
+    rowsum.finish(given=False)
+    rowsum2.finish()
+    for kind in range(2):
+
+        def done(k, carry, kind=kind):
+            small_copy(kind, me, (me + k) % count).wait_send()
             return carry
 
         lax.fori_loop(1, count, done, 0)
@@ -1192,53 +1327,59 @@
         ),
         ("sshhvvvvv", "h" * 14 + "vvv"),
     )
-    gqkv, dense_sum, layer_output = call(
-        functools.partial(attention_back_kernel, count),
+    pieces = 2
+    row_blocks = pltpu.VMEM((blocks, half, width), half_type)
+    row_slots = pltpu.VMEM((min(3, blocks), half, width), half_type)
+    part, side = hidden // pieces, 2 * local_width
+    layer_output, tokens_grad, dense_sum, weight_sum, small_sum = call(
+        functools.partial(back_kernel, count),
         1,
         [
-            ((rows, 3 * local_width), half_type),
+            ((rows, width), half_type),
+            ((rows, width), half_type),
             ((2, wide, hidden), full_type),
-            ((rows, width), half_type),
-        ],
-        [
-            pltpu.VMEM(heads_shape, half_type),
-            pltpu.VMEM((local_width, rows), half_type),
-            pltpu.VMEM((local_width, rows), full_type),
-            *row_sum,
-            pltpu.VMEM((2, count - 1, wide, hidden), half_type),
-            pltpu.VMEM((2, count - 1, wide, hidden), half_type),
-            dma(4, blocks),
-            dma(2, blocks),
-            dma(4, count - 1),
-        ],
-        (ga, o, qb, ka, va, wo, up, dn, down.reshape(blocks, BLOCK, width), h2, vec),
-        ("v" * 11, "v" * 3),
-    )
-    tokens_grad, weight_sum, small_sum = call(
-        functools.partial(end_kernel, count),
-        2,
-        [
-            ((rows, width), half_type),
             ((4, wide, local_width), full_type),
             ((8, lanes + local_width), full_type),
         ],
         [
-            pltpu.VMEM((blocks, BLOCK, width), half_type),
-            *row_sum,
-            pltpu.VMEM((4, width, local_width), full_type),
-            pltpu.VMEM((2, count - 1, 2, wide, local_width), half_type),
-            pltpu.VMEM((2, count - 1, 2, wide, local_width), half_type),
+            pltpu.VMEM((rows, width), half_type),
+            pltpu.VMEM((rows, width), half_type),
+            pltpu.VMEM((rows // 2, width), full_type),
+            pltpu.VMEM((rows // 2, width), half_type),
+            pltpu.VMEM(heads_shape, half_type),
+            pltpu.VMEM((local_width, rows), half_type),
+            pltpu.VMEM((local_width, rows), full_type),
+            pltpu.VMEM((rows, 3 * local_width), half_type),
+            pltpu.VMEM((rows // 2, width), half_type),
+            row_blocks,
+            row_slots,
+            row_blocks,
+            two_terms,
+            row_blocks,
+            row_slots,
+            row_blocks,
+            pltpu.VMEM((2, 2, wide, hidden), full_type),
+            pltpu.VMEM((pieces, 2, 2, wide, part), half_type),
+            pltpu.VMEM((pieces, 2, count - 1, wide, part), half_type),
+            pltpu.VMEM((width, 4 * local_width), full_type),
+            pltpu.VMEM((2, 2, wide, side), half_type),
+            pltpu.VMEM((2, count - 1, wide, side), half_type),
             pltpu.VMEM((8, width + local_width), full_type),
             pltpu.VMEM((count, 8, lanes + local_width), full_type),
             pltpu.VMEM((8, lanes), full_type),
             dma(4, blocks),
-            dma(2, blocks),
+            dma(4, blocks),
+            dma(3, blocks),
+            dma(3, blocks),
+            dma(pieces, 4, count - 1),
             dma(4, count - 1),
             dma(4, count),
             dma(2),
+            dma(6, blocks),
+            dma(2, 2),
         ],
-        (gqkv, w, a1, ga, o, gh2, own, vec, gbias, gvec),
-        ("v" * 10, "v" * 3),
+        (ga, o, qb, ka, va, wo, w, up, dn, down, h2, gh2, own, a1, vec, gbias, gvec),
+        ("hvvvvvvhhhhhhhvvv", "hhvvv"),
     )
     if wide % LANES:
         layer_output, tokens_grad = (permuted(x, owner, True) for x in (layer_output, tokens_grad))

time: 279 us -> 251 us (0.90)
  Pallas kernels: 278 us -> 250 us
    pallas_call x3 -> x2, Pallas kernels: 264 us -> 236 us  [call(): pl.pallas_call(kernel, out_shape=[jax.ShapeDtypeStruct(shape, dtype) for...]
where the time goes in v4:
time: 251 us
  Pallas kernels  250 us (100%)
    pallas_call x2, Pallas kernels, call(): pl.pallas_call(kernel, out_shape=[jax.ShapeDtypeStruct(shape, dtype) for...  236 us
    pallas_call x1, Pallas kernels, last(): pl.pallas_call(functools.partial(last_kernel, rates), out_shape=[jax.Shap...  13.7 us

profile of v4, /device:TPU:0, one launch (start us, length us, event | category | flops | bytes accessed | tf_op | source)
XLA Modules:
  0.0 250.7 jit_solution(5134091458173742711)
XLA Ops:
  0.7 132.0 %shard_map.314 = (bf16[1792,1024]{1,0:T(8,128)(2,1)}, bf16[1792,1024]{1,0:T(8,128)(2,1)}, f32[896,1024]{1,0:T(8,128)}, bf16[896,1024]{1,0:T(8,128)(2,1)}, bf16[4...) custom-call(s32[1,8]{1,0:T(1,128)} %len_ref.1, ...), custom_call_target="tpu_custom_call" | custom-call | tf_op jit(solution)/shard_map/pallas_call | solution.py:1219
  132.7 104.2 %shard_map.315 = (bf16[1792,1024]{1,0:T(8,128)(2,1)}, bf16[1792,1024]{1,0:T(8,128)(2,1)}, f32[2,128,1024]{2,1,0:T(8,128)}, f32[4,128,256]{2,1,0:T(8,128)}, f32[8,384]{1,0:T(8,128)}) custom-call(bf16[1792,1024]{1,0:T(8,128)(2,1)} %get-tuple-element.39.ga_hbm, bf16[1792,256]{1,0:T(8,128)(2,1)} %get-tuple-element.40.o_ref, ...), custom_call_target="tpu_custom_call" | custom-call | tf_op jit(solution)/shard_map/pallas_call | solution.py:1219
  236.9 13.7 %shard_map.316 = (bf16[1792,1024]{1,0:T(8,128)(2,1)}, bf16[1792,1024]{1,0:T(8,128)(2,1)}, f32[3,128,256]{2,1,0:T(8,128)}, f32[3,128,256]{2,1,0:T(8,128)}, f32[3,...) custom-call(s32[8]{0:T(128)} %owner_ref.3, ...), custom_call_target="tpu_custom_call" | custom-call | tf_op jit(solution)/shard_map/pallas_call | solution.py:1203
